TPU v7x, 32 devices: a whole 2x2x4 slice. The times are simulated.
32 devices in a mesh: groups: 2 (over y), ep: 4 (over x, core), sub: 4 (over z).
Axes of the slice: x: 2, y: 2, z: 4, core: 2. Of those that a mesh axis runs over, the one named last changes fastest.
Arguments:
- row_codes: bfloat16 [2, 256, 7168], P(None, ('groups', 'ep', 'sub')), parts along dimension 1, may hold values from -6 to 6
- row_scales: float32 [2, 256, 56], P(None, ('groups', 'ep', 'sub')), parts along dimension 1, may hold values from 0.3 to 3
- expert_ids: int32 [2, 256, 2], P(None, ('groups', 'ep', 'sub')), parts along dimension 1, may hold values from 0 to 3, all different within a row; in each aligned block of 8 rows (0 to 7, 8 to 15, ..., all dimensions but the last counted through in order) at most 5 rows name the same one
- gate_codes: int32 [2, 256, 2], P(None, ('groups', 'ep', 'sub')), parts along dimension 1, may hold values from 1 to 1023
- w_gate: bfloat16 [4, 7168, 2048], P('ep', None, 'sub'), may hold values from -0.0625 to 0.0625
- w_up: bfloat16 [4, 7168, 2048], P('ep', None, 'sub'), may hold values from -0.0625 to 0.0625
- w_down: bfloat16 [4, 2048, 7168], P('ep', 'sub'), may hold values from -0.125 to 0.125
Outputs:
- combined: bfloat16 [2, 256, 7168], P(None, ('groups', 'ep', 'sub')), parts along dimension 1
There are 2 independent parts, one for each index of `groups`. A program takes and returns all parts, laid end to end along the dimension named above; an argument that names none is the same for every part. Nothing has to cross between parts.
Inputs may be any that keep to these rules, and one draw needn't show every extreme that they name: `expert_ids`: each row names 2 different experts. In each step no expert is named by more than 5 of one device's 8 rows, and in every draw some expert is named by exactly 5 rows of one device.
All inputs are finite; a program needn't handle non-finite values.
Results may differ from a plain program's by a relative error of at most 0.012.
Values may be sent and summed in bfloat16 or wider, within the bound.
No kernel may reach another device: no remote copies, remote signals or barrier semaphores. Data moves between devices by JAX's collectives and lax.ppermute only.
A program may use at most 128 MiB of HBM per device.

v0:
```python
import jax
import jax.numpy as jnp
from jax import lax
from jax.sharding import PartitionSpec as P

routed_scale = 2.5


def dequantize(codes, scales):
    block_size = codes.shape[1] // scales.shape[1]
    blocks = codes.astype(jnp.float32).reshape(codes.shape[0], -1, block_size)
    scaled = blocks * scales[:, :, None]
    return scaled.reshape(codes.shape[0], -1).astype(jnp.bfloat16)


def routing(chosen_ids, codes, ep_count, capacity):
    row_count, fanout = chosen_ids.shape
    flat_ids = chosen_ids.reshape(-1)
    onehot = (flat_ids[:, None] == jnp.arange(ep_count, dtype=jnp.int32)[None, :]).astype(jnp.int32)
    before = jnp.cumsum(onehot, axis=0) - onehot
    position = jnp.sum(before * onehot, axis=1)
    slot_of = (flat_ids * capacity + position).reshape(row_count, fanout)
    slot_range = jnp.arange(ep_count * capacity, dtype=jnp.int32)
    table = slot_of[:, :, None] == slot_range[None, None, :]
    pick = jnp.any(slot_range[:, None, None] == slot_of[None, :, :], axis=2).astype(jnp.bfloat16)
    codes_f = codes.astype(jnp.float32)
    total = jnp.sum(codes_f, axis=1, keepdims=True)
    weights = routed_scale * codes_f / total
    combine = jnp.sum(weights[:, :, None] * table.astype(jnp.float32), axis=1)
    return (pick, combine)


def body(row_codes, row_scales, expert_ids, gate_codes, w_gate, w_up, w_down):
    ep_count = lax.axis_size("ep")
    sub_count = lax.axis_size("sub")
    steps_here, row_count, features = row_codes.shape
    fanout = expert_ids.shape[2]
    capacity = (row_count * fanout + ep_count - 1) // ep_count + 1
    slot_count = ep_count * capacity
    gate_slice = w_gate[0]
    up_slice = w_up[0]
    down_slice = w_down[0]
    results = []
    for step_index in range(steps_here):
        tokens = dequantize(row_codes[step_index], row_scales[step_index])
        pick, combine = routing(expert_ids[step_index], gate_codes[step_index], ep_count, capacity)
        outgoing = jnp.dot(pick, tokens, preferred_element_type=jnp.float32).astype(jnp.bfloat16)
        outgoing = outgoing.reshape(ep_count, capacity, features)
        copies = jnp.broadcast_to(outgoing[:, None], (ep_count, sub_count, capacity, features))
        copies = copies.reshape(ep_count * sub_count, capacity, features)
        arrived = lax.all_to_all(copies, ("ep", "sub"), split_axis=0, concat_axis=0, tiled=True)
        width_here = arrived.shape[1]
        inputs = arrived.reshape(-1, features)
        gate_value = jnp.dot(inputs, gate_slice, preferred_element_type=jnp.float32)
        up_value = jnp.dot(inputs, up_slice, preferred_element_type=jnp.float32)
        hidden = (jax.nn.silu(gate_value) * up_value).astype(jnp.bfloat16)
        blocks = jnp.dot(hidden, down_slice, preferred_element_type=jnp.float32).astype(
            jnp.bfloat16
        )
        blocks = blocks.reshape(ep_count * sub_count, width_here, features)
        returned = lax.all_to_all(blocks, ("ep", "sub"), split_axis=0, concat_axis=0, tiled=True)
        returned = returned.reshape(ep_count, sub_count, capacity, features)
        expert_out = jnp.sum(returned.astype(jnp.float32), axis=1).astype(jnp.bfloat16)
        mixed = jnp.dot(
            combine,
            expert_out.reshape(slot_count, features).astype(jnp.float32),
            precision=lax.Precision.HIGHEST,
        )
        results.append(mixed.astype(jnp.bfloat16))
    return jnp.stack(results)


def solution(mesh):
    return jax.shard_map(
        body,
        mesh=mesh,
        in_specs=(
            P(None, ("groups", "ep", "sub"), None),
            P(None, ("groups", "ep", "sub"), None),
            P(None, ("groups", "ep", "sub"), None),
            P(None, ("groups", "ep", "sub"), None),
            P("ep", None, "sub"),
            P("ep", None, "sub"),
            P("ep", "sub", None),
        ),
        out_specs=P(None, ("groups", "ep", "sub"), None),
        check_vma=False,
    )
```

profile of v0, /device:TPU:0, one launch (start us, length us, event | category | flops | bytes accessed | tf_op | source)
XLA Modules:
  0.0 205.0 jit_solution(12118392512228197404)
XLA Ops:
  0.0 0.7 fusion.58
  1.0 0.2 select_reduce_fusion.3
  1.4 0.7 slice_bitcast_fusion.1
  2.2 1.2 convolution_convert_fusion.3
  3.4 0.1 broadcast_in_dim.8
  3.6 1.4 broadcast_in_dim.9
  5.0 7.5 %all-to-all-start = ((bf16[16,5,7168]{2,1,0:T(8,128)(2,1)}), bf16[16,5,7168]{2,1,0:T(8,128)(2,1)S(1)}, u32[]{:S(2)}, u32[]{:S(2)}) async-start(bf16[16,5,7168]{2,1,0:T(8,128)(2,1)} %bitcast.79), calls=%async_computation | async-start | bytes 3670016 | tf_op jit(solution)/shard_map/all_to_all | solution.py:51
  12.8 0.2 select_reduce_fusion.1
  13.3 0.3 convolution_convert_fusion.2
  13.6 0.1 broadcast_in_dim.10
  13.7 42.6 %all-to-all-done = bf16[16,5,7168]{2,1,0:T(8,128)(2,1)S(1)} async-done(((bf16[16,5,7168]{2,1,0:T(8,128)(2,1)}), bf16[16,5,7168]{2,1,0:T(8,128)(2,1)S(1)}, u32[]{:S(2)}, u32[]{:S(2)}) %all-to-all-start) | async-done | bytes 1146912 | tf_op jit(solution)/shard_map/all_to_all | solution.py:51
  56.3 1.4 broadcast_in_dim.11
  57.7 4.4 %all-to-all-start.2 = ((bf16[16,5,7168]{2,1,0:T(8,128)(2,1)}), bf16[16,5,7168]{2,1,0:T(8,128)(2,1)}, u32[]{:S(2)}, u32[]{:S(2)}) async-start(bf16[16,5,7168]{2,1,0:T(8,128)(2,1)} %bitcast.80), calls=%async_computation.2 | async-start | bytes 3670016 | tf_op jit(solution)/shard_map/all_to_all | solution.py:51
  62.2 0.6 reshape.127
  62.7 4.5 %fusion.10 = f32[80,512]{1,0:T(8,128)S(1)} fusion(bf16[80,7168]{1,0:T(8,128)(2,1)S(1)} %reshape.127, bf16[1,7168,512]{2,1,0:T(8,128)(2,1)} %param.11), kind=kOutput, calls=%fused_computation.16 | convolution fusion | flops 587202560 | bytes 8650752 | tf_op jit(solution)/shard_map/dot_general | solution.py:54
  67.2 7.9 %convolution_convert_fusion.1 = bf16[80,7168]{1,0:T(8,128)(2,1)S(1)} fusion(bf16[1,512,7168]{2,1,0:T(8,128)(2,1)} %param.13, bf16[80,7168]{1,0:T(8,128)(2,1)S(1)} %reshape.127, bf16[1,7168,512]{2,1,0:T(8,128)(2,1)} %param.12, f32[80,512]{1,0:T(8,128)S(1)} %fusion.10), kind=kOutput, calls=%fused_computation.1 | convolution fusion | flops 1175224320 | bytes 17137664 | tf_op jit(solution)/shard_map/dot_general | solution.py:57
  75.1 1.5 reshape.128
  76.7 29.3 %all-to-all-done.2 = bf16[16,5,7168]{2,1,0:T(8,128)(2,1)} async-done(((bf16[16,5,7168]{2,1,0:T(8,128)(2,1)}), bf16[16,5,7168]{2,1,0:T(8,128)(2,1)}, u32[]{:S(2)}, u32[]{:S(2)}) %all-to-all-start.2) | async-done | bytes 1146912 | tf_op jit(solution)/shard_map/all_to_all | solution.py:51
  106.0 3.7 %all-to-all-start.1 = ((bf16[16,5,7168]{2,1,0:T(8,128)(2,1)}), bf16[16,5,7168]{2,1,0:T(8,128)(2,1)S(1)}, u32[]{:S(2)}, u32[]{:S(2)}) async-start(bf16[16,5,7168]{2,1,0:T(8,128)(2,1)} %reshape.128), calls=%async_computation.1 | async-start | bytes 3670016 | tf_op jit(solution)/shard_map/all_to_all | solution.py:61
  109.7 1.7 reshape.132
  111.5 4.5 %fusion.8 = f32[80,512]{1,0:T(8,128)S(1)} fusion(bf16[80,7168]{1,0:T(8,128)(2,1)S(1)} %reshape.132, bf16[1,7168,512]{2,1,0:T(8,128)(2,1)} %param.11), kind=kOutput, calls=%fused_computation.14 | convolution fusion | flops 587202560 | bytes 8650752 | tf_op jit(solution)/shard_map/dot_general | solution.py:54
  115.9 8.9 %convolution_convert_fusion = bf16[80,7168]{1,0:T(8,128)(2,1)} fusion(bf16[1,512,7168]{2,1,0:T(8,128)(2,1)} %param.13, bf16[80,7168]{1,0:T(8,128)(2,1)S(1)} %reshape.132, bf16[1,7168,512]{2,1,0:T(8,128)(2,1)} %param.12, f32[80,512]{1,0:T(8,128)S(1)} %fusion.8), kind=kOutput, calls=%fused_computation | convolution fusion | flops 1175224320 | bytes 17137664 | tf_op jit(solution)/shard_map/dot_general | solution.py:57
  124.9 2.5 %reshape.133 = bf16[16,5,7168]{2,1,0:T(8,128)(2,1)} reshape(bf16[80,7168]{1,0:T(8,128)(2,1)} %convolution_convert_fusion) | data formatting | bytes 2293760 | tf_op jit(solution)/shard_map/reshape | solution.py:60
  127.4 26.1 %all-to-all-done.1 = bf16[16,5,7168]{2,1,0:T(8,128)(2,1)S(1)} async-done(((bf16[16,5,7168]{2,1,0:T(8,128)(2,1)}), bf16[16,5,7168]{2,1,0:T(8,128)(2,1)S(1)}, u32[]{:S(2)}, u32[]{:S(2)}) %all-to-all-start.1) | async-done | bytes 1146912 | tf_op jit(solution)/shard_map/all_to_all | solution.py:61
  153.5 4.4 %all-to-all-start.3 = ((bf16[16,5,7168]{2,1,0:T(8,128)(2,1)}), bf16[16,5,7168]{2,1,0:T(8,128)(2,1)}, u32[]{:S(2)}, u32[]{:S(2)}) async-start(bf16[16,5,7168]{2,1,0:T(8,128)(2,1)} %reshape.133), calls=%async_computation.3 | async-start | bytes 3670016 | tf_op jit(solution)/shard_map/all_to_all | solution.py:61
  158.5 0.4 bitcast_reduce_fusion.1
  158.9 0.1 reshape.130
  159.0 42.7 %all-to-all-done.3 = bf16[16,5,7168]{2,1,0:T(8,128)(2,1)} async-done(((bf16[16,5,7168]{2,1,0:T(8,128)(2,1)}), bf16[16,5,7168]{2,1,0:T(8,128)(2,1)}, u32[]{:S(2)}, u32[]{:S(2)}) %all-to-all-start.3) | async-done | bytes 1146912 | tf_op jit(solution)/shard_map/all_to_all | solution.py:61
  201.7 1.9 bitcast_reduce_fusion
  203.7 0.3 fusion
  204.0 0.3 fusion.1
  204.3 0.7 pad_maximum_fusion
  (34 shorter events, 1.9 us)
Async XLA Ops:
  5.0 8.3 %copy-start = (bf16[2,8,7168]{2,1,0:T(8,128)(2,1)S(1)}, bf16[2,8,7168]{2,1,0:T(8,128)(2,1)}, u32[]{:S(2)}) copy-start(bf16[2,8,7168]{2,1,0:T(8,128)(2,1)} %param.7) | copy-start | bytes 688132
  5.0 51.3 %all-to-all-start = ((bf16[16,5,7168]{2,1,0:T(8,128)(2,1)}), bf16[16,5,7168]{2,1,0:T(8,128)(2,1)S(1)}, u32[]{:S(2)}, u32[]{:S(2)}) async-start(bf16[16,5,7168]{2,1,0:T(8,128)(2,1)} %bitcast.79), calls=%async_computation | async-start | bytes 3670016 | tf_op jit(solution)/shard_map/all_to_all | solution.py:51
  57.7 48.2 %all-to-all-start.2 = ((bf16[16,5,7168]{2,1,0:T(8,128)(2,1)}), bf16[16,5,7168]{2,1,0:T(8,128)(2,1)}, u32[]{:S(2)}, u32[]{:S(2)}) async-start(bf16[16,5,7168]{2,1,0:T(8,128)(2,1)} %bitcast.80), calls=%async_computation.2 | async-start | bytes 3670016 | tf_op jit(solution)/shard_map/all_to_all | solution.py:51
  106.0 47.5 %all-to-all-start.1 = ((bf16[16,5,7168]{2,1,0:T(8,128)(2,1)}), bf16[16,5,7168]{2,1,0:T(8,128)(2,1)S(1)}, u32[]{:S(2)}, u32[]{:S(2)}) async-start(bf16[16,5,7168]{2,1,0:T(8,128)(2,1)} %reshape.128), calls=%async_computation.1 | async-start | bytes 3670016 | tf_op jit(solution)/shard_map/all_to_all | solution.py:61
  127.4 31.0 %copy-start.1 = (s32[2,8,2]{1,2,0:T(2,128)S(1)}, s32[2,8,2]{1,2,0:T(2,128)}, u32[]{:S(2)}) copy-start(s32[2,8,2]{1,2,0:T(2,128)} %param.10) | copy-start | bytes 388
  153.5 48.2 %all-to-all-start.3 = ((bf16[16,5,7168]{2,1,0:T(8,128)(2,1)}), bf16[16,5,7168]{2,1,0:T(8,128)(2,1)}, u32[]{:S(2)}, u32[]{:S(2)}) async-start(bf16[16,5,7168]{2,1,0:T(8,128)(2,1)} %reshape.133), calls=%async_computation.3 | async-start | bytes 3670016 | tf_op jit(solution)/shard_map/all_to_all | solution.py:61
where the time goes:
time: 206 us; the launch traced here: 205 us
  waiting for transfers between devices  141 us (68%)
  matrix products  27.9 us (14%)
  starting transfers between devices  20 us (10%)
  local copies, waits for them, and re-layouts  12.5 us (6%)
  other arithmetic  3.82 us (2%)
    all_to_all x2, waiting for transfers between devices, body(): lax.all_to_all(copies, ('ep', 'sub'), split_axis=0, concat_axis=0, tiled=...  71.9 us
    all_to_all x2, waiting for transfers between devices, body(): lax.all_to_all(blocks, ('ep', 'sub'), split_axis=0, concat_axis=0, tiled=...  68.7 us
    dot_general x2, matrix products, body(): jnp.dot(hidden, down_slice, preferred_element_type=jnp.float32)  16.9 us
    all_to_all x2, starting transfers between devices, body(): lax.all_to_all(copies, ('ep', 'sub'), split_axis=0, concat_axis=0, tiled=...  11.9 us
    dot_general x2, matrix products, body(): gate_value = jnp.dot(inputs, gate_slice, preferred_element_type=jnp.float32)  8.94 us
    all_to_all x2, starting transfers between devices, body(): lax.all_to_all(blocks, ('ep', 'sub'), split_axis=0, concat_axis=0, tiled=...  8.12 us
  transfers between devices with their start and end apart: 4, of which 4 were waited for; matrix products, arithmetic and copies ran while one was open for 17% of the time, Pallas kernels for 0%

commit v1 on v0

v1 whole, which is shorter than its diff:
```python
import jax
import jax.numpy as jnp
from jax import lax
from jax.sharding import PartitionSpec as P

routed_scale = 2.5
chunk_count = 4


def bits_of(count):
    return [1 << b for b in reversed(range(count.bit_length() - 1))]


def swap(value, axis_name, bit):
    count = lax.axis_size(axis_name)
    return lax.ppermute(value, axis_name, [(i, i ^ bit) for i in range(count)])


def dequantize(codes, scales):
    block_size = codes.shape[1] // scales.shape[1]
    blocks = codes.astype(jnp.float32).reshape(codes.shape[0], -1, block_size)
    scaled = blocks * scales[:, :, None]
    return scaled.reshape(codes.shape[0], -1).astype(jnp.bfloat16)


def route_columns(chosen_ids, codes, ep_count):
    experts = jnp.arange(ep_count, dtype=jnp.int32)
    dense = jnp.sum(jnp.where(chosen_ids[:, :, None] == experts, codes[:, :, None], 0), axis=1)
    both = jnp.concatenate([dense // 16 * 16, dense % 16], axis=1).astype(jnp.bfloat16)
    return jnp.pad(both, ((0, 0), (0, -both.shape[1] % 128)))


def body(row_codes, row_scales, expert_ids, gate_codes, w_gate, w_up, w_down):
    ep_count = lax.axis_size("ep")
    sub_count = lax.axis_size("sub")
    steps_here, row_count, features = row_codes.shape
    rows = steps_here * row_count
    stages = [("sub", b) for b in bits_of(sub_count)] + [("ep", b) for b in bits_of(ep_count)]
    tokens = dequantize(row_codes.reshape(rows, features), row_scales.reshape(rows, -1))
    codes = route_columns(expert_ids.reshape(rows, -1), gate_codes.reshape(rows, -1), ep_count)
    width = features // chunk_count
    parts = []
    for k in range(chunk_count):
        part = tokens[:, k * width : (k + 1) * width]
        parts.append(jnp.concatenate([part, codes], axis=1) if k == 0 else part)
    gathered = []
    for part in parts:
        for axis_name, bit in stages:
            part = jnp.concatenate([part, swap(part, axis_name, bit)], axis=0)
        gathered.append(part)
    me = lax.axis_index("ep")
    sent = gathered[0][:, width : width + 2 * ep_count].astype(jnp.float32)
    dense = sent[:, :ep_count] + sent[:, ep_count:]
    total = jnp.sum(dense, axis=1, keepdims=True)
    mine = jnp.sum(jnp.where(jnp.arange(ep_count) == me, dense, 0.0), axis=1, keepdims=True)
    weight = routed_scale * mine / total
    gate_value = up_value = 0.0
    for k, part in enumerate(gathered):
        inputs = part[:, :width]
        span = slice(k * width, (k + 1) * width)
        gate_value += jnp.dot(inputs, w_gate[0, span], preferred_element_type=jnp.float32)
        up_value += jnp.dot(inputs, w_up[0, span], preferred_element_type=jnp.float32)
    hidden = (jax.nn.silu(gate_value) * up_value).astype(jnp.bfloat16)
    results = []
    for k in range(chunk_count):
        span = slice(k * width, (k + 1) * width)
        held = jnp.dot(hidden, w_down[0, :, span], preferred_element_type=jnp.float32)
        held = (held * weight).astype(jnp.bfloat16)
        for axis_name, bit in reversed(stages):
            half = held.shape[0] // 2
            came = swap(held[half:], axis_name, bit)
            held = held[:half].astype(jnp.float32) + came.astype(jnp.float32)
            held = held.astype(jnp.bfloat16)
        results.append(held)
    return jnp.concatenate(results, axis=1).reshape(steps_here, row_count, features)


def solution(mesh):
    rows = P(None, ("groups", "ep", "sub"), None)
    return jax.shard_map(
        body,
        mesh=mesh,
        in_specs=(rows, rows, rows, rows, P("ep", None, "sub"), P("ep", None, "sub"), P("ep", "sub", None)),
        out_specs=rows,
        check_vma=False,
    )
```

time: 206 us -> 94.7 us (0.46)
  waiting for transfers between devices: 141 us -> 39.8 us
  matrix products: 27.9 us -> 9.45 us
  starting transfers between devices: 20 us -> 36.2 us
  local copies, waits for them, and re-layouts: 12.5 us -> 5.24 us
    all_to_all x4 -> x0, waiting for transfers between devices: 141 us -> none  [the longest x2 71.9 us: body(): lax.all_to_all(copies, ('ep', 'sub'), split_axis=0, concat_axis=0, tiled=...]
    ppermute x0 -> x32, waiting for transfers between devices: none -> 39.8 us  [swap(): return lax.ppermute(value, axis_name, [(i, i ^ bit) for i in range(count)])]
    ppermute x0 -> x32, starting transfers between devices: none -> 36.2 us  [swap(): return lax.ppermute(value, axis_name, [(i, i ^ bit) for i in range(count)])]
    all_to_all x4 -> x0, starting transfers between devices: 20 us -> none  [the longest x2 11.9 us: body(): lax.all_to_all(copies, ('ep', 'sub'), split_axis=0, concat_axis=0, tiled=...]
    dot_general x8 -> x12, matrix products: 27.9 us -> 9.45 us  [the longest x4 4.27 us: body(): jnp.dot(inputs, w_up[0, span], preferred_element_type=jnp.float32)]
    reshape x6 -> x0, local copies, waits for them, and re-layouts: 6.65 us -> none  [the longest x2 4.08 us: body(): blocks = blocks.reshape(ep_count * sub_count, width_here, features)]
    broadcast_in_dim x4 -> x1, local copies, waits for them, and re-layouts: 3.13 us -> 0.08 us  [route_columns(): jnp.where(chosen_ids[:, :, None] == experts, codes[:, :, None], 0)]
    unnamed x6 -> x31, local copies, waits for them, and re-layouts: 0.17 us -> 3.12 us
  transfers between devices with their start and end apart: 4 -> 32, of which waited for: 4 -> 13; matrix products, arithmetic and copies ran while one was open for 17% -> 10% of each run, Pallas kernels for 0% -> 0%
where the time goes in v1:
time: 94.7 us; the launch traced here: 94.5 us
  waiting for transfers between devices  39.8 us (42%)
  starting transfers between devices  36.2 us (38%)
  matrix products  9.45 us (10%)
  local copies, waits for them, and re-layouts  5.24 us (6%)
  other arithmetic  3.17 us (3%)
    ppermute x32, waiting for transfers between devices, swap(): return lax.ppermute(value, axis_name, [(i, i ^ bit) for i in range(count)])  39.8 us
    ppermute x32, starting transfers between devices, swap(): return lax.ppermute(value, axis_name, [(i, i ^ bit) for i in range(count)])  36.2 us
    dot_general x4, matrix products, body(): jnp.dot(inputs, w_up[0, span], preferred_element_type=jnp.float32)  4.27 us
    unnamed x31, local copies, waits for them, and re-layouts  3.12 us
    dot_general x4, matrix products, body(): jnp.dot(hidden, w_down[0, :, span], preferred_element_type=jnp.float32)  2.6 us
    dot_general x4, matrix products, body(): jnp.dot(inputs, w_gate[0, span], preferred_element_type=jnp.float32)  2.58 us
  transfers between devices with their start and end apart: 32, of which 13 were waited for; matrix products, arithmetic and copies ran while one was open for 10% of the time, Pallas kernels for 0%

profile of v1, /device:TPU:0, one launch (start us, length us, event | category | flops | bytes accessed | tf_op | source)
XLA Modules:
  0.0 94.5 jit_solution(15809260238243029786)
XLA Ops:
  0.0 0.9 mul.62
  0.9 1.0 %fusion.56 = bf16[16,7168]{1,0:T(8,128)(2,1)S(1)} fusion(f32[2,8,56,128]{3,2,1,0:T(8,128)S(1)} %bitcast.75, bf16[2,8,7168]{2,1,0:T(8,128)(2,1)} %param.7), kind=kLoop, calls=%fused_computation.55 | loop fusion | flops 344064 | bytes 917504 | tf_op jit(solution)/shard_map/convert_element_type | solution.py:23
  2.6 4.0 %collective-permute-start.12 = (bf16[16,1792]{1,0:T(8,128)(2,1)S(1)}, bf16[16,1792]{1,0:T(8,128)(2,1)S(1)}, u32[]{:S(2)}, u32[]{:S(2)}) collective-permute-start(bf16[16,1792]{1,0:T(8,128)(2,1)S(1)} %get-tuple-element.11), channel_id=1, source_target_pairs={{0,2},{1,3},{2,0},{3,1},{4,6},{5,7},{6,4},{7,5},{8,10},{9,11},{10,... | collective-permute-start | bytes 172040 | tf_op jit(solution)/shard_map/ppermute | solution.py:16
  6.7 2.9 %collective-permute-start.4 = (bf16[16,1792]{1,0:T(8,128)(2,1)S(1)}, bf16[16,1792]{1,0:T(8,128)(2,1)S(1)}, u32[]{:S(2)}, u32[]{:S(2)}) collective-permute-start(bf16[16,1792]{1,0:T(8,128)(2,1)S(1)} %get-tuple-element.13), channel_id=1, source_target_pairs={{0,2},{1,3},{2,0},{3,1},{4,6},{5,7},{6,4},{7,5},{8,10},{9,11},{10,... | collective-permute-start | bytes 172040 | tf_op jit(solution)/shard_map/ppermute | solution.py:16
  10.0 4.4 %collective-permute-start.13 = (bf16[32,1792]{1,0:T(8,128)(2,1)S(1)}, bf16[32,1792]{1,0:T(8,128)(2,1)S(1)}, u32[]{:S(2)}, u32[]{:S(2)}) collective-permute-start(bf16[32,1792]{1,0:T(8,128)(2,1)S(1)} %pad_maximum_fusion.11), channel_id=1, source_target_pairs={{0,1},{1,0},{2,3},{3,2},{4,5},{5,4},{6,7},{7,6},{8,9},{9,8},{10,11... | collective-permute-start | bytes 344072 | tf_op jit(solution)/shard_map/ppermute | solution.py:16
  14.4 0.7 collective-permute-done.8
  15.7 1.4 %collective-permute-done.4 = bf16[16,1792]{1,0:T(8,128)(2,1)S(1)} collective-permute-done((bf16[16,1792]{1,0:T(8,128)(2,1)S(1)}, bf16[16,1792]{1,0:T(8,128)(2,1)S(1)}, u32[]{:S(2)}, u32[]{:S(2)}) %collective-permute-start.4) | collective-permute-done | bytes 57376 | tf_op jit(solution)/shard_map/ppermute | solution.py:16
  18.0 1.9 %collective-permute-start.1 = (bf16[32,1920]{1,0:T(8,128)(2,1)S(1)}, bf16[32,1920]{1,0:T(8,128)(2,1)S(1)}, u32[]{:S(2)}, u32[]{:S(2)}) collective-permute-start(bf16[32,1920]{1,0:T(8,128)(2,1)S(1)} %pad_maximum_fusion.8), channel_id=1, source_target_pairs={{0,1},{1,0},{2,3},{3,2},{4,5},{5,4},{6,7},{7,6},{8,9},{9,8},{10,11... | collective-permute-start | bytes 368648 | tf_op jit(solution)/shard_map/ppermute | solution.py:16
  20.0 1.6 %collective-permute-start.14 = (bf16[64,1792]{1,0:T(8,128)(2,1)S(1)}, bf16[64,1792]{1,0:T(8,128)(2,1)S(1)}, u32[]{:S(2)}, u32[]{:S(2)}) collective-permute-start(bf16[64,1792]{1,0:T(8,128)(2,1)S(1)} %pad_maximum_fusion.7), channel_id=1, source_target_pairs={{0,8},{4,12},{8,0},{12,4},{1,9},{5,13},{9,1},{13,5},{2,10},{6,14},... | collective-permute-start | bytes 688136 | tf_op jit(solution)/shard_map/ppermute | solution.py:16
  21.6 0.8 collective-permute-done.9
  22.4 1.7 %collective-permute-start.10 = (bf16[64,1792]{1,0:T(8,128)(2,1)S(1)}, bf16[64,1792]{1,0:T(8,128)(2,1)S(1)}, u32[]{:S(2)}, u32[]{:S(2)}) collective-permute-start(bf16[64,1792]{1,0:T(8,128)(2,1)S(1)} %pad_maximum_fusion.6), channel_id=1, source_target_pairs={{0,8},{4,12},{8,0},{12,4},{1,9},{5,13},{9,1},{13,5},{2,10},{6,14},... | collective-permute-start | bytes 688136 | tf_op jit(solution)/shard_map/ppermute | solution.py:16
  24.0 0.8 collective-permute-done.5
  24.8 1.7 %collective-permute-start.6 = (bf16[64,1792]{1,0:T(8,128)(2,1)S(1)}, bf16[64,1792]{1,0:T(8,128)(2,1)S(1)}, u32[]{:S(2)}, u32[]{:S(2)}) collective-permute-start(bf16[64,1792]{1,0:T(8,128)(2,1)S(1)} %pad_maximum_fusion.5), channel_id=1, source_target_pairs={{0,8},{4,12},{8,0},{12,4},{1,9},{5,13},{9,1},{13,5},{2,10},{6,14},... | collective-permute-start | bytes 688136 | tf_op jit(solution)/shard_map/ppermute | solution.py:16
  27.2 1.5 %collective-permute-start.2 = (bf16[64,1920]{1,0:T(8,128)(2,1)S(1)}, bf16[64,1920]{1,0:T(8,128)(2,1)S(1)}, u32[]{:S(2)}, u32[]{:S(2)}) collective-permute-start(bf16[64,1920]{1,0:T(8,128)(2,1)S(1)} %pad_maximum_fusion.4), channel_id=1, source_target_pairs={{0,8},{4,12},{8,0},{12,4},{1,9},{5,13},{9,1},{13,5},{2,10},{6,14},... | collective-permute-start | bytes 737288 | tf_op jit(solution)/shard_map/ppermute | solution.py:16
  28.7 9.7 %collective-permute-done.6 = bf16[64,1792]{1,0:T(8,128)(2,1)S(1)} collective-permute-done((bf16[64,1792]{1,0:T(8,128)(2,1)S(1)}, bf16[64,1792]{1,0:T(8,128)(2,1)S(1)}, u32[]{:S(2)}, u32[]{:S(2)}) %collective-permute-start.6) | collective-permute-done | bytes 229408 | tf_op jit(solution)/shard_map/ppermute | solution.py:16
  39.4 2.5 %collective-permute-done.2 = bf16[64,1920]{1,0:T(8,128)(2,1)S(1)} collective-permute-done((bf16[64,1920]{1,0:T(8,128)(2,1)S(1)}, bf16[64,1920]{1,0:T(8,128)(2,1)S(1)}, u32[]{:S(2)}, u32[]{:S(2)}) %collective-permute-start.2) | collective-permute-done | bytes 245792 | tf_op jit(solution)/shard_map/ppermute | solution.py:16
  42.1 2.3 %fusion.8 = f32[256,512]{1,0:T(8,128)S(1)} fusion(bf16[256,1792]{1,0:T(8,128)(2,1)S(1)} %constant_dynamic-update-slice_fusion.15, bf16[1,7168,512]{2,1,0:T(8,128)(2,1)} %param.12), kind=kOutput, calls=%fused_computation.12 | convolution fusion | flops 469762048 | bytes 3276800 | tf_op jit(solution)/shard_map/dot_general | solution.py:62
  49.3 0.7 multiply_convert_fusion
  50.1 1.0 %slice-done.3 = s8[3145728]{0:T(1024)(128)(4,1)S(1)} async-done(((s8[7340032]{0:T(1024)(128)(4,1)}), s8[3145728]{0:T(1024)(128)(4,1)S(1)}, s32[]{:S(2)}) %slice-start.3) | async-done | bytes 3145752
  55.3 1.6 %collective-permute-start.21 = (bf16[64,1792]{1,0:T(8,128)(2,1)S(1)}, bf16[64,1792]{1,0:T(8,128)(2,1)S(1)}, u32[]{:S(2)}, u32[]{:S(2)}) collective-permute-start(bf16[64,1792]{1,0:T(8,128)(2,1)S(1)} %slice.227), channel_id=1, source_target_pairs={{0,8},{4,12},{8,0},{12,4},{1,9},{5,13},{9,1},{13,5},{2,10},{6,14},... | collective-permute-start | bytes 688136 | tf_op jit(solution)/shard_map/ppermute | solution.py:16
  57.7 1.6 %collective-permute-start.29 = (bf16[64,1792]{1,0:T(8,128)(2,1)S(1)}, bf16[64,1792]{1,0:T(8,128)(2,1)S(1)}, u32[]{:S(2)}, u32[]{:S(2)}) collective-permute-start(bf16[64,1792]{1,0:T(8,128)(2,1)S(1)} %slice.243), channel_id=1, source_target_pairs={{0,8},{4,12},{8,0},{12,4},{1,9},{5,13},{9,1},{13,5},{2,10},{6,14},... | collective-permute-start | bytes 688136 | tf_op jit(solution)/shard_map/ppermute | solution.py:16
  60.0 3.7 %collective-permute-done.21 = bf16[64,1792]{1,0:T(8,128)(2,1)S(1)} collective-permute-done((bf16[64,1792]{1,0:T(8,128)(2,1)S(1)}, bf16[64,1792]{1,0:T(8,128)(2,1)S(1)}, u32[]{:S(2)}, u32[]{:S(2)}) %collective-permute-start.21) | collective-permute-done | bytes 229408 | tf_op jit(solution)/shard_map/ppermute | solution.py:16
  64.0 4.6 %collective-permute-done.25 = bf16[64,1792]{1,0:T(8,128)(2,1)S(1)} collective-permute-done((bf16[64,1792]{1,0:T(8,128)(2,1)S(1)}, bf16[64,1792]{1,0:T(8,128)(2,1)S(1)}, u32[]{:S(2)}, u32[]{:S(2)}) %collective-permute-start.25) | collective-permute-done | bytes 229408 | tf_op jit(solution)/shard_map/ppermute | solution.py:16
  69.0 4.6 %collective-permute-done.29 = bf16[64,1792]{1,0:T(8,128)(2,1)S(1)} collective-permute-done((bf16[64,1792]{1,0:T(8,128)(2,1)S(1)}, bf16[64,1792]{1,0:T(8,128)(2,1)S(1)}, u32[]{:S(2)}, u32[]{:S(2)}) %collective-permute-start.29) | collective-permute-done | bytes 229408 | tf_op jit(solution)/shard_map/ppermute | solution.py:16
  73.9 4.2 %collective-permute-done.17 = bf16[64,1792]{1,0:T(8,128)(2,1)S(1)} collective-permute-done((bf16[64,1792]{1,0:T(8,128)(2,1)S(1)}, bf16[64,1792]{1,0:T(8,128)(2,1)S(1)}, u32[]{:S(2)}, u32[]{:S(2)}) %collective-permute-start.17) | collective-permute-done | bytes 229408 | tf_op jit(solution)/shard_map/ppermute | solution.py:16
  78.3 4.8 %collective-permute-start.23 = (bf16[16,1792]{1,0:T(8,128)(2,1)S(1)}, bf16[16,1792]{1,0:T(8,128)(2,1)S(1)}, u32[]{:S(2)}, u32[]{:S(2)}) collective-permute-start(bf16[16,1792]{1,0:T(8,128)(2,1)S(1)} %slice.231), channel_id=1, source_target_pairs={{0,2},{1,3},{2,0},{3,1},{4,6},{5,7},{6,4},{7,5},{8,10},{9,11},{10,... | collective-permute-start | bytes 172040 | tf_op jit(solution)/shard_map/ppermute | solution.py:16
  83.3 3.0 %collective-permute-start.31 = (bf16[16,1792]{1,0:T(8,128)(2,1)S(1)}, bf16[16,1792]{1,0:T(8,128)(2,1)S(1)}, u32[]{:S(2)}, u32[]{:S(2)}) collective-permute-start(bf16[16,1792]{1,0:T(8,128)(2,1)S(1)} %slice.247), channel_id=1, source_target_pairs={{0,2},{1,3},{2,0},{3,1},{4,6},{5,7},{6,4},{7,5},{8,10},{9,11},{10,... | collective-permute-start | bytes 172040 | tf_op jit(solution)/shard_map/ppermute | solution.py:16
  86.3 0.8 collective-permute-start.19
  87.1 4.6 %collective-permute-done.27 = bf16[16,1792]{1,0:T(8,128)(2,1)S(1)} collective-permute-done((bf16[16,1792]{1,0:T(8,128)(2,1)S(1)}, bf16[16,1792]{1,0:T(8,128)(2,1)S(1)}, u32[]{:S(2)}, u32[]{:S(2)}) %collective-permute-start.27) | collective-permute-done | bytes 57376 | tf_op jit(solution)/shard_map/ppermute | solution.py:16
  91.7 1.2 %collective-permute-done.31 = bf16[16,1792]{1,0:T(8,128)(2,1)S(1)} collective-permute-done((bf16[16,1792]{1,0:T(8,128)(2,1)S(1)}, bf16[16,1792]{1,0:T(8,128)(2,1)S(1)}, u32[]{:S(2)}, u32[]{:S(2)}) %collective-permute-start.31) | collective-permute-done | bytes 57376 | tf_op jit(solution)/shard_map/ppermute | solution.py:16
  93.0 0.8 collective-permute-done.19
  93.8 0.7 maximum_bitcast_fusion
  (140 shorter events, 16.1 us)
Async XLA Ops:
  2.6 7.4 %collective-permute-start.12 = (bf16[16,1792]{1,0:T(8,128)(2,1)S(1)}, bf16[16,1792]{1,0:T(8,128)(2,1)S(1)}, u32[]{:S(2)}, u32[]{:S(2)}) collective-permute-start(bf16[16,1792]{1,0:T(8,128)(2,1)S(1)} %get-tuple-element.11), channel_id=1, source_target_pairs={{0,2},{1,3},{2,0},{3,1},{4,6},{5,7},{6,4},{7,5},{8,10},{9,11},{10,... | collective-permute-start | bytes 172040 | tf_op jit(solution)/shard_map/ppermute | solution.py:16
  6.6 8.6 %collective-permute-start.8 = (bf16[16,1792]{1,0:T(8,128)(2,1)S(1)}, bf16[16,1792]{1,0:T(8,128)(2,1)S(1)}, u32[]{:S(2)}, u32[]{:S(2)}) collective-permute-start(bf16[16,1792]{1,0:T(8,128)(2,1)S(1)} %get-tuple-element.12), channel_id=1, source_target_pairs={{0,2},{1,3},{2,0},{3,1},{4,6},{5,7},{6,4},{7,5},{8,10},{9,11},{10,... | collective-permute-start | bytes 172040 | tf_op jit(solution)/shard_map/ppermute | solution.py:16
  6.7 10.5 %collective-permute-start.4 = (bf16[16,1792]{1,0:T(8,128)(2,1)S(1)}, bf16[16,1792]{1,0:T(8,128)(2,1)S(1)}, u32[]{:S(2)}, u32[]{:S(2)}) collective-permute-start(bf16[16,1792]{1,0:T(8,128)(2,1)S(1)} %get-tuple-element.13), channel_id=1, source_target_pairs={{0,2},{1,3},{2,0},{3,1},{4,6},{5,7},{6,4},{7,5},{8,10},{9,11},{10,... | collective-permute-start | bytes 172040 | tf_op jit(solution)/shard_map/ppermute | solution.py:16
  9.9 8.1 %collective-permute-start = (bf16[16,1920]{1,0:T(8,128)(2,1)S(1)}, bf16[16,1920]{1,0:T(8,128)(2,1)S(1)}, u32[]{:S(2)}, u32[]{:S(2)}) collective-permute-start(bf16[16,1920]{1,0:T(8,128)(2,1)S(1)} %get-tuple-element.14), channel_id=1, source_target_pairs={{0,2},{1,3},{2,0},{3,1},{4,6},{5,7},{6,4},{7,5},{8,10},{9,11},{10,... | collective-permute-start | bytes 184328 | tf_op jit(solution)/shard_map/ppermute | solution.py:16
  10.0 9.9 %collective-permute-start.13 = (bf16[32,1792]{1,0:T(8,128)(2,1)S(1)}, bf16[32,1792]{1,0:T(8,128)(2,1)S(1)}, u32[]{:S(2)}, u32[]{:S(2)}) collective-permute-start(bf16[32,1792]{1,0:T(8,128)(2,1)S(1)} %pad_maximum_fusion.11), channel_id=1, source_target_pairs={{0,1},{1,0},{2,3},{3,2},{4,5},{5,4},{6,7},{7,6},{8,9},{9,8},{10,11... | collective-permute-start | bytes 344072 | tf_op jit(solution)/shard_map/ppermute | solution.py:16
  15.2 7.2 %collective-permute-start.9 = (bf16[32,1792]{1,0:T(8,128)(2,1)S(1)}, bf16[32,1792]{1,0:T(8,128)(2,1)S(1)}, u32[]{:S(2)}, u32[]{:S(2)}) collective-permute-start(bf16[32,1792]{1,0:T(8,128)(2,1)S(1)} %pad_maximum_fusion.10), channel_id=1, source_target_pairs={{0,1},{1,0},{2,3},{3,2},{4,5},{5,4},{6,7},{7,6},{8,9},{9,8},{10,11... | collective-permute-start | bytes 344072 | tf_op jit(solution)/shard_map/ppermute | solution.py:16
  17.1 7.7 %collective-permute-start.5 = (bf16[32,1792]{1,0:T(8,128)(2,1)S(1)}, bf16[32,1792]{1,0:T(8,128)(2,1)S(1)}, u32[]{:S(2)}, u32[]{:S(2)}) collective-permute-start(bf16[32,1792]{1,0:T(8,128)(2,1)S(1)} %pad_maximum_fusion.9), channel_id=1, source_target_pairs={{0,1},{1,0},{2,3},{3,2},{4,5},{5,4},{6,7},{7,6},{8,9},{9,8},{10,11... | collective-permute-start | bytes 344072 | tf_op jit(solution)/shard_map/ppermute | solution.py:16
  18.0 9.1 %collective-permute-start.1 = (bf16[32,1920]{1,0:T(8,128)(2,1)S(1)}, bf16[32,1920]{1,0:T(8,128)(2,1)S(1)}, u32[]{:S(2)}, u32[]{:S(2)}) collective-permute-start(bf16[32,1920]{1,0:T(8,128)(2,1)S(1)} %pad_maximum_fusion.8), channel_id=1, source_target_pairs={{0,1},{1,0},{2,3},{3,2},{4,5},{5,4},{6,7},{7,6},{8,9},{9,8},{10,11... | collective-permute-start | bytes 368648 | tf_op jit(solution)/shard_map/ppermute | solution.py:16
  20.0 19.2 %collective-permute-start.14 = (bf16[64,1792]{1,0:T(8,128)(2,1)S(1)}, bf16[64,1792]{1,0:T(8,128)(2,1)S(1)}, u32[]{:S(2)}, u32[]{:S(2)}) collective-permute-start(bf16[64,1792]{1,0:T(8,128)(2,1)S(1)} %pad_maximum_fusion.7), channel_id=1, source_target_pairs={{0,8},{4,12},{8,0},{12,4},{1,9},{5,13},{9,1},{13,5},{2,10},{6,14},... | collective-permute-start | bytes 688136 | tf_op jit(solution)/shard_map/ppermute | solution.py:16
  22.4 16.2 %collective-permute-start.10 = (bf16[64,1792]{1,0:T(8,128)(2,1)S(1)}, bf16[64,1792]{1,0:T(8,128)(2,1)S(1)}, u32[]{:S(2)}, u32[]{:S(2)}) collective-permute-start(bf16[64,1792]{1,0:T(8,128)(2,1)S(1)} %pad_maximum_fusion.6), channel_id=1, source_target_pairs={{0,8},{4,12},{8,0},{12,4},{1,9},{5,13},{9,1},{13,5},{2,10},{6,14},... | collective-permute-start | bytes 688136 | tf_op jit(solution)/shard_map/ppermute | solution.py:16
  24.8 13.6 %collective-permute-start.6 = (bf16[64,1792]{1,0:T(8,128)(2,1)S(1)}, bf16[64,1792]{1,0:T(8,128)(2,1)S(1)}, u32[]{:S(2)}, u32[]{:S(2)}) collective-permute-start(bf16[64,1792]{1,0:T(8,128)(2,1)S(1)} %pad_maximum_fusion.5), channel_id=1, source_target_pairs={{0,8},{4,12},{8,0},{12,4},{1,9},{5,13},{9,1},{13,5},{2,10},{6,14},... | collective-permute-start | bytes 688136 | tf_op jit(solution)/shard_map/ppermute | solution.py:16
  27.2 14.6 %collective-permute-start.2 = (bf16[64,1920]{1,0:T(8,128)(2,1)S(1)}, bf16[64,1920]{1,0:T(8,128)(2,1)S(1)}, u32[]{:S(2)}, u32[]{:S(2)}) collective-permute-start(bf16[64,1920]{1,0:T(8,128)(2,1)S(1)} %pad_maximum_fusion.4), channel_id=1, source_target_pairs={{0,8},{4,12},{8,0},{12,4},{1,9},{5,13},{9,1},{13,5},{2,10},{6,14},... | collective-permute-start | bytes 737288 | tf_op jit(solution)/shard_map/ppermute | solution.py:16
  38.5 8.5 %collective-permute-start.7 = (bf16[128,1792]{1,0:T(8,128)(2,1)S(1)}, bf16[128,1792]{1,0:T(8,128)(2,1)S(1)}, u32[]{:S(2)}, u32[]{:S(2)}) collective-permute-start(bf16[128,1792]{1,0:T(8,128)(2,1)S(1)} %pad_maximum_fusion.1), channel_id=1, source_target_pairs={{0,4},{4,0},{8,12},{12,8},{1,5},{5,1},{9,13},{13,9},{2,6},{6,2},{1... | collective-permute-start | bytes 1376264 | tf_op jit(solution)/shard_map/ppermute | solution.py:16
  38.6 6.4 %collective-permute-start.11 = (bf16[128,1792]{1,0:T(8,128)(2,1)S(1)}, bf16[128,1792]{1,0:T(8,128)(2,1)S(1)}, u32[]{:S(2)}, u32[]{:S(2)}) collective-permute-start(bf16[128,1792]{1,0:T(8,128)(2,1)S(1)} %pad_maximum_fusion.2), channel_id=1, source_target_pairs={{0,4},{4,0},{8,12},{12,8},{1,5},{5,1},{9,13},{13,9},{2,6},{6,2},{1... | collective-permute-start | bytes 1376264 | tf_op jit(solution)/shard_map/ppermute | solution.py:16
  39.2 2.8 %collective-permute-start.15 = (bf16[128,1792]{1,0:T(8,128)(2,1)S(1)}, bf16[128,1792]{1,0:T(8,128)(2,1)S(1)}, u32[]{:S(2)}, u32[]{:S(2)}) collective-permute-start(bf16[128,1792]{1,0:T(8,128)(2,1)S(1)} %pad_maximum_fusion.3), channel_id=1, source_target_pairs={{0,4},{4,0},{8,12},{12,8},{1,5},{5,1},{9,13},{13,9},{2,6},{6,2},{1... | collective-permute-start | bytes 1376264 | tf_op jit(solution)/shard_map/ppermute | solution.py:16
  41.9 6.4 %collective-permute-start.3 = (bf16[128,1920]{1,0:T(8,128)(2,1)S(1)}, bf16[128,1920]{1,0:T(8,128)(2,1)S(1)}, u32[]{:S(2)}, u32[]{:S(2)}) collective-permute-start(bf16[128,1920]{1,0:T(8,128)(2,1)S(1)} %pad_maximum_fusion), channel_id=1, source_target_pairs={{0,4},{4,0},{8,12},{12,8},{1,5},{5,1},{9,13},{13,9},{2,6},{6,2},{1... | collective-permute-start | bytes 1474568 | tf_op jit(solution)/shard_map/ppermute | solution.py:16
  52.4 2.7 %collective-permute-start.20 = (bf16[128,1792]{1,0:T(8,128)(2,1)S(1)}, bf16[128,1792]{1,0:T(8,128)(2,1)S(1)}, u32[]{:S(2)}, u32[]{:S(2)}) collective-permute-start(bf16[128,1792]{1,0:T(8,128)(2,1)S(1)} %slice.225), channel_id=1, source_target_pairs={{0,4},{4,0},{8,12},{12,8},{1,5},{5,1},{9,13},{13,9},{2,6},{6,2},{1... | collective-permute-start | bytes 1376264 | tf_op jit(solution)/shard_map/ppermute | solution.py:16
  53.0 3.9 %collective-permute-start.24 = (bf16[128,1792]{1,0:T(8,128)(2,1)S(1)}, bf16[128,1792]{1,0:T(8,128)(2,1)S(1)}, u32[]{:S(2)}, u32[]{:S(2)}) collective-permute-start(bf16[128,1792]{1,0:T(8,128)(2,1)S(1)} %slice.233), channel_id=1, source_target_pairs={{0,4},{4,0},{8,12},{12,8},{1,5},{5,1},{9,13},{13,9},{2,6},{6,2},{1... | collective-permute-start | bytes 1376264 | tf_op jit(solution)/shard_map/ppermute | solution.py:16
  53.8 3.8 %collective-permute-start.28 = (bf16[128,1792]{1,0:T(8,128)(2,1)S(1)}, bf16[128,1792]{1,0:T(8,128)(2,1)S(1)}, u32[]{:S(2)}, u32[]{:S(2)}) collective-permute-start(bf16[128,1792]{1,0:T(8,128)(2,1)S(1)} %slice.241), channel_id=1, source_target_pairs={{0,4},{4,0},{8,12},{12,8},{1,5},{5,1},{9,13},{13,9},{2,6},{6,2},{1... | collective-permute-start | bytes 1376264 | tf_op jit(solution)/shard_map/ppermute | solution.py:16
  55.1 4.3 %collective-permute-start.16 = (bf16[128,1792]{1,0:T(8,128)(2,1)S(1)}, bf16[128,1792]{1,0:T(8,128)(2,1)S(1)}, u32[]{:S(2)}, u32[]{:S(2)}) collective-permute-start(bf16[128,1792]{1,0:T(8,128)(2,1)S(1)} %slice.217), channel_id=1, source_target_pairs={{0,4},{4,0},{8,12},{12,8},{1,5},{5,1},{9,13},{13,9},{2,6},{6,2},{1... | collective-permute-start | bytes 1376264 | tf_op jit(solution)/shard_map/ppermute | solution.py:16
  55.3 8.5 %collective-permute-start.21 = (bf16[64,1792]{1,0:T(8,128)(2,1)S(1)}, bf16[64,1792]{1,0:T(8,128)(2,1)S(1)}, u32[]{:S(2)}, u32[]{:S(2)}) collective-permute-start(bf16[64,1792]{1,0:T(8,128)(2,1)S(1)} %slice.227), channel_id=1, source_target_pairs={{0,8},{4,12},{8,0},{12,4},{1,9},{5,13},{9,1},{13,5},{2,10},{6,14},... | collective-permute-start | bytes 688136 | tf_op jit(solution)/shard_map/ppermute | solution.py:16
  57.1 11.6 %collective-permute-start.25 = (bf16[64,1792]{1,0:T(8,128)(2,1)S(1)}, bf16[64,1792]{1,0:T(8,128)(2,1)S(1)}, u32[]{:S(2)}, u32[]{:S(2)}) collective-permute-start(bf16[64,1792]{1,0:T(8,128)(2,1)S(1)} %slice.235), channel_id=1, source_target_pairs={{0,8},{4,12},{8,0},{12,4},{1,9},{5,13},{9,1},{13,5},{2,10},{6,14},... | collective-permute-start | bytes 688136 | tf_op jit(solution)/shard_map/ppermute | solution.py:16
  57.7 15.9 %collective-permute-start.29 = (bf16[64,1792]{1,0:T(8,128)(2,1)S(1)}, bf16[64,1792]{1,0:T(8,128)(2,1)S(1)}, u32[]{:S(2)}, u32[]{:S(2)}) collective-permute-start(bf16[64,1792]{1,0:T(8,128)(2,1)S(1)} %slice.243), channel_id=1, source_target_pairs={{0,8},{4,12},{8,0},{12,4},{1,9},{5,13},{9,1},{13,5},{2,10},{6,14},... | collective-permute-start | bytes 688136 | tf_op jit(solution)/shard_map/ppermute | solution.py:16
  59.5 18.6 %collective-permute-start.17 = (bf16[64,1792]{1,0:T(8,128)(2,1)S(1)}, bf16[64,1792]{1,0:T(8,128)(2,1)S(1)}, u32[]{:S(2)}, u32[]{:S(2)}) collective-permute-start(bf16[64,1792]{1,0:T(8,128)(2,1)S(1)} %slice.219), channel_id=1, source_target_pairs={{0,8},{4,12},{8,0},{12,4},{1,9},{5,13},{9,1},{13,5},{2,10},{6,14},... | collective-permute-start | bytes 688136 | tf_op jit(solution)/shard_map/ppermute | solution.py:16
  63.8 14.4 %collective-permute-start.22 = (bf16[32,1792]{1,0:T(8,128)(2,1)S(1)}, bf16[32,1792]{1,0:T(8,128)(2,1)S(1)}, u32[]{:S(2)}, u32[]{:S(2)}) collective-permute-start(bf16[32,1792]{1,0:T(8,128)(2,1)S(1)} %slice.229), channel_id=1, source_target_pairs={{0,1},{1,0},{2,3},{3,2},{4,5},{5,4},{6,7},{7,6},{8,9},{9,8},{10,11... | collective-permute-start | bytes 344072 | tf_op jit(solution)/shard_map/ppermute | solution.py:16
  68.7 14.3 %collective-permute-start.26 = (bf16[32,1792]{1,0:T(8,128)(2,1)S(1)}, bf16[32,1792]{1,0:T(8,128)(2,1)S(1)}, u32[]{:S(2)}, u32[]{:S(2)}) collective-permute-start(bf16[32,1792]{1,0:T(8,128)(2,1)S(1)} %slice.237), channel_id=1, source_target_pairs={{0,1},{1,0},{2,3},{3,2},{4,5},{5,4},{6,7},{7,6},{8,9},{9,8},{10,11... | collective-permute-start | bytes 344072 | tf_op jit(solution)/shard_map/ppermute | solution.py:16
  73.7 9.6 %collective-permute-start.30 = (bf16[32,1792]{1,0:T(8,128)(2,1)S(1)}, bf16[32,1792]{1,0:T(8,128)(2,1)S(1)}, u32[]{:S(2)}, u32[]{:S(2)}) collective-permute-start(bf16[32,1792]{1,0:T(8,128)(2,1)S(1)} %slice.245), channel_id=1, source_target_pairs={{0,1},{1,0},{2,3},{3,2},{4,5},{5,4},{6,7},{7,6},{8,9},{9,8},{10,11... | collective-permute-start | bytes 344072 | tf_op jit(solution)/shard_map/ppermute | solution.py:16
  78.2 8.1 %collective-permute-start.18 = (bf16[32,1792]{1,0:T(8,128)(2,1)S(1)}, bf16[32,1792]{1,0:T(8,128)(2,1)S(1)}, u32[]{:S(2)}, u32[]{:S(2)}) collective-permute-start(bf16[32,1792]{1,0:T(8,128)(2,1)S(1)} %slice.221), channel_id=1, source_target_pairs={{0,1},{1,0},{2,3},{3,2},{4,5},{5,4},{6,7},{7,6},{8,9},{9,8},{10,11... | collective-permute-start | bytes 344072 | tf_op jit(solution)/shard_map/ppermute | solution.py:16
  78.3 8.8 %collective-permute-start.23 = (bf16[16,1792]{1,0:T(8,128)(2,1)S(1)}, bf16[16,1792]{1,0:T(8,128)(2,1)S(1)}, u32[]{:S(2)}, u32[]{:S(2)}) collective-permute-start(bf16[16,1792]{1,0:T(8,128)(2,1)S(1)} %slice.231), channel_id=1, source_target_pairs={{0,2},{1,3},{2,0},{3,1},{4,6},{5,7},{6,4},{7,5},{8,10},{9,11},{10,... | collective-permute-start | bytes 172040 | tf_op jit(solution)/shard_map/ppermute | solution.py:16
  83.1 8.6 %collective-permute-start.27 = (bf16[16,1792]{1,0:T(8,128)(2,1)S(1)}, bf16[16,1792]{1,0:T(8,128)(2,1)S(1)}, u32[]{:S(2)}, u32[]{:S(2)}) collective-permute-start(bf16[16,1792]{1,0:T(8,128)(2,1)S(1)} %slice.239), channel_id=1, source_target_pairs={{0,2},{1,3},{2,0},{3,1},{4,6},{5,7},{6,4},{7,5},{8,10},{9,11},{10,... | collective-permute-start | bytes 172040 | tf_op jit(solution)/shard_map/ppermute | solution.py:16
  83.3 9.7 %collective-permute-start.31 = (bf16[16,1792]{1,0:T(8,128)(2,1)S(1)}, bf16[16,1792]{1,0:T(8,128)(2,1)S(1)}, u32[]{:S(2)}, u32[]{:S(2)}) collective-permute-start(bf16[16,1792]{1,0:T(8,128)(2,1)S(1)} %slice.247), channel_id=1, source_target_pairs={{0,2},{1,3},{2,0},{3,1},{4,6},{5,7},{6,4},{7,5},{8,10},{9,11},{10,... | collective-permute-start | bytes 172040 | tf_op jit(solution)/shard_map/ppermute | solution.py:16
  86.3 7.5 %collective-permute-start.19 = (bf16[16,1792]{1,0:T(8,128)(2,1)S(1)}, bf16[16,1792]{1,0:T(8,128)(2,1)S(1)}, u32[]{:S(2)}, u32[]{:S(2)}) collective-permute-start(bf16[16,1792]{1,0:T(8,128)(2,1)S(1)} %slice.223), channel_id=1, source_target_pairs={{0,2},{1,3},{2,0},{3,1},{4,6},{5,7},{6,4},{7,5},{8,10},{9,11},{10,... | collective-permute-start | bytes 172040 | tf_op jit(solution)/shard_map/ppermute | solution.py:16
  (8 other events, 79.4 us)

commit v2 on v1

v2 whole, which is shorter than its diff:
```python
import jax
import jax.numpy as jnp
from jax import lax
from jax.sharding import PartitionSpec as P

routed_scale = 2.5
column_parts = 2


def bits_of(count):
    return [1 << b for b in reversed(range(count.bit_length() - 1))]


def swap(value, axis_name, bit):
    count = lax.axis_size(axis_name)
    return lax.ppermute(value, axis_name, [(i, i ^ bit) for i in range(count)])


def after(value, *others):
    return lax.optimization_barrier((value, *others))[0] if others else value


def join(*parts):
    return jnp.concatenate(parts, axis=0)


def add_up(*terms):
    total = terms[0].astype(jnp.float32)
    for term in terms[1:]:
        total = total + term.astype(jnp.float32)
    return total


def dequantize(codes, scales):
    block_size = codes.shape[1] // scales.shape[1]
    blocks = codes.astype(jnp.float32).reshape(codes.shape[0], -1, block_size)
    scaled = blocks * scales[:, :, None]
    return scaled.reshape(codes.shape[0], -1).astype(jnp.bfloat16)


def route_columns(chosen_ids, codes, ep_count):
    experts = jnp.arange(ep_count, dtype=jnp.int32)
    dense = jnp.sum(jnp.where(chosen_ids[:, :, None] == experts, codes[:, :, None], 0), axis=1)
    both = jnp.concatenate([dense // 16 * 16, dense % 16], axis=1).astype(jnp.bfloat16)
    return jnp.pad(both, ((0, 0), (0, -both.shape[1] % 128)))


def body(row_codes, row_scales, expert_ids, gate_codes, w_gate, w_up, w_down):
    ep_count = lax.axis_size("ep")
    sub_bits = bits_of(lax.axis_size("sub"))
    ep_bits = bits_of(ep_count)
    steps_here, rows, features = row_codes.shape
    width = features // column_parts
    tokens = dequantize(row_codes.reshape(-1, features), row_scales.reshape(steps_here * rows, -1))
    codes = route_columns(expert_ids.reshape(steps_here * rows, -1), gate_codes.reshape(steps_here * rows, -1), ep_count)
    tokens = jnp.concatenate([codes, tokens], axis=1)
    extra = codes.shape[1]
    crossed = swap(tokens, "ep", ep_bits[0])
    me = lax.axis_index("ep")
    first = None
    own_gives = []
    waiting = []
    step_done = []
    returned = []
    for step in range(steps_here):
        gate_value = up_value = 0.0
        for k in range(column_parts):
            low = 0 if k == 0 else extra + k * width
            block = (slice(step * rows, (step + 1) * rows), slice(low, extra + (k + 1) * width))
            own = tokens[block]
            part = own
            for n, bit in enumerate(sub_bits):
                if n == 0 and first is not None:
                    part = after(part, first)
                came = swap(part, "sub", bit)
                if first is None:
                    first = came
                part = join(part, came)
            part = join(part, crossed[block], swap(part[rows:], "ep", ep_bits[0]))
            for bit in ep_bits[1:]:
                part = after(part, *step_done)
                part = join(part, swap(part, "ep", bit))
            if k == 0:
                sent = part[:, : 2 * ep_count].astype(jnp.float32)
                dense = sent[:, :ep_count] + sent[:, ep_count:]
                total = jnp.sum(dense, axis=1, keepdims=True)
                mine = jnp.sum(jnp.where(jnp.arange(ep_count) == me, dense, 0.0), axis=1, keepdims=True)
                weight = routed_scale * mine / total
            inputs = part[:, extra - low :] if k == 0 else part
            span = slice(k * width, (k + 1) * width)
            gate_value += jnp.dot(inputs, w_gate[0, span], preferred_element_type=jnp.float32)
            up_value += jnp.dot(inputs, w_up[0, span], preferred_element_type=jnp.float32)
        hidden = (jax.nn.silu(gate_value) * up_value).astype(jnp.bfloat16)
        step_done = []
        for k in range(column_parts):
            span = slice(k * width, (k + 1) * width)
            held = jnp.dot(hidden, w_down[0, :, span], preferred_element_type=jnp.float32)
            held = (held * weight).astype(jnp.bfloat16)
            step_done.append(held)
            for bit in reversed(ep_bits[1:]):
                half = held.shape[0] // 2
                held = add_up(held[:half], swap(held[half:], "ep", bit)).astype(jnp.bfloat16)
            half = held.shape[0] // 2
            give = held[half + rows :]
            if len(waiting) >= 3:
                give = after(give, waiting[-3])
            own_gives.append(held[half : half + rows])
            own = [held[:rows]]
            rest = add_up(held[rows:half], swap(give, "ep", ep_bits[0])).astype(jnp.bfloat16)
            for n, bit in enumerate(reversed(sub_bits)):
                half = (rest.shape[0] + rows) // 2
                came = swap(rest[half - rows :], "sub", bit)
                if n == 0:
                    waiting.append(came)
                own.append(came[:rows])
                if half > rows:
                    rest = add_up(rest[: half - rows], came[rows:]).astype(jnp.bfloat16)
            returned.append(own)
    by_step = [own_gives[s * column_parts : (s + 1) * column_parts] for s in range(steps_here)]
    crossed = swap(join(*[jnp.concatenate(gives, axis=1) for gives in by_step]), "ep", ep_bits[0])
    results = []
    for step in range(steps_here):
        outs = []
        for k in range(column_parts):
            own = returned[step * column_parts + k]
            block = (slice(step * rows, (step + 1) * rows), slice(k * width, (k + 1) * width))
            outs.append(add_up(*own, crossed[block]).astype(jnp.bfloat16))
        results.append(jnp.concatenate(outs, axis=1))
    return jnp.stack(results)


def solution(mesh):
    rows = P(None, ("groups", "ep", "sub"), None)
    return jax.shard_map(
        body,
        mesh=mesh,
        in_specs=(rows, rows, rows, rows, P("ep", None, "sub"), P("ep", None, "sub"), P("ep", "sub", None)),
        out_specs=rows,
        check_vma=False,
    )
```

time: 94.7 us -> 88.5 us (0.935)
  waiting for transfers between devices: 39.8 us -> 35.7 us
  matrix products: 9.45 us -> 7.81 us
    ppermute x32 -> x34, waiting for transfers between devices: 39.8 us -> 35.7 us  [swap(): return lax.ppermute(value, axis_name, [(i, i ^ bit) for i in range(count)])]
    dot_general x4, matrix products: 4.27 us -> 2.58 us  [body(): jnp.dot(inputs, w_up[0, span], preferred_element_type=jnp.float32)]
    ppermute x32 -> x34, starting transfers between devices: 36.2 us -> 35.3 us  [swap(): return lax.ppermute(value, axis_name, [(i, i ^ bit) for i in range(count)])]
    unnamed x31 -> x36, local copies, waits for them, and re-layouts: 3.12 us -> 3.98 us
  transfers between devices with their start and end apart: 32 -> 34, of which waited for: 13 -> 20; matrix products, arithmetic and copies ran while one was open for 10% -> 7% of each run, Pallas kernels for 0% -> 0%
where the time goes in v2:
time: 88.5 us; the launch traced here: 88.2 us
  waiting for transfers between devices  35.7 us (40%)
  starting transfers between devices  35.3 us (40%)
  matrix products  7.81 us (9%)
  local copies, waits for them, and re-layouts  5.51 us (6%)
  other arithmetic  3.21 us (4%)
    ppermute x34, waiting for transfers between devices, swap(): return lax.ppermute(value, axis_name, [(i, i ^ bit) for i in range(count)])  35.7 us
    ppermute x34, starting transfers between devices, swap(): return lax.ppermute(value, axis_name, [(i, i ^ bit) for i in range(count)])  35.3 us
    unnamed x36, local copies, waits for them, and re-layouts  3.98 us
    dot_general x4, matrix products, body(): jnp.dot(hidden, w_down[0, :, span], preferred_element_type=jnp.float32)  2.67 us
    dot_general x4, matrix products, body(): jnp.dot(inputs, w_up[0, span], preferred_element_type=jnp.float32)  2.58 us
    dot_general x4, matrix products, body(): jnp.dot(inputs, w_gate[0, span], preferred_element_type=jnp.float32)  2.56 us
  transfers between devices with their start and end apart: 34, of which 20 were waited for; matrix products, arithmetic and copies ran while one was open for 7% of the time, Pallas kernels for 0%

profile of v2, /device:TPU:0, one launch (start us, length us, event | category | flops | bytes accessed | tf_op | source)
XLA Modules:
  0.0 88.2 jit_solution(9395789760672751324)
XLA Ops:
  2.5 1.0 %fusion.53 = bf16[16,7168]{1,0:T(8,128)(2,1)S(1)} fusion(f32[2,8,56,128]{3,2,1,0:T(8,128)S(1)} %bitcast.67, bf16[2,8,7168]{2,1,0:T(8,128)(2,1)} %param.7), kind=kLoop, calls=%fused_computation.55 | loop fusion | flops 344064 | bytes 917504 | tf_op jit(solution)/shard_map/convert_element_type | solution.py:38
  3.6 3.0 %collective-permute-start.2 = (bf16[16,7296]{1,0:T(8,128)(2,1)S(1)}, bf16[16,7296]{1,0:T(8,128)(2,1)S(1)}, u32[]{:S(2)}, u32[]{:S(2)}) collective-permute-start(bf16[16,7296]{1,0:T(8,128)(2,1)S(1)} %fusion.54), channel_id=1, source_target_pairs={{0,8},{4,12},{8,0},{12,4},{1,9},{5,13},{9,1},{13,5},{2,10},{6,14},... | collective-permute-start | bytes 700424 | tf_op jit(solution)/shard_map/ppermute | solution.py:16
  6.6 2.7 %collective-permute-start = (bf16[8,3712]{1,0:T(8,128)(2,1)S(1)}, bf16[8,3712]{1,0:T(8,128)(2,1)S(1)}, u32[]{:S(2)}, u32[]{:S(2)}) collective-permute-start(bf16[8,3712]{1,0:T(8,128)(2,1)S(1)} %get-tuple-element.27), channel_id=1, source_target_pairs={{0,2},{1,3},{2,0},{3,1},{4,6},{5,7},{6,4},{7,5},{8,10},{9,11},{10,... | collective-permute-start | bytes 178184 | tf_op jit(solution)/shard_map/ppermute | solution.py:16
  9.3 2.7 %collective-permute-done = bf16[8,3712]{1,0:T(8,128)(2,1)S(1)} collective-permute-done((bf16[8,3712]{1,0:T(8,128)(2,1)S(1)}, bf16[8,3712]{1,0:T(8,128)(2,1)S(1)}, u32[]{:S(2)}, u32[]{:S(2)}) %collective-permute-start) | collective-permute-done | bytes 59424 | tf_op jit(solution)/shard_map/ppermute | solution.py:16
  12.0 2.4 %collective-permute-start.18 = (bf16[8,3584]{1,0:T(8,128)(2,1)S(1)}, bf16[8,3584]{1,0:T(8,128)(2,1)S(1)}, u32[]{:S(2)}, u32[]{:S(2)}) collective-permute-start(bf16[8,3584]{1,0:T(8,128)(2,1)S(1)} %get-tuple-element.14), channel_id=1, source_target_pairs={{0,2},{1,3},{2,0},{3,1},{4,6},{5,7},{6,4},{7,5},{8,10},{9,11},{10,... | collective-permute-start | bytes 172040 | tf_op jit(solution)/shard_map/ppermute | solution.py:16
  15.0 2.4 %collective-permute-start.5 = (bf16[8,3584]{1,0:T(8,128)(2,1)S(1)}, bf16[8,3584]{1,0:T(8,128)(2,1)S(1)}, u32[]{:S(2)}, u32[]{:S(2)}) collective-permute-start(bf16[8,3584]{1,0:T(8,128)(2,1)S(1)} %get-tuple-element.11), channel_id=1, source_target_pairs={{0,2},{1,3},{2,0},{3,1},{4,6},{5,7},{6,4},{7,5},{8,10},{9,11},{10,... | collective-permute-start | bytes 172040 | tf_op jit(solution)/shard_map/ppermute | solution.py:16
  17.4 2.1 %collective-permute-start.1 = (bf16[16,3712]{1,0:T(8,128)(2,1)S(1)}, bf16[16,3712]{1,0:T(8,128)(2,1)S(1)}, u32[]{:S(2)}, u32[]{:S(2)}) collective-permute-start(bf16[16,3712]{1,0:T(8,128)(2,1)S(1)} %pad_maximum_fusion.5), channel_id=1, source_target_pairs={{0,1},{1,0},{2,3},{3,2},{4,5},{5,4},{6,7},{7,6},{8,9},{9,8},{10,11... | collective-permute-start | bytes 356360 | tf_op jit(solution)/shard_map/ppermute | solution.py:16
  20.2 1.4 %collective-permute-done.5 = bf16[8,3584]{1,0:T(8,128)(2,1)S(1)} collective-permute-done((bf16[8,3584]{1,0:T(8,128)(2,1)S(1)}, bf16[8,3584]{1,0:T(8,128)(2,1)S(1)}, u32[]{:S(2)}, u32[]{:S(2)}) %collective-permute-start.5) | collective-permute-done | bytes 57376 | tf_op jit(solution)/shard_map/ppermute | solution.py:16
  21.6 1.9 %collective-permute-start.6 = (bf16[16,3584]{1,0:T(8,128)(2,1)S(1)}, bf16[16,3584]{1,0:T(8,128)(2,1)S(1)}, u32[]{:S(2)}, u32[]{:S(2)}) collective-permute-start(bf16[16,3584]{1,0:T(8,128)(2,1)S(1)} %pad_maximum_fusion.7), channel_id=1, source_target_pairs={{0,1},{1,0},{2,3},{3,2},{4,5},{5,4},{6,7},{7,6},{8,9},{9,8},{10,11... | collective-permute-start | bytes 344072 | tf_op jit(solution)/shard_map/ppermute | solution.py:16
  24.5 1.8 %collective-permute-done.19 = bf16[16,3584]{1,0:T(8,128)(2,1)S(1)} collective-permute-done((bf16[16,3584]{1,0:T(8,128)(2,1)S(1)}, bf16[16,3584]{1,0:T(8,128)(2,1)S(1)}, u32[]{:S(2)}, u32[]{:S(2)}) %collective-permute-start.19) | collective-permute-done | bytes 114720 | tf_op jit(solution)/shard_map/ppermute | solution.py:16
  27.0 1.5 %collective-permute-done.6 = bf16[16,3584]{1,0:T(8,128)(2,1)S(1)} collective-permute-done((bf16[16,3584]{1,0:T(8,128)(2,1)S(1)}, bf16[16,3584]{1,0:T(8,128)(2,1)S(1)}, u32[]{:S(2)}, u32[]{:S(2)}) %collective-permute-start.6) | collective-permute-done | bytes 114720 | tf_op jit(solution)/shard_map/ppermute | solution.py:16
  29.8 1.0 %collective-permute-start.16 = (bf16[24,3712]{1,0:T(8,128)(2,1)S(1)}, bf16[24,3712]{1,0:T(8,128)(2,1)S(1)}, u32[]{:S(2)}, u32[]{:S(2)}) collective-permute-start(bf16[24,3712]{1,0:T(8,128)(2,1)S(1)} %pad_maximum_fusion.2), channel_id=1, source_target_pairs={{0,8},{4,12},{8,0},{12,4},{1,9},{5,13},{9,1},{13,5},{2,10},{6,14},... | collective-permute-start | bytes 534536 | tf_op jit(solution)/shard_map/ppermute | solution.py:16
  31.5 6.1 %collective-permute-done.7 = bf16[24,3584]{1,0:T(8,128)(2,1)S(1)} collective-permute-done((bf16[24,3584]{1,0:T(8,128)(2,1)S(1)}, bf16[24,3584]{1,0:T(8,128)(2,1)S(1)}, u32[]{:S(2)}, u32[]{:S(2)}) %collective-permute-start.7) | collective-permute-done | bytes 172064 | tf_op jit(solution)/shard_map/ppermute | solution.py:16
  37.8 1.8 %collective-permute-done.16 = bf16[24,3712]{1,0:T(8,128)(2,1)S(1)} collective-permute-done((bf16[24,3712]{1,0:T(8,128)(2,1)S(1)}, bf16[24,3712]{1,0:T(8,128)(2,1)S(1)}, u32[]{:S(2)}, u32[]{:S(2)}) %collective-permute-start.16) | collective-permute-done | bytes 178208 | tf_op jit(solution)/shard_map/ppermute | solution.py:16
  43.7 1.1 %slice-done.5 = s8[3145728]{0:T(1024)(128)(4,1)S(1)} async-done(((s8[7340032]{0:T(1024)(128)(4,1)}), s8[3145728]{0:T(1024)(128)(4,1)S(1)}, s32[]{:S(2)}) %slice-start.5) | async-done | bytes 3145752
  47.4 1.3 %collective-permute-done.13 = bf16[64,3584]{1,0:T(8,128)(2,1)S(1)} collective-permute-done((bf16[64,3584]{1,0:T(8,128)(2,1)S(1)}, bf16[64,3584]{1,0:T(8,128)(2,1)S(1)}, u32[]{:S(2)}, u32[]{:S(2)}) %collective-permute-start.13) | collective-permute-done | bytes 458784 | tf_op jit(solution)/shard_map/ppermute | solution.py:16
  50.2 1.5 %collective-permute-start.10 = (bf16[24,3584]{1,0:T(8,128)(2,1)S(1)}, bf16[24,3584]{1,0:T(8,128)(2,1)S(1)}, u32[]{:S(2)}, u32[]{:S(2)}) collective-permute-start(bf16[24,3584]{1,0:T(8,128)(2,1)S(1)} %slice.290), channel_id=1, source_target_pairs={{0,8},{4,12},{8,0},{12,4},{1,9},{5,13},{9,1},{13,5},{2,10},{6,14},... | collective-permute-start | bytes 516104 | tf_op jit(solution)/shard_map/ppermute | solution.py:16
  57.4 2.4 %collective-permute-done.10 = bf16[24,3584]{1,0:T(8,128)(2,1)S(1)} collective-permute-done((bf16[24,3584]{1,0:T(8,128)(2,1)S(1)}, bf16[24,3584]{1,0:T(8,128)(2,1)S(1)}, u32[]{:S(2)}, u32[]{:S(2)}) %collective-permute-start.10) | collective-permute-done | bytes 172064 | tf_op jit(solution)/shard_map/ppermute | solution.py:16
  60.2 1.9 %collective-permute-done.26 = bf16[16,3584]{1,0:T(8,128)(2,1)S(1)} collective-permute-done((bf16[16,3584]{1,0:T(8,128)(2,1)S(1)}, bf16[16,3584]{1,0:T(8,128)(2,1)S(1)}, u32[]{:S(2)}, u32[]{:S(2)}) %collective-permute-start.26) | collective-permute-done | bytes 114720 | tf_op jit(solution)/shard_map/ppermute | solution.py:16
  62.2 1.6 %collective-permute-start.27 = (bf16[8,3584]{1,0:T(8,128)(2,1)S(1)}, bf16[8,3584]{1,0:T(8,128)(2,1)S(1)}, u32[]{:S(2)}, u32[]{:S(2)}) collective-permute-start(bf16[8,3584]{1,0:T(8,128)(2,1)S(1)} %add_convert_fusion.13), channel_id=1, source_target_pairs={{0,2},{1,3},{2,0},{3,1},{4,6},{5,7},{6,4},{7,5},{8,10},{9,11},{10,... | collective-permute-start | bytes 172040 | tf_op jit(solution)/shard_map/ppermute | solution.py:16
  63.8 1.2 %collective-permute-done.11 = bf16[16,3584]{1,0:T(8,128)(2,1)S(1)} collective-permute-done((bf16[16,3584]{1,0:T(8,128)(2,1)S(1)}, bf16[16,3584]{1,0:T(8,128)(2,1)S(1)}, u32[]{:S(2)}, u32[]{:S(2)}) %collective-permute-start.11) | collective-permute-done | bytes 114720 | tf_op jit(solution)/shard_map/ppermute | solution.py:16
  65.0 2.0 %collective-permute-start.12 = (bf16[8,3584]{1,0:T(8,128)(2,1)S(1)}, bf16[8,3584]{1,0:T(8,128)(2,1)S(1)}, u32[]{:S(2)}, u32[]{:S(2)}) collective-permute-start(bf16[8,3584]{1,0:T(8,128)(2,1)S(1)} %add_convert_fusion.15), channel_id=1, source_target_pairs={{0,2},{1,3},{2,0},{3,1},{4,6},{5,7},{6,4},{7,5},{8,10},{9,11},{10,... | collective-permute-start | bytes 172040 | tf_op jit(solution)/shard_map/ppermute | solution.py:16
  67.9 1.5 %collective-permute-start.28 = (bf16[24,3584]{1,0:T(8,128)(2,1)S(1)}, bf16[24,3584]{1,0:T(8,128)(2,1)S(1)}, u32[]{:S(2)}, u32[]{:S(2)}) collective-permute-start(bf16[24,3584]{1,0:T(8,128)(2,1)S(1)} %slice.324), channel_id=1, source_target_pairs={{0,8},{4,12},{8,0},{12,4},{1,9},{5,13},{9,1},{13,5},{2,10},{6,14},... | collective-permute-start | bytes 516104 | tf_op jit(solution)/shard_map/ppermute | solution.py:16
  70.0 4.7 %collective-permute-done.31 = bf16[24,3584]{1,0:T(8,128)(2,1)S(1)} collective-permute-done((bf16[24,3584]{1,0:T(8,128)(2,1)S(1)}, bf16[24,3584]{1,0:T(8,128)(2,1)S(1)}, u32[]{:S(2)}, u32[]{:S(2)}) %collective-permute-start.31) | collective-permute-done | bytes 172064 | tf_op jit(solution)/shard_map/ppermute | solution.py:16
  74.7 1.2 %collective-permute-start.32 = (bf16[16,3584]{1,0:T(8,128)(2,1)S(1)}, bf16[16,3584]{1,0:T(8,128)(2,1)S(1)}, u32[]{:S(2)}, u32[]{:S(2)}) collective-permute-start(bf16[16,3584]{1,0:T(8,128)(2,1)S(1)} %slice.333), channel_id=1, source_target_pairs={{0,1},{1,0},{2,3},{3,2},{4,5},{5,4},{6,7},{7,6},{8,9},{9,8},{10,11... | collective-permute-start | bytes 344072 | tf_op jit(solution)/shard_map/ppermute | solution.py:16
  76.0 1.3 %collective-permute-done.28 = bf16[24,3584]{1,0:T(8,128)(2,1)S(1)} collective-permute-done((bf16[24,3584]{1,0:T(8,128)(2,1)S(1)}, bf16[24,3584]{1,0:T(8,128)(2,1)S(1)}, u32[]{:S(2)}, u32[]{:S(2)}) %collective-permute-start.28) | collective-permute-done | bytes 172064 | tf_op jit(solution)/shard_map/ppermute | solution.py:16
  77.3 1.8 %collective-permute-start.29 = (bf16[16,3584]{1,0:T(8,128)(2,1)S(1)}, bf16[16,3584]{1,0:T(8,128)(2,1)S(1)}, u32[]{:S(2)}, u32[]{:S(2)}) collective-permute-start(bf16[16,3584]{1,0:T(8,128)(2,1)S(1)} %slice.325), channel_id=1, source_target_pairs={{0,1},{1,0},{2,3},{3,2},{4,5},{5,4},{6,7},{7,6},{8,9},{9,8},{10,11... | collective-permute-start | bytes 344072 | tf_op jit(solution)/shard_map/ppermute | solution.py:16
  79.6 1.1 %collective-permute-start.33 = (bf16[8,3584]{1,0:T(8,128)(2,1)S(1)}, bf16[8,3584]{1,0:T(8,128)(2,1)S(1)}, u32[]{:S(2)}, u32[]{:S(2)}) collective-permute-start(bf16[8,3584]{1,0:T(8,128)(2,1)S(1)} %add_convert_fusion.9), channel_id=1, source_target_pairs={{0,2},{1,3},{2,0},{3,1},{4,6},{5,7},{6,4},{7,5},{8,10},{9,11},{10,... | collective-permute-start | bytes 172040 | tf_op jit(solution)/shard_map/ppermute | solution.py:16
  80.7 1.4 %collective-permute-done.29 = bf16[16,3584]{1,0:T(8,128)(2,1)S(1)} collective-permute-done((bf16[16,3584]{1,0:T(8,128)(2,1)S(1)}, bf16[16,3584]{1,0:T(8,128)(2,1)S(1)}, u32[]{:S(2)}, u32[]{:S(2)}) %collective-permute-start.29) | collective-permute-done | bytes 114720 | tf_op jit(solution)/shard_map/ppermute | solution.py:16
  82.2 1.4 %collective-permute-start.30 = (bf16[8,3584]{1,0:T(8,128)(2,1)S(1)}, bf16[8,3584]{1,0:T(8,128)(2,1)S(1)}, u32[]{:S(2)}, u32[]{:S(2)}) collective-permute-start(bf16[8,3584]{1,0:T(8,128)(2,1)S(1)} %add_convert_fusion.11), channel_id=1, source_target_pairs={{0,2},{1,3},{2,0},{3,1},{4,6},{5,7},{6,4},{7,5},{8,10},{9,11},{10,... | collective-permute-start | bytes 172040 | tf_op jit(solution)/shard_map/ppermute | solution.py:16
  83.6 1.2 %collective-permute-done.33 = bf16[8,3584]{1,0:T(8,128)(2,1)S(1)} collective-permute-done((bf16[8,3584]{1,0:T(8,128)(2,1)S(1)}, bf16[8,3584]{1,0:T(8,128)(2,1)S(1)}, u32[]{:S(2)}, u32[]{:S(2)}) %collective-permute-start.33) | collective-permute-done | bytes 57376 | tf_op jit(solution)/shard_map/ppermute | solution.py:16
  84.8 2.6 %collective-permute-done.30 = bf16[8,3584]{1,0:T(8,128)(2,1)S(1)} collective-permute-done((bf16[8,3584]{1,0:T(8,128)(2,1)S(1)}, bf16[8,3584]{1,0:T(8,128)(2,1)S(1)}, u32[]{:S(2)}, u32[]{:S(2)}) %collective-permute-start.30) | collective-permute-done | bytes 57376 | tf_op jit(solution)/shard_map/ppermute | solution.py:16
  (153 shorter events, 24.4 us)
Async XLA Ops:
  3.6 25.6 %collective-permute-start.2 = (bf16[16,7296]{1,0:T(8,128)(2,1)S(1)}, bf16[16,7296]{1,0:T(8,128)(2,1)S(1)}, u32[]{:S(2)}, u32[]{:S(2)}) collective-permute-start(bf16[16,7296]{1,0:T(8,128)(2,1)S(1)} %fusion.54), channel_id=1, source_target_pairs={{0,8},{4,12},{8,0},{12,4},{1,9},{5,13},{9,1},{13,5},{2,10},{6,14},... | collective-permute-start | bytes 700424 | tf_op jit(solution)/shard_map/ppermute | solution.py:16
  6.6 5.4 %collective-permute-start = (bf16[8,3712]{1,0:T(8,128)(2,1)S(1)}, bf16[8,3712]{1,0:T(8,128)(2,1)S(1)}, u32[]{:S(2)}, u32[]{:S(2)}) collective-permute-start(bf16[8,3712]{1,0:T(8,128)(2,1)S(1)} %get-tuple-element.27), channel_id=1, source_target_pairs={{0,2},{1,3},{2,0},{3,1},{4,6},{5,7},{6,4},{7,5},{8,10},{9,11},{10,... | collective-permute-start | bytes 178184 | tf_op jit(solution)/shard_map/ppermute | solution.py:16
  12.0 7.5 %collective-permute-start.18 = (bf16[8,3584]{1,0:T(8,128)(2,1)S(1)}, bf16[8,3584]{1,0:T(8,128)(2,1)S(1)}, u32[]{:S(2)}, u32[]{:S(2)}) collective-permute-start(bf16[8,3584]{1,0:T(8,128)(2,1)S(1)} %get-tuple-element.14), channel_id=1, source_target_pairs={{0,2},{1,3},{2,0},{3,1},{4,6},{5,7},{6,4},{7,5},{8,10},{9,11},{10,... | collective-permute-start | bytes 172040 | tf_op jit(solution)/shard_map/ppermute | solution.py:16
  14.4 9.2 %collective-permute-start.14 = (bf16[8,3712]{1,0:T(8,128)(2,1)S(1)}, bf16[8,3712]{1,0:T(8,128)(2,1)S(1)}, u32[]{:S(2)}, u32[]{:S(2)}) collective-permute-start(bf16[8,3712]{1,0:T(8,128)(2,1)S(1)} %get-tuple-element.12), channel_id=1, source_target_pairs={{0,2},{1,3},{2,0},{3,1},{4,6},{5,7},{6,4},{7,5},{8,10},{9,11},{10,... | collective-permute-start | bytes 178184 | tf_op jit(solution)/shard_map/ppermute | solution.py:16
  15.0 6.7 %collective-permute-start.5 = (bf16[8,3584]{1,0:T(8,128)(2,1)S(1)}, bf16[8,3584]{1,0:T(8,128)(2,1)S(1)}, u32[]{:S(2)}, u32[]{:S(2)}) collective-permute-start(bf16[8,3584]{1,0:T(8,128)(2,1)S(1)} %get-tuple-element.11), channel_id=1, source_target_pairs={{0,2},{1,3},{2,0},{3,1},{4,6},{5,7},{6,4},{7,5},{8,10},{9,11},{10,... | collective-permute-start | bytes 172040 | tf_op jit(solution)/shard_map/ppermute | solution.py:16
  17.4 6.5 %collective-permute-start.1 = (bf16[16,3712]{1,0:T(8,128)(2,1)S(1)}, bf16[16,3712]{1,0:T(8,128)(2,1)S(1)}, u32[]{:S(2)}, u32[]{:S(2)}) collective-permute-start(bf16[16,3712]{1,0:T(8,128)(2,1)S(1)} %pad_maximum_fusion.5), channel_id=1, source_target_pairs={{0,1},{1,0},{2,3},{3,2},{4,5},{5,4},{6,7},{7,6},{8,9},{9,8},{10,11... | collective-permute-start | bytes 356360 | tf_op jit(solution)/shard_map/ppermute | solution.py:16
  19.6 6.8 %collective-permute-start.19 = (bf16[16,3584]{1,0:T(8,128)(2,1)S(1)}, bf16[16,3584]{1,0:T(8,128)(2,1)S(1)}, u32[]{:S(2)}, u32[]{:S(2)}) collective-permute-start(bf16[16,3584]{1,0:T(8,128)(2,1)S(1)} %pad_maximum_fusion.8), channel_id=1, source_target_pairs={{0,1},{1,0},{2,3},{3,2},{4,5},{5,4},{6,7},{7,6},{8,9},{9,8},{10,11... | collective-permute-start | bytes 344072 | tf_op jit(solution)/shard_map/ppermute | solution.py:16
  21.6 6.9 %collective-permute-start.6 = (bf16[16,3584]{1,0:T(8,128)(2,1)S(1)}, bf16[16,3584]{1,0:T(8,128)(2,1)S(1)}, u32[]{:S(2)}, u32[]{:S(2)}) collective-permute-start(bf16[16,3584]{1,0:T(8,128)(2,1)S(1)} %pad_maximum_fusion.7), channel_id=1, source_target_pairs={{0,1},{1,0},{2,3},{3,2},{4,5},{5,4},{6,7},{7,6},{8,9},{9,8},{10,11... | collective-permute-start | bytes 344072 | tf_op jit(solution)/shard_map/ppermute | solution.py:16
  23.6 6.1 %collective-permute-start.15 = (bf16[16,3712]{1,0:T(8,128)(2,1)S(1)}, bf16[16,3712]{1,0:T(8,128)(2,1)S(1)}, u32[]{:S(2)}, u32[]{:S(2)}) collective-permute-start(bf16[16,3712]{1,0:T(8,128)(2,1)S(1)} %pad_maximum_fusion.6), channel_id=1, source_target_pairs={{0,1},{1,0},{2,3},{3,2},{4,5},{5,4},{6,7},{7,6},{8,9},{9,8},{10,11... | collective-permute-start | bytes 356360 | tf_op jit(solution)/shard_map/ppermute | solution.py:16
  23.9 7.5 %collective-permute-start.3 = (bf16[24,3712]{1,0:T(8,128)(2,1)S(1)}, bf16[24,3712]{1,0:T(8,128)(2,1)S(1)}, u32[]{:S(2)}, u32[]{:S(2)}) collective-permute-start(bf16[24,3712]{1,0:T(8,128)(2,1)S(1)} %pad_maximum_fusion.1), channel_id=1, source_target_pairs={{0,8},{4,12},{8,0},{12,4},{1,9},{5,13},{9,1},{13,5},{2,10},{6,14},... | collective-permute-start | bytes 534536 | tf_op jit(solution)/shard_map/ppermute | solution.py:16
  26.4 11.4 %collective-permute-start.20 = (bf16[24,3584]{1,0:T(8,128)(2,1)S(1)}, bf16[24,3584]{1,0:T(8,128)(2,1)S(1)}, u32[]{:S(2)}, u32[]{:S(2)}) collective-permute-start(bf16[24,3584]{1,0:T(8,128)(2,1)S(1)} %pad_maximum_fusion.4), channel_id=1, source_target_pairs={{0,8},{4,12},{8,0},{12,4},{1,9},{5,13},{9,1},{13,5},{2,10},{6,14},... | collective-permute-start | bytes 516104 | tf_op jit(solution)/shard_map/ppermute | solution.py:16
  28.5 9.1 %collective-permute-start.7 = (bf16[24,3584]{1,0:T(8,128)(2,1)S(1)}, bf16[24,3584]{1,0:T(8,128)(2,1)S(1)}, u32[]{:S(2)}, u32[]{:S(2)}) collective-permute-start(bf16[24,3584]{1,0:T(8,128)(2,1)S(1)} %pad_maximum_fusion.3), channel_id=1, source_target_pairs={{0,8},{4,12},{8,0},{12,4},{1,9},{5,13},{9,1},{13,5},{2,10},{6,14},... | collective-permute-start | bytes 516104 | tf_op jit(solution)/shard_map/ppermute | solution.py:16
  29.8 9.8 %collective-permute-start.16 = (bf16[24,3712]{1,0:T(8,128)(2,1)S(1)}, bf16[24,3712]{1,0:T(8,128)(2,1)S(1)}, u32[]{:S(2)}, u32[]{:S(2)}) collective-permute-start(bf16[24,3712]{1,0:T(8,128)(2,1)S(1)} %pad_maximum_fusion.2), channel_id=1, source_target_pairs={{0,8},{4,12},{8,0},{12,4},{1,9},{5,13},{9,1},{13,5},{2,10},{6,14},... | collective-permute-start | bytes 534536 | tf_op jit(solution)/shard_map/ppermute | solution.py:16
  31.4 8.1 %collective-permute-start.4 = (bf16[64,3712]{1,0:T(8,128)(2,1)S(1)}, bf16[64,3712]{1,0:T(8,128)(2,1)S(1)}, u32[]{:S(2)}, u32[]{:S(2)}) collective-permute-start(bf16[64,3712]{1,0:T(8,128)(2,1)S(1)} %get-tuple-element.37), channel_id=1, source_target_pairs={{0,4},{4,0},{8,12},{12,8},{1,5},{5,1},{9,13},{13,9},{2,6},{6,2},{1... | collective-permute-start | bytes 1425416 | tf_op jit(solution)/shard_map/ppermute | solution.py:16
  46.2 5.5 %collective-permute-start.21 = (bf16[64,3584]{1,0:T(8,128)(2,1)S(1)}, bf16[64,3584]{1,0:T(8,128)(2,1)S(1)}, u32[]{:S(2)}, u32[]{:S(2)}) collective-permute-start(bf16[64,3584]{1,0:T(8,128)(2,1)S(1)} %constant_dynamic-update-slice_fusion.29), channel_id=1, source_target_pairs={{0,4},{4,0},{8,12},{12,8},{1,5},{5,1},{9,13},{13,9},{2,6},{6,2},{1... | collective-permute-start | bytes 1376264 | tf_op jit(solution)/shard_map/ppermute | solution.py:16
  46.9 2.5 %collective-permute-start.9 = (bf16[64,3584]{1,0:T(8,128)(2,1)S(1)}, bf16[64,3584]{1,0:T(8,128)(2,1)S(1)}, u32[]{:S(2)}, u32[]{:S(2)}) collective-permute-start(bf16[64,3584]{1,0:T(8,128)(2,1)S(1)} %slice.287), channel_id=1, source_target_pairs={{0,4},{4,0},{8,12},{12,8},{1,5},{5,1},{9,13},{13,9},{2,6},{6,2},{1... | collective-permute-start | bytes 1376264 | tf_op jit(solution)/shard_map/ppermute | solution.py:16
  47.0 6.1 %collective-permute-start.17 = (bf16[64,3712]{1,0:T(8,128)(2,1)S(1)}, bf16[64,3712]{1,0:T(8,128)(2,1)S(1)}, u32[]{:S(2)}, u32[]{:S(2)}) collective-permute-start(bf16[64,3712]{1,0:T(8,128)(2,1)S(1)} %constant_dynamic-update-slice_fusion.22), channel_id=1, source_target_pairs={{0,4},{4,0},{8,12},{12,8},{1,5},{5,1},{9,13},{13,9},{2,6},{6,2},{1... | collective-permute-start | bytes 1425416 | tf_op jit(solution)/shard_map/ppermute | solution.py:16
  49.6 7.3 %collective-permute-start.25 = (bf16[24,3584]{1,0:T(8,128)(2,1)S(1)}, bf16[24,3584]{1,0:T(8,128)(2,1)S(1)}, u32[]{:S(2)}, u32[]{:S(2)}) collective-permute-start(bf16[24,3584]{1,0:T(8,128)(2,1)S(1)} %slice.316), channel_id=1, source_target_pairs={{0,8},{4,12},{8,0},{12,4},{1,9},{5,13},{9,1},{13,5},{2,10},{6,14},... | collective-permute-start | bytes 516104 | tf_op jit(solution)/shard_map/ppermute | solution.py:16
  50.2 9.6 %collective-permute-start.10 = (bf16[24,3584]{1,0:T(8,128)(2,1)S(1)}, bf16[24,3584]{1,0:T(8,128)(2,1)S(1)}, u32[]{:S(2)}, u32[]{:S(2)}) collective-permute-start(bf16[24,3584]{1,0:T(8,128)(2,1)S(1)} %slice.290), channel_id=1, source_target_pairs={{0,8},{4,12},{8,0},{12,4},{1,9},{5,13},{9,1},{13,5},{2,10},{6,14},... | collective-permute-start | bytes 516104 | tf_op jit(solution)/shard_map/ppermute | solution.py:16
  56.1 10.9 %collective-permute-start.23 = (bf16[64,3584]{1,0:T(8,128)(2,1)S(1)}, bf16[64,3584]{1,0:T(8,128)(2,1)S(1)}, u32[]{:S(2)}, u32[]{:S(2)}) collective-permute-start(bf16[64,3584]{1,0:T(8,128)(2,1)S(1)} %slice.311), channel_id=1, source_target_pairs={{0,4},{4,0},{8,12},{12,8},{1,5},{5,1},{9,13},{13,9},{2,6},{6,2},{1... | collective-permute-start | bytes 1376264 | tf_op jit(solution)/shard_map/ppermute | solution.py:16
  56.2 11.0 %collective-permute-start.22 = (bf16[64,3584]{1,0:T(8,128)(2,1)S(1)}, bf16[64,3584]{1,0:T(8,128)(2,1)S(1)}, u32[]{:S(2)}, u32[]{:S(2)}) collective-permute-start(bf16[64,3584]{1,0:T(8,128)(2,1)S(1)} %slice.308), channel_id=1, source_target_pairs={{0,4},{4,0},{8,12},{12,8},{1,5},{5,1},{9,13},{13,9},{2,6},{6,2},{1... | collective-permute-start | bytes 1376264 | tf_op jit(solution)/shard_map/ppermute | solution.py:16
  57.0 5.2 %collective-permute-start.26 = (bf16[16,3584]{1,0:T(8,128)(2,1)S(1)}, bf16[16,3584]{1,0:T(8,128)(2,1)S(1)}, u32[]{:S(2)}, u32[]{:S(2)}) collective-permute-start(bf16[16,3584]{1,0:T(8,128)(2,1)S(1)} %slice.317), channel_id=1, source_target_pairs={{0,1},{1,0},{2,3},{3,2},{4,5},{5,4},{6,7},{7,6},{8,9},{9,8},{10,11... | collective-permute-start | bytes 344072 | tf_op jit(solution)/shard_map/ppermute | solution.py:16
  59.8 5.1 %collective-permute-start.11 = (bf16[16,3584]{1,0:T(8,128)(2,1)S(1)}, bf16[16,3584]{1,0:T(8,128)(2,1)S(1)}, u32[]{:S(2)}, u32[]{:S(2)}) collective-permute-start(bf16[16,3584]{1,0:T(8,128)(2,1)S(1)} %slice.291), channel_id=1, source_target_pairs={{0,1},{1,0},{2,3},{3,2},{4,5},{5,4},{6,7},{7,6},{8,9},{9,8},{10,11... | collective-permute-start | bytes 344072 | tf_op jit(solution)/shard_map/ppermute | solution.py:16
  62.2 21.4 %collective-permute-start.27 = (bf16[8,3584]{1,0:T(8,128)(2,1)S(1)}, bf16[8,3584]{1,0:T(8,128)(2,1)S(1)}, u32[]{:S(2)}, u32[]{:S(2)}) collective-permute-start(bf16[8,3584]{1,0:T(8,128)(2,1)S(1)} %add_convert_fusion.13), channel_id=1, source_target_pairs={{0,2},{1,3},{2,0},{3,1},{4,6},{5,7},{6,4},{7,5},{8,10},{9,11},{10,... | collective-permute-start | bytes 172040 | tf_op jit(solution)/shard_map/ppermute | solution.py:16
  65.0 18.6 %collective-permute-start.12 = (bf16[8,3584]{1,0:T(8,128)(2,1)S(1)}, bf16[8,3584]{1,0:T(8,128)(2,1)S(1)}, u32[]{:S(2)}, u32[]{:S(2)}) collective-permute-start(bf16[8,3584]{1,0:T(8,128)(2,1)S(1)} %add_convert_fusion.15), channel_id=1, source_target_pairs={{0,2},{1,3},{2,0},{3,1},{4,6},{5,7},{6,4},{7,5},{8,10},{9,11},{10,... | collective-permute-start | bytes 172040 | tf_op jit(solution)/shard_map/ppermute | solution.py:16
  67.3 7.4 %collective-permute-start.31 = (bf16[24,3584]{1,0:T(8,128)(2,1)S(1)}, bf16[24,3584]{1,0:T(8,128)(2,1)S(1)}, u32[]{:S(2)}, u32[]{:S(2)}) collective-permute-start(bf16[24,3584]{1,0:T(8,128)(2,1)S(1)} %slice.332), channel_id=1, source_target_pairs={{0,8},{4,12},{8,0},{12,4},{1,9},{5,13},{9,1},{13,5},{2,10},{6,14},... | collective-permute-start | bytes 516104 | tf_op jit(solution)/shard_map/ppermute | solution.py:16
  67.9 9.3 %collective-permute-start.28 = (bf16[24,3584]{1,0:T(8,128)(2,1)S(1)}, bf16[24,3584]{1,0:T(8,128)(2,1)S(1)}, u32[]{:S(2)}, u32[]{:S(2)}) collective-permute-start(bf16[24,3584]{1,0:T(8,128)(2,1)S(1)} %slice.324), channel_id=1, source_target_pairs={{0,8},{4,12},{8,0},{12,4},{1,9},{5,13},{9,1},{13,5},{2,10},{6,14},... | collective-permute-start | bytes 516104 | tf_op jit(solution)/shard_map/ppermute | solution.py:16
  69.4 14.2 %collective-permute-start.24 = (bf16[16,7168]{1,0:T(8,128)(2,1)S(1)}, bf16[16,7168]{1,0:T(8,128)(2,1)S(1)}, u32[]{:S(2)}, u32[]{:S(2)}) collective-permute-start(bf16[16,7168]{1,0:T(8,128)(2,1)S(1)} %maximum_maximum_fusion), channel_id=1, source_target_pairs={{0,8},{4,12},{8,0},{12,4},{1,9},{5,13},{9,1},{13,5},{2,10},{6,14},... | collective-permute-start | bytes 688136 | tf_op jit(solution)/shard_map/ppermute | solution.py:16
  74.7 4.9 %collective-permute-start.32 = (bf16[16,3584]{1,0:T(8,128)(2,1)S(1)}, bf16[16,3584]{1,0:T(8,128)(2,1)S(1)}, u32[]{:S(2)}, u32[]{:S(2)}) collective-permute-start(bf16[16,3584]{1,0:T(8,128)(2,1)S(1)} %slice.333), channel_id=1, source_target_pairs={{0,1},{1,0},{2,3},{3,2},{4,5},{5,4},{6,7},{7,6},{8,9},{9,8},{10,11... | collective-permute-start | bytes 344072 | tf_op jit(solution)/shard_map/ppermute | solution.py:16
  77.3 4.9 %collective-permute-start.29 = (bf16[16,3584]{1,0:T(8,128)(2,1)S(1)}, bf16[16,3584]{1,0:T(8,128)(2,1)S(1)}, u32[]{:S(2)}, u32[]{:S(2)}) collective-permute-start(bf16[16,3584]{1,0:T(8,128)(2,1)S(1)} %slice.325), channel_id=1, source_target_pairs={{0,1},{1,0},{2,3},{3,2},{4,5},{5,4},{6,7},{7,6},{8,9},{9,8},{10,11... | collective-permute-start | bytes 344072 | tf_op jit(solution)/shard_map/ppermute | solution.py:16
  79.6 5.1 %collective-permute-start.33 = (bf16[8,3584]{1,0:T(8,128)(2,1)S(1)}, bf16[8,3584]{1,0:T(8,128)(2,1)S(1)}, u32[]{:S(2)}, u32[]{:S(2)}) collective-permute-start(bf16[8,3584]{1,0:T(8,128)(2,1)S(1)} %add_convert_fusion.9), channel_id=1, source_target_pairs={{0,2},{1,3},{2,0},{3,1},{4,6},{5,7},{6,4},{7,5},{8,10},{9,11},{10,... | collective-permute-start | bytes 172040 | tf_op jit(solution)/shard_map/ppermute | solution.py:16
  82.2 5.1 %collective-permute-start.30 = (bf16[8,3584]{1,0:T(8,128)(2,1)S(1)}, bf16[8,3584]{1,0:T(8,128)(2,1)S(1)}, u32[]{:S(2)}, u32[]{:S(2)}) collective-permute-start(bf16[8,3584]{1,0:T(8,128)(2,1)S(1)} %add_convert_fusion.11), channel_id=1, source_target_pairs={{0,2},{1,3},{2,0},{3,1},{4,6},{5,7},{6,4},{7,5},{8,10},{9,11},{10,... | collective-permute-start | bytes 172040 | tf_op jit(solution)/shard_map/ppermute | solution.py:16
  (13 other events, 156.1 us)

commit v3 on v2

v3 whole, which is shorter than its diff:
```python
import functools

import jax
import jax.numpy as jnp
from jax import lax
from jax.experimental import pallas as pl
from jax.experimental.pallas import tpu as pltpu
from jax.sharding import PartitionSpec as P

routed_scale = 2.5
column_parts = 2
F_Z2 = 2
F_XORD = 1
F_C1 = 1
F_RLAG = 0
F_Z2R = 2
F_CHOLD = 1


def bits_of(count):
    return [1 << b for b in reversed(range(count.bit_length() - 1))]


def swap(value, axis_name, bit):
    count = lax.axis_size(axis_name)
    return lax.ppermute(value, axis_name, [(i, i ^ bit) for i in range(count)])


def after(value, *others):
    return lax.optimization_barrier((value, *others))[0] if others else value


def join(*parts):
    return jnp.concatenate(parts, axis=0)


def add_up(*terms):
    total = terms[0].astype(jnp.float32)
    for term in terms[1:]:
        total = total + term.astype(jnp.float32)
    return total


def prepare_kernel(ep_count, extra, width, codes_ref, scales_ref, ids_ref, gates_ref, all_ref, *part_refs):
    steps_here, rows, features = codes_ref.shape
    blocks = scales_ref.shape[2]
    size = features // blocks
    lane = lax.broadcasted_iota(jnp.int32, (rows, extra), 1)
    expert = lax.rem(lane, ep_count)
    whole = [[], []]
    for step in range(steps_here):
        ids, gates = ids_ref[step], gates_ref[step]
        code = jnp.zeros((rows, extra), jnp.int32)
        for route in range(ids.shape[1]):
            here = jnp.broadcast_to(ids[:, route : route + 1], (rows, extra)) == expert
            code += jnp.where(here, jnp.broadcast_to(gates[:, route : route + 1], (rows, extra)), 0)
        low = code & 15
        sent = jnp.where(lane < ep_count, code - low, jnp.where(lane < 2 * ep_count, low, 0))
        pieces = [sent.astype(jnp.float32)]
        scales = scales_ref[step]
        codes = codes_ref[step].astype(jnp.float32)
        for b in range(blocks):
            pieces.append(codes[:, b * size : (b + 1) * size] * jnp.broadcast_to(scales[:, b : b + 1], (rows, size)))
        row = jnp.concatenate(pieces, axis=1)
        whole[step % 2].append(row)
        count = (features // width)
        for k in range(count):
            low_at = 0 if k == 0 else extra + k * width
            part_refs[step * count + k][...] = row[:, low_at : extra + (k + 1) * width].astype(jnp.bfloat16)
    every = [row for pair in zip(*whole) for row in pair]
    all_ref[...] = jnp.concatenate(every, axis=0).astype(jnp.bfloat16)


def prepare(row_codes, row_scales, expert_ids, gate_codes, ep_count, width):
    steps_here, rows, features = row_codes.shape
    extra = -(-2 * ep_count // 128) * 128
    count = features // width
    shapes = [jax.ShapeDtypeStruct((steps_here * rows, features + extra), jnp.bfloat16)]
    for step in range(steps_here):
        for k in range(count):
            shapes.append(jax.ShapeDtypeStruct((rows, width + (extra if k == 0 else 0)), jnp.bfloat16))
    outs = pl.pallas_call(
        functools.partial(prepare_kernel, ep_count, extra, width),
        out_shape=shapes,
        compiler_params=pltpu.CompilerParams(vmem_limit_bytes=16 << 20),
    )(row_codes, row_scales, expert_ids, gate_codes)
    return outs[0], outs[1:], extra


def body(row_codes, row_scales, expert_ids, gate_codes, w_gate, w_up, w_down):
    ep_count = lax.axis_size("ep")
    sub_bits = bits_of(lax.axis_size("sub"))
    ep_bits = bits_of(ep_count)
    steps_here, rows, features = row_codes.shape
    width = features // column_parts
    tokens, owns, extra = prepare(row_codes, row_scales, expert_ids, gate_codes, ep_count, width)
    crossed = swap(tokens, "ep", ep_bits[0])
    me = lax.axis_index("ep")
    z2s, z1s, xs = [], [], []
    own_gives = []
    waiting = []
    step_done, core_back = [], []
    returned = []
    gathered = []
    for step in range(steps_here):
        for k in range(column_parts):
            c = step * column_parts + k
            low = 0 if k == 0 else extra + k * width
            block = (slice(step * rows, (step + 1) * rows), slice(low, extra + (k + 1) * width))
            part = owns[c]
            for n, bit in enumerate(sub_bits):
                if n == 0:
                    if F_Z2 == 0 and c >= 1:
                        part = after(part, z2s[0])
                    if F_Z2 == 1 and c >= 2:
                        part = after(part, z1s[0])
                    if F_Z2 == 2 and c >= 2:
                        part = after(part, z2s[1])
                    if F_Z2 == 3 and c >= 2:
                        part = after(part, z2s[0])
                came = swap(part, "sub", bit)
                if n == 0:
                    z2s.append(came)
                if n == 1:
                    z1s.append(came)
                part = join(part, came)
            give = part[rows:]
            if F_XORD and c >= 2:
                give = after(give, xs[c - 2])
            xs.append(swap(give, "ep", ep_bits[0]))
            part = join(part, crossed[block], xs[-1])
            gathered.append((part, low))
    for step in range(steps_here):
        gate_value = up_value = 0.0
        for k in range(column_parts):
            part, low = gathered[step * column_parts + k]
            for bit in ep_bits[1:]:
                if F_C1:
                    part = after(part, *step_done)
                part = join(part, swap(part, "ep", bit))
            if F_CHOLD and core_back:
                part = after(part, *core_back)
            if k == 0:
                sent = part[:, : 2 * ep_count].astype(jnp.float32)
                dense = sent[:, :ep_count] + sent[:, ep_count:]
                total = jnp.sum(dense, axis=1, keepdims=True)
                mine = jnp.sum(jnp.where(jnp.arange(ep_count) == me, dense, 0.0), axis=1, keepdims=True)
                weight = routed_scale * mine / total
            inputs = part[:, extra - low :] if k == 0 else part
            span = slice(k * width, (k + 1) * width)
            gate_value += jnp.dot(inputs, w_gate[0, span], preferred_element_type=jnp.float32)
            up_value += jnp.dot(inputs, w_up[0, span], preferred_element_type=jnp.float32)
        hidden = (jax.nn.silu(gate_value) * up_value).astype(jnp.bfloat16)
        step_done = []
        core_back = []
        for k in range(column_parts):
            span = slice(k * width, (k + 1) * width)
            held = jnp.dot(hidden, w_down[0, :, span], preferred_element_type=jnp.float32)
            held = (held * weight).astype(jnp.bfloat16)
            step_done.append(held)
            for bit in reversed(ep_bits[1:]):
                half = held.shape[0] // 2
                held = add_up(held[:half], swap(held[half:], "ep", bit)).astype(jnp.bfloat16)
            core_back.append(held)
            returned.append(held)
    finals = []
    for c, held in enumerate(returned):
        half = held.shape[0] // 2
        give = held[half + rows :]
        if F_RLAG and len(waiting) >= F_RLAG:
            give = after(give, waiting[-F_RLAG])
        own_gives.append(held[half : half + rows])
        own = [held[:rows]]
        rest = add_up(held[rows:half], swap(give, "ep", ep_bits[0])).astype(jnp.bfloat16)
        for n, bit in enumerate(reversed(sub_bits)):
            half = (rest.shape[0] + rows) // 2
            give = rest[half - rows :]
            if F_Z2R == 1 and n == 1 and c == 0:
                give = after(give, *returned[2:])
            if F_Z2R == 2 and n == 0 and c == 0:
                give = after(give, *returned[2:])
            came = swap(give, "sub", bit)
            if n == 0:
                waiting.append(came)
            own.append(came[:rows])
            if half > rows:
                rest = add_up(rest[: half - rows], came[rows:]).astype(jnp.bfloat16)
        finals.append(own)
    by_step = [own_gives[s * column_parts : (s + 1) * column_parts] for s in range(steps_here)]
    crossed = swap(join(*[jnp.concatenate(gives, axis=1) for gives in by_step]), "ep", ep_bits[0])
    results = []
    for step in range(steps_here):
        outs = []
        for k in range(column_parts):
            own = finals[step * column_parts + k]
            block = (slice(step * rows, (step + 1) * rows), slice(k * width, (k + 1) * width))
            outs.append(add_up(*own, crossed[block]).astype(jnp.bfloat16))
        results.append(jnp.concatenate(outs, axis=1))
    return jnp.stack(results)


def solution(mesh):
    rows = P(None, ("groups", "ep", "sub"), None)
    return jax.shard_map(
        body,
        mesh=mesh,
        in_specs=(rows, rows, rows, rows, P("ep", None, "sub"), P("ep", None, "sub"), P("ep", "sub", None)),
        out_specs=rows,
        check_vma=False,
    )
```

time: 88.5 us -> 85.1 us (0.962)
  waiting for transfers between devices: 35.7 us -> 17.7 us
  starting transfers between devices: 35.3 us -> 44.2 us
  local copies, waits for them, and re-layouts: 5.51 us -> 9.66 us
  matrix products: 7.81 us -> 10.3 us
  other arithmetic: 3.21 us -> 2.2 us
    ppermute x34, waiting for transfers between devices: 35.7 us -> 17.7 us  [swap(): return lax.ppermute(value, axis_name, [(i, i ^ bit) for i in range(count)])]
    ppermute x34, starting transfers between devices: 35.3 us -> 44.2 us  [swap(): return lax.ppermute(value, axis_name, [(i, i ^ bit) for i in range(count)])]
    unnamed x36 -> x40, local copies, waits for them, and re-layouts: 3.98 us -> 7.81 us
    dot_general x4, matrix products: 2.58 us -> 5.04 us  [body(): jnp.dot(inputs, w_up[0, span], preferred_element_type=jnp.float32)]
    concatenate x8 -> x6, local copies, waits for them, and re-layouts: 0.23 us -> 1.61 us  [join(): return jnp.concatenate(parts, axis=0)]
    convert_element_type x1 -> x0, other arithmetic: 1.03 us -> none  [dequantize(): return scaled.reshape(codes.shape[0], -1).astype(jnp.bfloat16)]
  transfers between devices with their start and end apart: 34 -> 34, of which waited for: 20 -> 15; matrix products, arithmetic and copies ran while one was open for 7% -> 19% of each run, Pallas kernels for 0% -> 0%
where the time goes in v3:
time: 85.1 us; the launch traced here: 84.9 us
  starting transfers between devices  44.2 us (52%)
  waiting for transfers between devices  17.7 us (21%)
  matrix products  10.3 us (12%)
  local copies, waits for them, and re-layouts  9.66 us (11%)
  other arithmetic  2.2 us (3%)
    ppermute x34, starting transfers between devices, swap(): return lax.ppermute(value, axis_name, [(i, i ^ bit) for i in range(count)])  44.2 us
    ppermute x34, waiting for transfers between devices, swap(): return lax.ppermute(value, axis_name, [(i, i ^ bit) for i in range(count)])  17.7 us
    unnamed x40, local copies, waits for them, and re-layouts  7.81 us
    dot_general x4, matrix products, body(): jnp.dot(inputs, w_up[0, span], preferred_element_type=jnp.float32)  5.04 us
    dot_general x4, matrix products, body(): jnp.dot(hidden, w_down[0, :, span], preferred_element_type=jnp.float32)  2.73 us
    dot_general x4, matrix products, body(): jnp.dot(inputs, w_gate[0, span], preferred_element_type=jnp.float32)  2.56 us
  transfers between devices with their start and end apart: 34, of which 15 were waited for; matrix products, arithmetic and copies ran while one was open for 19% of the time, Pallas kernels for 0%

profile of v3, /device:TPU:0, one launch (start us, length us, event | category | flops | bytes accessed | tf_op | source)
XLA Modules:
  0.0 84.9 jit_solution(9867947220164611583)
XLA Ops:
  1.5 0.9 %copy-done = bf16[2,8,7168]{2,1,0:T(8,128)(2,1)S(1)} copy-done((bf16[2,8,7168]{2,1,0:T(8,128)(2,1)S(1)}, bf16[2,8,7168]{2,1,0:T(8,128)(2,1)}, u32[]{:S(2)}) %copy-start) | copy-done | bytes 229400
  3.4 4.1 %collective-permute-start.5 = (bf16[8,3584]{1,0:T(8,128)(2,1)S(1)}, bf16[8,3584]{1,0:T(8,128)(2,1)S(1)}, u32[]{:S(2)}, u32[]{:S(2)}) collective-permute-start(bf16[8,3584]{1,0:T(8,128)(2,1)S(1)} %get-tuple-element.21), channel_id=1, source_target_pairs={{0,2},{1,3},{2,0},{3,1},{4,6},{5,7},{6,4},{7,5},{8,10},{9,11},{10,... | collective-permute-start | bytes 172040 | tf_op jit(solution)/shard_map/ppermute | solution.py:26
  7.6 1.7 %collective-permute-start.2 = (bf16[16,7296]{1,0:T(8,128)(2,1)S(1)}, bf16[16,7296]{1,0:T(8,128)(2,1)S(1)}, u32[]{:S(2)}, u32[]{:S(2)}) collective-permute-start(bf16[16,7296]{1,0:T(8,128)(2,1)S(1)} %get-tuple-element.20), channel_id=1, source_target_pairs={{0,8},{4,12},{8,0},{12,4},{1,9},{5,13},{9,1},{13,5},{2,10},{6,14},... | collective-permute-start | bytes 700424 | tf_op jit(solution)/shard_map/ppermute | solution.py:26
  10.3 2.5 %collective-permute-start.16 = (bf16[8,3584]{1,0:T(8,128)(2,1)S(1)}, bf16[8,3584]{1,0:T(8,128)(2,1)S(1)}, u32[]{:S(2)}, u32[]{:S(2)}) collective-permute-start(bf16[8,3584]{1,0:T(8,128)(2,1)S(1)} %get-tuple-element.28), channel_id=1, source_target_pairs={{0,2},{1,3},{2,0},{3,1},{4,6},{5,7},{6,4},{7,5},{8,10},{9,11},{10,... | collective-permute-start | bytes 172040 | tf_op jit(solution)/shard_map/ppermute | solution.py:26
  13.9 3.0 %collective-permute-start.6 = (bf16[16,3584]{1,0:T(8,128)(2,1)S(1)}, bf16[16,3584]{1,0:T(8,128)(2,1)S(1)}, u32[]{:S(2)}, u32[]{:S(2)}) collective-permute-start(bf16[16,3584]{1,0:T(8,128)(2,1)S(1)} %pad_maximum_fusion.9), channel_id=1, source_target_pairs={{0,1},{1,0},{2,3},{3,2},{4,5},{5,4},{6,7},{7,6},{8,9},{9,8},{10,11... | collective-permute-start | bytes 344072 | tf_op jit(solution)/shard_map/ppermute | solution.py:26
  17.0 2.1 %collective-permute-start.17 = (bf16[16,3584]{1,0:T(8,128)(2,1)S(1)}, bf16[16,3584]{1,0:T(8,128)(2,1)S(1)}, u32[]{:S(2)}, u32[]{:S(2)}) collective-permute-start(bf16[16,3584]{1,0:T(8,128)(2,1)S(1)} %pad_maximum_fusion.10), channel_id=1, source_target_pairs={{0,1},{1,0},{2,3},{3,2},{4,5},{5,4},{6,7},{7,6},{8,9},{9,8},{10,11... | collective-permute-start | bytes 344072 | tf_op jit(solution)/shard_map/ppermute | solution.py:26
  19.1 2.8 %collective-permute-start.12 = (bf16[16,3712]{1,0:T(8,128)(2,1)S(1)}, bf16[16,3712]{1,0:T(8,128)(2,1)S(1)}, u32[]{:S(2)}, u32[]{:S(2)}) collective-permute-start(bf16[16,3712]{1,0:T(8,128)(2,1)S(1)} %pad_maximum_fusion.8), channel_id=1, source_target_pairs={{0,1},{1,0},{2,3},{3,2},{4,5},{5,4},{6,7},{7,6},{8,9},{9,8},{10,11... | collective-permute-start | bytes 356360 | tf_op jit(solution)/shard_map/ppermute | solution.py:26
  21.9 1.6 %collective-permute-start.7 = (bf16[24,3584]{1,0:T(8,128)(2,1)S(1)}, bf16[24,3584]{1,0:T(8,128)(2,1)S(1)}, u32[]{:S(2)}, u32[]{:S(2)}) collective-permute-start(bf16[24,3584]{1,0:T(8,128)(2,1)S(1)} %pad_maximum_fusion.5), channel_id=1, source_target_pairs={{0,8},{4,12},{8,0},{12,4},{1,9},{5,13},{9,1},{13,5},{2,10},{6,14},... | collective-permute-start | bytes 516104 | tf_op jit(solution)/shard_map/ppermute | solution.py:26
  24.2 0.9 %collective-permute-start.3 = (bf16[24,3712]{1,0:T(8,128)(2,1)S(1)}, bf16[24,3712]{1,0:T(8,128)(2,1)S(1)}, u32[]{:S(2)}, u32[]{:S(2)}) collective-permute-start(bf16[24,3712]{1,0:T(8,128)(2,1)S(1)} %pad_maximum_fusion.3), channel_id=1, source_target_pairs={{0,8},{4,12},{8,0},{12,4},{1,9},{5,13},{9,1},{13,5},{2,10},{6,14},... | collective-permute-start | bytes 534536 | tf_op jit(solution)/shard_map/ppermute | solution.py:26
  25.1 0.9 %collective-permute-done.17 = bf16[16,3584]{1,0:T(8,128)(2,1)S(1)} collective-permute-done((bf16[16,3584]{1,0:T(8,128)(2,1)S(1)}, bf16[16,3584]{1,0:T(8,128)(2,1)S(1)}, u32[]{:S(2)}, u32[]{:S(2)}) %collective-permute-start.17) | collective-permute-done | bytes 114720 | tf_op jit(solution)/shard_map/ppermute | solution.py:26
  26.6 1.4 %collective-permute-done.12 = bf16[16,3712]{1,0:T(8,128)(2,1)S(1)} collective-permute-done((bf16[16,3712]{1,0:T(8,128)(2,1)S(1)}, bf16[16,3712]{1,0:T(8,128)(2,1)S(1)}, u32[]{:S(2)}, u32[]{:S(2)}) %collective-permute-start.12) | collective-permute-done | bytes 118816 | tf_op jit(solution)/shard_map/ppermute | solution.py:26
  28.1 1.0 %collective-permute-done.7 = bf16[24,3584]{1,0:T(8,128)(2,1)S(1)} collective-permute-done((bf16[24,3584]{1,0:T(8,128)(2,1)S(1)}, bf16[24,3584]{1,0:T(8,128)(2,1)S(1)}, u32[]{:S(2)}, u32[]{:S(2)}) %collective-permute-start.7) | collective-permute-done | bytes 172064 | tf_op jit(solution)/shard_map/ppermute | solution.py:26
  29.1 1.5 %collective-permute-start.18 = (bf16[24,3584]{1,0:T(8,128)(2,1)S(1)}, bf16[24,3584]{1,0:T(8,128)(2,1)S(1)}, u32[]{:S(2)}, u32[]{:S(2)}) collective-permute-start(bf16[24,3584]{1,0:T(8,128)(2,1)S(1)} %pad_maximum_fusion.6), channel_id=1, source_target_pairs={{0,8},{4,12},{8,0},{12,4},{1,9},{5,13},{9,1},{13,5},{2,10},{6,14},... | collective-permute-start | bytes 516104 | tf_op jit(solution)/shard_map/ppermute | solution.py:26
  31.5 1.5 %collective-permute-start.13 = (bf16[24,3712]{1,0:T(8,128)(2,1)S(1)}, bf16[24,3712]{1,0:T(8,128)(2,1)S(1)}, u32[]{:S(2)}, u32[]{:S(2)}) collective-permute-start(bf16[24,3712]{1,0:T(8,128)(2,1)S(1)} %pad_maximum_fusion.4), channel_id=1, source_target_pairs={{0,8},{4,12},{8,0},{12,4},{1,9},{5,13},{9,1},{13,5},{2,10},{6,14},... | collective-permute-start | bytes 534536 | tf_op jit(solution)/shard_map/ppermute | solution.py:26
  33.1 1.9 %collective-permute-done.18 = bf16[24,3584]{1,0:T(8,128)(2,1)S(1)} collective-permute-done((bf16[24,3584]{1,0:T(8,128)(2,1)S(1)}, bf16[24,3584]{1,0:T(8,128)(2,1)S(1)}, u32[]{:S(2)}, u32[]{:S(2)}) %collective-permute-start.18) | collective-permute-done | bytes 172064 | tf_op jit(solution)/shard_map/ppermute | solution.py:26
  35.8 3.1 %fusion.10 = f32[128,512]{1,0:T(8,128)S(1)} fusion(bf16[128,3584]{1,0:T(8,128)(2,1)} %constant_dynamic-update-slice_fusion.16, bf16[1,7168,512]{2,1,0:T(8,128)(2,1)} %param.12), kind=kOutput, calls=%fused_computation.14 | convolution fusion | flops 469762048 | bytes 4849664 | tf_op jit(solution)/shard_map/dot_general | solution.py:152
  42.2 1.0 %slice-done.5 = s8[3145728]{0:T(1024)(128)(4,1)S(1)} async-done(((s8[7340032]{0:T(1024)(128)(4,1)}), s8[3145728]{0:T(1024)(128)(4,1)S(1)}, s32[]{:S(2)}) %slice-start.5) | async-done | bytes 3145752
  46.9 2.6 %collective-permute-start.25 = (bf16[24,3584]{1,0:T(8,128)(2,1)S(1)}, bf16[24,3584]{1,0:T(8,128)(2,1)S(1)}, u32[]{:S(2)}, u32[]{:S(2)}) collective-permute-start(bf16[24,3584]{1,0:T(8,128)(2,1)S(1)} %slice.294), channel_id=1, source_target_pairs={{0,8},{4,12},{8,0},{12,4},{1,9},{5,13},{9,1},{13,5},{2,10},{6,14},... | collective-permute-start | bytes 516104 | tf_op jit(solution)/shard_map/ppermute | solution.py:26
  55.1 3.0 %collective-permute-done.10 = bf16[24,3584]{1,0:T(8,128)(2,1)S(1)} collective-permute-done((bf16[24,3584]{1,0:T(8,128)(2,1)S(1)}, bf16[24,3584]{1,0:T(8,128)(2,1)S(1)}, u32[]{:S(2)}, u32[]{:S(2)}) %collective-permute-start.10) | collective-permute-done | bytes 172064 | tf_op jit(solution)/shard_map/ppermute | solution.py:26
  58.2 1.8 %collective-permute-done.26 = bf16[16,3584]{1,0:T(8,128)(2,1)S(1)} collective-permute-done((bf16[16,3584]{1,0:T(8,128)(2,1)S(1)}, bf16[16,3584]{1,0:T(8,128)(2,1)S(1)}, u32[]{:S(2)}, u32[]{:S(2)}) %collective-permute-start.26) | collective-permute-done | bytes 114720 | tf_op jit(solution)/shard_map/ppermute | solution.py:26
  59.9 2.5 %collective-permute-start.27 = (bf16[8,3584]{1,0:T(8,128)(2,1)S(1)}, bf16[8,3584]{1,0:T(8,128)(2,1)S(1)}, u32[]{:S(2)}, u32[]{:S(2)}) collective-permute-start(bf16[8,3584]{1,0:T(8,128)(2,1)S(1)} %add_convert_fusion.13), channel_id=1, source_target_pairs={{0,2},{1,3},{2,0},{3,1},{4,6},{5,7},{6,4},{7,5},{8,10},{9,11},{10,... | collective-permute-start | bytes 172040 | tf_op jit(solution)/shard_map/ppermute | solution.py:26
  62.8 1.9 %collective-permute-start.31 = (bf16[24,3584]{1,0:T(8,128)(2,1)S(1)}, bf16[24,3584]{1,0:T(8,128)(2,1)S(1)}, u32[]{:S(2)}, u32[]{:S(2)}) collective-permute-start(bf16[24,3584]{1,0:T(8,128)(2,1)S(1)} %slice.310), channel_id=1, source_target_pairs={{0,8},{4,12},{8,0},{12,4},{1,9},{5,13},{9,1},{13,5},{2,10},{6,14},... | collective-permute-start | bytes 516104 | tf_op jit(solution)/shard_map/ppermute | solution.py:26
  64.7 1.7 %collective-permute-start.22 = (bf16[16,3584]{1,0:T(8,128)(2,1)S(1)}, bf16[16,3584]{1,0:T(8,128)(2,1)S(1)}, u32[]{:S(2)}, u32[]{:S(2)}) collective-permute-start(bf16[16,3584]{1,0:T(8,128)(2,1)S(1)} %slice.273), channel_id=1, source_target_pairs={{0,1},{1,0},{2,3},{3,2},{4,5},{5,4},{6,7},{7,6},{8,9},{9,8},{10,11... | collective-permute-start | bytes 344072 | tf_op jit(solution)/shard_map/ppermute | solution.py:26
  66.6 1.9 %collective-permute-start.24 = (bf16[16,7168]{1,0:T(8,128)(2,1)S(1)}, bf16[16,7168]{1,0:T(8,128)(2,1)S(1)}, u32[]{:S(2)}, u32[]{:S(2)}) collective-permute-start(bf16[16,7168]{1,0:T(8,128)(2,1)S(1)} %maximum_maximum_fusion), channel_id=1, source_target_pairs={{0,8},{4,12},{8,0},{12,4},{1,9},{5,13},{9,1},{13,5},{2,10},{6,14},... | collective-permute-start | bytes 688136 | tf_op jit(solution)/shard_map/ppermute | solution.py:26
  68.6 0.9 %collective-permute-done.22 = bf16[16,3584]{1,0:T(8,128)(2,1)S(1)} collective-permute-done((bf16[16,3584]{1,0:T(8,128)(2,1)S(1)}, bf16[16,3584]{1,0:T(8,128)(2,1)S(1)}, u32[]{:S(2)}, u32[]{:S(2)}) %collective-permute-start.22) | collective-permute-done | bytes 114720 | tf_op jit(solution)/shard_map/ppermute | solution.py:26
  70.1 2.0 %collective-permute-start.32 = (bf16[16,3584]{1,0:T(8,128)(2,1)S(1)}, bf16[16,3584]{1,0:T(8,128)(2,1)S(1)}, u32[]{:S(2)}, u32[]{:S(2)}) collective-permute-start(bf16[16,3584]{1,0:T(8,128)(2,1)S(1)} %slice.311), channel_id=1, source_target_pairs={{0,1},{1,0},{2,3},{3,2},{4,5},{5,4},{6,7},{7,6},{8,9},{9,8},{10,11... | collective-permute-start | bytes 344072 | tf_op jit(solution)/shard_map/ppermute | solution.py:26
  72.1 1.7 %collective-permute-done.28 = bf16[24,3584]{1,0:T(8,128)(2,1)S(1)} collective-permute-done((bf16[24,3584]{1,0:T(8,128)(2,1)S(1)}, bf16[24,3584]{1,0:T(8,128)(2,1)S(1)}, u32[]{:S(2)}, u32[]{:S(2)}) %collective-permute-start.28) | collective-permute-done | bytes 172064 | tf_op jit(solution)/shard_map/ppermute | solution.py:26
  73.8 1.9 %collective-permute-start.29 = (bf16[16,3584]{1,0:T(8,128)(2,1)S(1)}, bf16[16,3584]{1,0:T(8,128)(2,1)S(1)}, u32[]{:S(2)}, u32[]{:S(2)}) collective-permute-start(bf16[16,3584]{1,0:T(8,128)(2,1)S(1)} %slice.303), channel_id=1, source_target_pairs={{0,1},{1,0},{2,3},{3,2},{4,5},{5,4},{6,7},{7,6},{8,9},{9,8},{10,11... | collective-permute-start | bytes 344072 | tf_op jit(solution)/shard_map/ppermute | solution.py:26
  76.3 2.6 %collective-permute-start.33 = (bf16[8,3584]{1,0:T(8,128)(2,1)S(1)}, bf16[8,3584]{1,0:T(8,128)(2,1)S(1)}, u32[]{:S(2)}, u32[]{:S(2)}) collective-permute-start(bf16[8,3584]{1,0:T(8,128)(2,1)S(1)} %add_convert_fusion.9), channel_id=1, source_target_pairs={{0,2},{1,3},{2,0},{3,1},{4,6},{5,7},{6,4},{7,5},{8,10},{9,11},{10,... | collective-permute-start | bytes 172040 | tf_op jit(solution)/shard_map/ppermute | solution.py:26
  78.9 1.9 %collective-permute-start.30 = (bf16[8,3584]{1,0:T(8,128)(2,1)S(1)}, bf16[8,3584]{1,0:T(8,128)(2,1)S(1)}, u32[]{:S(2)}, u32[]{:S(2)}) collective-permute-start(bf16[8,3584]{1,0:T(8,128)(2,1)S(1)} %add_convert_fusion.11), channel_id=1, source_target_pairs={{0,2},{1,3},{2,0},{3,1},{4,6},{5,7},{6,4},{7,5},{8,10},{9,11},{10,... | collective-permute-start | bytes 172040 | tf_op jit(solution)/shard_map/ppermute | solution.py:26
  80.8 1.2 %collective-permute-done.33 = bf16[8,3584]{1,0:T(8,128)(2,1)S(1)} collective-permute-done((bf16[8,3584]{1,0:T(8,128)(2,1)S(1)}, bf16[8,3584]{1,0:T(8,128)(2,1)S(1)}, u32[]{:S(2)}, u32[]{:S(2)}) %collective-permute-start.33) | collective-permute-done | bytes 57376 | tf_op jit(solution)/shard_map/ppermute | solution.py:26
  82.0 2.0 %collective-permute-done.30 = bf16[8,3584]{1,0:T(8,128)(2,1)S(1)} collective-permute-done((bf16[8,3584]{1,0:T(8,128)(2,1)S(1)}, bf16[8,3584]{1,0:T(8,128)(2,1)S(1)}, u32[]{:S(2)}, u32[]{:S(2)}) %collective-permute-start.30) | collective-permute-done | bytes 57376 | tf_op jit(solution)/shard_map/ppermute | solution.py:26
  (148 shorter events, 22.8 us)
Async XLA Ops:
  3.4 6.9 %collective-permute-start.5 = (bf16[8,3584]{1,0:T(8,128)(2,1)S(1)}, bf16[8,3584]{1,0:T(8,128)(2,1)S(1)}, u32[]{:S(2)}, u32[]{:S(2)}) collective-permute-start(bf16[8,3584]{1,0:T(8,128)(2,1)S(1)} %get-tuple-element.21), channel_id=1, source_target_pairs={{0,2},{1,3},{2,0},{3,1},{4,6},{5,7},{6,4},{7,5},{8,10},{9,11},{10,... | collective-permute-start | bytes 172040 | tf_op jit(solution)/shard_map/ppermute | solution.py:26
  7.5 9.3 %collective-permute-start = (bf16[8,3712]{1,0:T(8,128)(2,1)S(1)}, bf16[8,3712]{1,0:T(8,128)(2,1)S(1)}, u32[]{:S(2)}, u32[]{:S(2)}) collective-permute-start(bf16[8,3712]{1,0:T(8,128)(2,1)S(1)} %get-tuple-element.19), channel_id=1, source_target_pairs={{0,2},{1,3},{2,0},{3,1},{4,6},{5,7},{6,4},{7,5},{8,10},{9,11},{10,... | collective-permute-start | bytes 178184 | tf_op jit(solution)/shard_map/ppermute | solution.py:26
  7.6 18.4 %collective-permute-start.2 = (bf16[16,7296]{1,0:T(8,128)(2,1)S(1)}, bf16[16,7296]{1,0:T(8,128)(2,1)S(1)}, u32[]{:S(2)}, u32[]{:S(2)}) collective-permute-start(bf16[16,7296]{1,0:T(8,128)(2,1)S(1)} %get-tuple-element.20), channel_id=1, source_target_pairs={{0,8},{4,12},{8,0},{12,4},{1,9},{5,13},{9,1},{13,5},{2,10},{6,14},... | collective-permute-start | bytes 700424 | tf_op jit(solution)/shard_map/ppermute | solution.py:26
  10.3 6.7 %collective-permute-start.16 = (bf16[8,3584]{1,0:T(8,128)(2,1)S(1)}, bf16[8,3584]{1,0:T(8,128)(2,1)S(1)}, u32[]{:S(2)}, u32[]{:S(2)}) collective-permute-start(bf16[8,3584]{1,0:T(8,128)(2,1)S(1)} %get-tuple-element.28), channel_id=1, source_target_pairs={{0,2},{1,3},{2,0},{3,1},{4,6},{5,7},{6,4},{7,5},{8,10},{9,11},{10,... | collective-permute-start | bytes 172040 | tf_op jit(solution)/shard_map/ppermute | solution.py:26
  12.8 6.3 %collective-permute-start.11 = (bf16[8,3712]{1,0:T(8,128)(2,1)S(1)}, bf16[8,3712]{1,0:T(8,128)(2,1)S(1)}, u32[]{:S(2)}, u32[]{:S(2)}) collective-permute-start(bf16[8,3712]{1,0:T(8,128)(2,1)S(1)} %get-tuple-element.23), channel_id=1, source_target_pairs={{0,2},{1,3},{2,0},{3,1},{4,6},{5,7},{6,4},{7,5},{8,10},{9,11},{10,... | collective-permute-start | bytes 178184 | tf_op jit(solution)/shard_map/ppermute | solution.py:26
  13.9 8.0 %collective-permute-start.6 = (bf16[16,3584]{1,0:T(8,128)(2,1)S(1)}, bf16[16,3584]{1,0:T(8,128)(2,1)S(1)}, u32[]{:S(2)}, u32[]{:S(2)}) collective-permute-start(bf16[16,3584]{1,0:T(8,128)(2,1)S(1)} %pad_maximum_fusion.9), channel_id=1, source_target_pairs={{0,1},{1,0},{2,3},{3,2},{4,5},{5,4},{6,7},{7,6},{8,9},{9,8},{10,11... | collective-permute-start | bytes 344072 | tf_op jit(solution)/shard_map/ppermute | solution.py:26
  16.9 7.3 %collective-permute-start.1 = (bf16[16,3712]{1,0:T(8,128)(2,1)S(1)}, bf16[16,3712]{1,0:T(8,128)(2,1)S(1)}, u32[]{:S(2)}, u32[]{:S(2)}) collective-permute-start(bf16[16,3712]{1,0:T(8,128)(2,1)S(1)} %pad_maximum_fusion.7), channel_id=1, source_target_pairs={{0,1},{1,0},{2,3},{3,2},{4,5},{5,4},{6,7},{7,6},{8,9},{9,8},{10,11... | collective-permute-start | bytes 356360 | tf_op jit(solution)/shard_map/ppermute | solution.py:26
  17.0 8.9 %collective-permute-start.17 = (bf16[16,3584]{1,0:T(8,128)(2,1)S(1)}, bf16[16,3584]{1,0:T(8,128)(2,1)S(1)}, u32[]{:S(2)}, u32[]{:S(2)}) collective-permute-start(bf16[16,3584]{1,0:T(8,128)(2,1)S(1)} %pad_maximum_fusion.10), channel_id=1, source_target_pairs={{0,1},{1,0},{2,3},{3,2},{4,5},{5,4},{6,7},{7,6},{8,9},{9,8},{10,11... | collective-permute-start | bytes 344072 | tf_op jit(solution)/shard_map/ppermute | solution.py:26
  19.1 8.9 %collective-permute-start.12 = (bf16[16,3712]{1,0:T(8,128)(2,1)S(1)}, bf16[16,3712]{1,0:T(8,128)(2,1)S(1)}, u32[]{:S(2)}, u32[]{:S(2)}) collective-permute-start(bf16[16,3712]{1,0:T(8,128)(2,1)S(1)} %pad_maximum_fusion.8), channel_id=1, source_target_pairs={{0,1},{1,0},{2,3},{3,2},{4,5},{5,4},{6,7},{7,6},{8,9},{9,8},{10,11... | collective-permute-start | bytes 356360 | tf_op jit(solution)/shard_map/ppermute | solution.py:26
  21.9 7.1 %collective-permute-start.7 = (bf16[24,3584]{1,0:T(8,128)(2,1)S(1)}, bf16[24,3584]{1,0:T(8,128)(2,1)S(1)}, u32[]{:S(2)}, u32[]{:S(2)}) collective-permute-start(bf16[24,3584]{1,0:T(8,128)(2,1)S(1)} %pad_maximum_fusion.5), channel_id=1, source_target_pairs={{0,8},{4,12},{8,0},{12,4},{1,9},{5,13},{9,1},{13,5},{2,10},{6,14},... | collective-permute-start | bytes 516104 | tf_op jit(solution)/shard_map/ppermute | solution.py:26
  24.2 7.3 %collective-permute-start.3 = (bf16[24,3712]{1,0:T(8,128)(2,1)S(1)}, bf16[24,3712]{1,0:T(8,128)(2,1)S(1)}, u32[]{:S(2)}, u32[]{:S(2)}) collective-permute-start(bf16[24,3712]{1,0:T(8,128)(2,1)S(1)} %pad_maximum_fusion.3), channel_id=1, source_target_pairs={{0,8},{4,12},{8,0},{12,4},{1,9},{5,13},{9,1},{13,5},{2,10},{6,14},... | collective-permute-start | bytes 534536 | tf_op jit(solution)/shard_map/ppermute | solution.py:26
  29.1 5.9 %collective-permute-start.18 = (bf16[24,3584]{1,0:T(8,128)(2,1)S(1)}, bf16[24,3584]{1,0:T(8,128)(2,1)S(1)}, u32[]{:S(2)}, u32[]{:S(2)}) collective-permute-start(bf16[24,3584]{1,0:T(8,128)(2,1)S(1)} %pad_maximum_fusion.6), channel_id=1, source_target_pairs={{0,8},{4,12},{8,0},{12,4},{1,9},{5,13},{9,1},{13,5},{2,10},{6,14},... | collective-permute-start | bytes 516104 | tf_op jit(solution)/shard_map/ppermute | solution.py:26
  31.3 3.7 %collective-permute-start.8 = (bf16[64,3584]{1,0:T(8,128)(2,1)S(1)}, bf16[64,3584]{1,0:T(8,128)(2,1)S(1)}, u32[]{:S(2)}, u32[]{:S(2)}) collective-permute-start(bf16[64,3584]{1,0:T(8,128)(2,1)S(1)} %get-tuple-element.49), channel_id=1, source_target_pairs={{0,4},{4,0},{8,12},{12,8},{1,5},{5,1},{9,13},{13,9},{2,6},{6,2},{1... | collective-permute-start | bytes 1376264 | tf_op jit(solution)/shard_map/ppermute | solution.py:26
  31.5 12.5 %collective-permute-start.13 = (bf16[24,3712]{1,0:T(8,128)(2,1)S(1)}, bf16[24,3712]{1,0:T(8,128)(2,1)S(1)}, u32[]{:S(2)}, u32[]{:S(2)}) collective-permute-start(bf16[24,3712]{1,0:T(8,128)(2,1)S(1)} %pad_maximum_fusion.4), channel_id=1, source_target_pairs={{0,8},{4,12},{8,0},{12,4},{1,9},{5,13},{9,1},{13,5},{2,10},{6,14},... | collective-permute-start | bytes 534536 | tf_op jit(solution)/shard_map/ppermute | solution.py:26
  33.0 6.6 %collective-permute-start.4 = (bf16[64,3712]{1,0:T(8,128)(2,1)S(1)}, bf16[64,3712]{1,0:T(8,128)(2,1)S(1)}, u32[]{:S(2)}, u32[]{:S(2)}) collective-permute-start(bf16[64,3712]{1,0:T(8,128)(2,1)S(1)} %get-tuple-element.47), channel_id=1, source_target_pairs={{0,4},{4,0},{8,12},{12,8},{1,5},{5,1},{9,13},{13,9},{2,6},{6,2},{1... | collective-permute-start | bytes 1425416 | tf_op jit(solution)/shard_map/ppermute | solution.py:26
  45.3 4.2 %collective-permute-start.19 = (bf16[64,3584]{1,0:T(8,128)(2,1)S(1)}, bf16[64,3584]{1,0:T(8,128)(2,1)S(1)}, u32[]{:S(2)}, u32[]{:S(2)}) collective-permute-start(bf16[64,3584]{1,0:T(8,128)(2,1)S(1)} %constant_dynamic-update-slice_fusion.27), channel_id=1, source_target_pairs={{0,4},{4,0},{8,12},{12,8},{1,5},{5,1},{9,13},{13,9},{2,6},{6,2},{1... | collective-permute-start | bytes 1376264 | tf_op jit(solution)/shard_map/ppermute | solution.py:26
  45.4 5.5 %collective-permute-start.14 = (bf16[64,3712]{1,0:T(8,128)(2,1)S(1)}, bf16[64,3712]{1,0:T(8,128)(2,1)S(1)}, u32[]{:S(2)}, u32[]{:S(2)}) collective-permute-start(bf16[64,3712]{1,0:T(8,128)(2,1)S(1)} %constant_dynamic-update-slice_fusion.22), channel_id=1, source_target_pairs={{0,4},{4,0},{8,12},{12,8},{1,5},{5,1},{9,13},{13,9},{2,6},{6,2},{1... | collective-permute-start | bytes 1425416 | tf_op jit(solution)/shard_map/ppermute | solution.py:26
  46.9 7.8 %collective-permute-start.25 = (bf16[24,3584]{1,0:T(8,128)(2,1)S(1)}, bf16[24,3584]{1,0:T(8,128)(2,1)S(1)}, u32[]{:S(2)}, u32[]{:S(2)}) collective-permute-start(bf16[24,3584]{1,0:T(8,128)(2,1)S(1)} %slice.294), channel_id=1, source_target_pairs={{0,8},{4,12},{8,0},{12,4},{1,9},{5,13},{9,1},{13,5},{2,10},{6,14},... | collective-permute-start | bytes 516104 | tf_op jit(solution)/shard_map/ppermute | solution.py:26
  49.5 8.6 %collective-permute-start.10 = (bf16[24,3584]{1,0:T(8,128)(2,1)S(1)}, bf16[24,3584]{1,0:T(8,128)(2,1)S(1)}, u32[]{:S(2)}, u32[]{:S(2)}) collective-permute-start(bf16[24,3584]{1,0:T(8,128)(2,1)S(1)} %slice.272), channel_id=1, source_target_pairs={{0,8},{4,12},{8,0},{12,4},{1,9},{5,13},{9,1},{13,5},{2,10},{6,14},... | collective-permute-start | bytes 516104 | tf_op jit(solution)/shard_map/ppermute | solution.py:26
  53.9 8.5 %collective-permute-start.21 = (bf16[64,3584]{1,0:T(8,128)(2,1)S(1)}, bf16[64,3584]{1,0:T(8,128)(2,1)S(1)}, u32[]{:S(2)}, u32[]{:S(2)}) collective-permute-start(bf16[64,3584]{1,0:T(8,128)(2,1)S(1)} %slice.283), channel_id=1, source_target_pairs={{0,4},{4,0},{8,12},{12,8},{1,5},{5,1},{9,13},{13,9},{2,6},{6,2},{1... | collective-permute-start | bytes 1376264 | tf_op jit(solution)/shard_map/ppermute | solution.py:26
  54.1 8.5 %collective-permute-start.20 = (bf16[64,3584]{1,0:T(8,128)(2,1)S(1)}, bf16[64,3584]{1,0:T(8,128)(2,1)S(1)}, u32[]{:S(2)}, u32[]{:S(2)}) collective-permute-start(bf16[64,3584]{1,0:T(8,128)(2,1)S(1)} %slice.281), channel_id=1, source_target_pairs={{0,4},{4,0},{8,12},{12,8},{1,5},{5,1},{9,13},{13,9},{2,6},{6,2},{1... | collective-permute-start | bytes 1376264 | tf_op jit(solution)/shard_map/ppermute | solution.py:26
  54.8 5.1 %collective-permute-start.26 = (bf16[16,3584]{1,0:T(8,128)(2,1)S(1)}, bf16[16,3584]{1,0:T(8,128)(2,1)S(1)}, u32[]{:S(2)}, u32[]{:S(2)}) collective-permute-start(bf16[16,3584]{1,0:T(8,128)(2,1)S(1)} %slice.295), channel_id=1, source_target_pairs={{0,1},{1,0},{2,3},{3,2},{4,5},{5,4},{6,7},{7,6},{8,9},{9,8},{10,11... | collective-permute-start | bytes 344072 | tf_op jit(solution)/shard_map/ppermute | solution.py:26
  59.9 20.9 %collective-permute-start.27 = (bf16[8,3584]{1,0:T(8,128)(2,1)S(1)}, bf16[8,3584]{1,0:T(8,128)(2,1)S(1)}, u32[]{:S(2)}, u32[]{:S(2)}) collective-permute-start(bf16[8,3584]{1,0:T(8,128)(2,1)S(1)} %add_convert_fusion.13), channel_id=1, source_target_pairs={{0,2},{1,3},{2,0},{3,1},{4,6},{5,7},{6,4},{7,5},{8,10},{9,11},{10,... | collective-permute-start | bytes 172040 | tf_op jit(solution)/shard_map/ppermute | solution.py:26
  62.8 7.3 %collective-permute-start.31 = (bf16[24,3584]{1,0:T(8,128)(2,1)S(1)}, bf16[24,3584]{1,0:T(8,128)(2,1)S(1)}, u32[]{:S(2)}, u32[]{:S(2)}) collective-permute-start(bf16[24,3584]{1,0:T(8,128)(2,1)S(1)} %slice.310), channel_id=1, source_target_pairs={{0,8},{4,12},{8,0},{12,4},{1,9},{5,13},{9,1},{13,5},{2,10},{6,14},... | collective-permute-start | bytes 516104 | tf_op jit(solution)/shard_map/ppermute | solution.py:26
  64.7 4.8 %collective-permute-start.22 = (bf16[16,3584]{1,0:T(8,128)(2,1)S(1)}, bf16[16,3584]{1,0:T(8,128)(2,1)S(1)}, u32[]{:S(2)}, u32[]{:S(2)}) collective-permute-start(bf16[16,3584]{1,0:T(8,128)(2,1)S(1)} %slice.273), channel_id=1, source_target_pairs={{0,1},{1,0},{2,3},{3,2},{4,5},{5,4},{6,7},{7,6},{8,9},{9,8},{10,11... | collective-permute-start | bytes 344072 | tf_op jit(solution)/shard_map/ppermute | solution.py:26
  66.5 7.3 %collective-permute-start.28 = (bf16[24,3584]{1,0:T(8,128)(2,1)S(1)}, bf16[24,3584]{1,0:T(8,128)(2,1)S(1)}, u32[]{:S(2)}, u32[]{:S(2)}) collective-permute-start(bf16[24,3584]{1,0:T(8,128)(2,1)S(1)} %slice.302), channel_id=1, source_target_pairs={{0,8},{4,12},{8,0},{12,4},{1,9},{5,13},{9,1},{13,5},{2,10},{6,14},... | collective-permute-start | bytes 516104 | tf_op jit(solution)/shard_map/ppermute | solution.py:26
  66.6 14.2 %collective-permute-start.24 = (bf16[16,7168]{1,0:T(8,128)(2,1)S(1)}, bf16[16,7168]{1,0:T(8,128)(2,1)S(1)}, u32[]{:S(2)}, u32[]{:S(2)}) collective-permute-start(bf16[16,7168]{1,0:T(8,128)(2,1)S(1)} %maximum_maximum_fusion), channel_id=1, source_target_pairs={{0,8},{4,12},{8,0},{12,4},{1,9},{5,13},{9,1},{13,5},{2,10},{6,14},... | collective-permute-start | bytes 688136 | tf_op jit(solution)/shard_map/ppermute | solution.py:26
  69.5 11.3 %collective-permute-start.23 = (bf16[8,3584]{1,0:T(8,128)(2,1)S(1)}, bf16[8,3584]{1,0:T(8,128)(2,1)S(1)}, u32[]{:S(2)}, u32[]{:S(2)}) collective-permute-start(bf16[8,3584]{1,0:T(8,128)(2,1)S(1)} %add_convert_fusion.15), channel_id=1, source_target_pairs={{0,2},{1,3},{2,0},{3,1},{4,6},{5,7},{6,4},{7,5},{8,10},{9,11},{10,... | collective-permute-start | bytes 172040 | tf_op jit(solution)/shard_map/ppermute | solution.py:26
  70.1 6.1 %collective-permute-start.32 = (bf16[16,3584]{1,0:T(8,128)(2,1)S(1)}, bf16[16,3584]{1,0:T(8,128)(2,1)S(1)}, u32[]{:S(2)}, u32[]{:S(2)}) collective-permute-start(bf16[16,3584]{1,0:T(8,128)(2,1)S(1)} %slice.311), channel_id=1, source_target_pairs={{0,1},{1,0},{2,3},{3,2},{4,5},{5,4},{6,7},{7,6},{8,9},{9,8},{10,11... | collective-permute-start | bytes 344072 | tf_op jit(solution)/shard_map/ppermute | solution.py:26
  73.8 5.0 %collective-permute-start.29 = (bf16[16,3584]{1,0:T(8,128)(2,1)S(1)}, bf16[16,3584]{1,0:T(8,128)(2,1)S(1)}, u32[]{:S(2)}, u32[]{:S(2)}) collective-permute-start(bf16[16,3584]{1,0:T(8,128)(2,1)S(1)} %slice.303), channel_id=1, source_target_pairs={{0,1},{1,0},{2,3},{3,2},{4,5},{5,4},{6,7},{7,6},{8,9},{9,8},{10,11... | collective-permute-start | bytes 344072 | tf_op jit(solution)/shard_map/ppermute | solution.py:26
  76.3 5.8 %collective-permute-start.33 = (bf16[8,3584]{1,0:T(8,128)(2,1)S(1)}, bf16[8,3584]{1,0:T(8,128)(2,1)S(1)}, u32[]{:S(2)}, u32[]{:S(2)}) collective-permute-start(bf16[8,3584]{1,0:T(8,128)(2,1)S(1)} %add_convert_fusion.9), channel_id=1, source_target_pairs={{0,2},{1,3},{2,0},{3,1},{4,6},{5,7},{6,4},{7,5},{8,10},{9,11},{10,... | collective-permute-start | bytes 172040 | tf_op jit(solution)/shard_map/ppermute | solution.py:26
  78.9 5.1 %collective-permute-start.30 = (bf16[8,3584]{1,0:T(8,128)(2,1)S(1)}, bf16[8,3584]{1,0:T(8,128)(2,1)S(1)}, u32[]{:S(2)}, u32[]{:S(2)}) collective-permute-start(bf16[8,3584]{1,0:T(8,128)(2,1)S(1)} %add_convert_fusion.11), channel_id=1, source_target_pairs={{0,2},{1,3},{2,0},{3,1},{4,6},{5,7},{6,4},{7,5},{8,10},{9,11},{10,... | collective-permute-start | bytes 172040 | tf_op jit(solution)/shard_map/ppermute | solution.py:26
  (16 other events, 126.3 us)

commit v4 on v2

v4 whole, which is shorter than its diff:
```python
import functools

import jax
import jax.numpy as jnp
from jax import lax
from jax.experimental import pallas as pl
from jax.experimental.pallas import tpu as pltpu
from jax.sharding import PartitionSpec as P

routed_scale = 2.5
column_parts = 2
F_Z2 = 2
F_XORD = 1
F_C1 = 1
F_Z2R = 2
F_CHOLD = 1
F_OUT1 = 2
F_FIN0 = 1
F_OWN0 = 0
F_LATE = 1
F_SPLIT1 = 1
F_BACK0 = 2


def bits_of(count):
    return [1 << b for b in reversed(range(count.bit_length() - 1))]


def swap(value, axis_name, bit):
    count = lax.axis_size(axis_name)
    return lax.ppermute(value, axis_name, [(i, i ^ bit) for i in range(count)])


def after(value, *others):
    return lax.optimization_barrier((value, *others))[0] if others else value


def join(*parts):
    return jnp.concatenate(parts, axis=0)


def add_up(*terms):
    total = terms[0].astype(jnp.float32)
    for term in terms[1:]:
        total = total + term.astype(jnp.float32)
    return total


def prepare_kernel(ep_count, extra, cuts, codes_hbm, scales_hbm, ids_hbm, gates_hbm, all_ref, *refs):
    part_refs, (codes_ref, scales_ref, ids_ref, gates_ref, sems) = refs[:-5], refs[-5:]
    moves = []
    for n, (source, target) in enumerate(
        [(codes_hbm, codes_ref), (scales_hbm, scales_ref), (ids_hbm, ids_ref), (gates_hbm, gates_ref)]
    ):
        moves.append(pltpu.make_async_copy(source, target, sems.at[n]))
        moves[-1].start()
    for move in moves:
        move.wait()
    steps_here, rows, features = codes_ref.shape
    blocks = scales_ref.shape[2]
    size = features // blocks
    lane = lax.broadcasted_iota(jnp.int32, (rows, extra), 1)
    expert = lax.rem(lane, ep_count)
    diagonal = lax.broadcasted_iota(jnp.int32, (rows, rows), 0) == lax.broadcasted_iota(jnp.int32, (rows, rows), 1)

    def column(values):
        spread = jnp.broadcast_to(values.astype(jnp.float32), (rows, rows))
        total = jnp.sum(jnp.where(diagonal, spread, 0.0), axis=1, keepdims=True)
        return jnp.broadcast_to(total.astype(jnp.int32), (rows, extra))

    every = []
    target = 0
    for step in range(steps_here):
        ids, gates = ids_ref[step], gates_ref[step]
        code = jnp.zeros((rows, extra), jnp.int32)
        for route in range(ids.shape[0]):
            code += jnp.where(column(ids[route : route + 1]) == expert, column(gates[route : route + 1]), 0)
        low = code & 15
        sent = jnp.where(lane < ep_count, code - low, jnp.where(lane < 2 * ep_count, low, 0))
        pieces = [sent.astype(jnp.float32)]
        scales = scales_ref[step]
        codes = codes_ref[step].astype(jnp.float32)
        for b in range(blocks):
            pieces.append(codes[:, b * size : (b + 1) * size] * jnp.broadcast_to(scales[:, b : b + 1], (rows, size)))
        row = jnp.concatenate(pieces, axis=1)
        every.append(row)
        for start, end in spans_of(features, cuts[step], extra):
            part_refs[target][...] = row[:, start:end].astype(jnp.bfloat16)
            target += 1
    all_ref[...] = jnp.concatenate(every, axis=0).astype(jnp.bfloat16)


def spans_of(features, count, extra):
    width = features // count
    return [(extra + k * width if k else 0, extra + (k + 1) * width) for k in range(count)]


def prepare(row_codes, row_scales, expert_ids, gate_codes, ep_count, cuts):
    steps_here, rows, features = row_codes.shape
    extra = -(-2 * ep_count // 128) * 128
    shapes = [jax.ShapeDtypeStruct((steps_here * rows, features + extra), jnp.bfloat16)]
    for step in range(steps_here):
        for start, end in spans_of(features, cuts[step], extra):
            shapes.append(jax.ShapeDtypeStruct((rows, end - start), jnp.bfloat16))
    ins = [row_codes, row_scales, expert_ids.transpose(0, 2, 1), gate_codes.transpose(0, 2, 1)]
    outs = pl.pallas_call(
        functools.partial(prepare_kernel, ep_count, extra, cuts),
        out_shape=shapes,
        in_specs=[pl.BlockSpec(memory_space=pl.ANY)] * len(ins),
        scratch_shapes=[pltpu.VMEM(v.shape, v.dtype) for v in ins] + [pltpu.SemaphoreType.DMA((len(ins),))],
    )(*ins)
    return outs[0], outs[1:], extra


def body(row_codes, row_scales, expert_ids, gate_codes, w_gate, w_up, w_down):
    ep_count = lax.axis_size("ep")
    sub_bits = bits_of(lax.axis_size("sub"))
    ep_bits = bits_of(ep_count)
    steps_here, rows, features = row_codes.shape
    out_cuts = [column_parts] + [F_OUT1] * (steps_here - 1)
    back_cuts = [F_BACK0] + [column_parts] * (steps_here - 1)
    tokens, owns, extra = prepare(row_codes, row_scales, expert_ids, gate_codes, ep_count, out_cuts)
    crossed = swap(tokens, "ep", ep_bits[0])
    me = lax.axis_index("ep")
    far, near, xs = [], [], []
    gathered = []
    for step in range(steps_here):
        parts = []
        for k, (start, end) in enumerate(spans_of(features, out_cuts[step], extra)):
            part = owns[len(xs)]
            for n, bit in enumerate(sub_bits):
                if n == 0 and step >= 1 and F_Z2 == 1:
                    part = after(part, near[0])
                if n == 0 and step >= 1 and F_Z2 == 2:
                    part = after(part, far[1])
                if n == 0 and step >= 1 and F_Z2 == 3:
                    part = after(part, far[0])
                came = swap(part, "sub", bit)
                if n == 0:
                    far.append(came)
                if n == 1:
                    near.append(came)
                part = join(part, came)
            give = part[rows:]
            if F_XORD and step >= 1:
                give = after(give, xs[F_XORD - 1])
            xs.append(swap(give, "ep", ep_bits[0]))
            parts.append((part, crossed[step * rows : (step + 1) * rows, start:end], xs[-1]))
        gathered.append(parts)
    step_done, core_back = [], []
    returned = []
    for step in range(steps_here):
        gate_value = up_value = 0.0
        for part, (start, end) in zip(gathered[step], spans_of(features, out_cuts[step], extra)):
            part, came_own, came_rest = part
            if F_LATE and step_done:
                came_rest = after(came_rest, *step_done)
            part = join(part, came_own, came_rest)
            for bit in ep_bits[1:]:
                part = after(part, *step_done) if F_C1 else part
                part = join(part, swap(part, "ep", bit))
            part = after(part, *core_back) if F_CHOLD else part
            if start == 0:
                sent = part[:, : 2 * ep_count].astype(jnp.float32)
                dense = sent[:, :ep_count] + sent[:, ep_count:]
                total = jnp.sum(dense, axis=1, keepdims=True)
                mine = jnp.sum(jnp.where(jnp.arange(ep_count) == me, dense, 0.0), axis=1, keepdims=True)
                weight = routed_scale * mine / total
                part = part[:, extra:]
            span = slice(max(start - extra, 0), end - extra)
            gate_value += jnp.dot(part, w_gate[0, span], preferred_element_type=jnp.float32)
            up_value += jnp.dot(part, w_up[0, span], preferred_element_type=jnp.float32)
        hidden = (jax.nn.silu(gate_value) * up_value).astype(jnp.bfloat16)
        step_done = []
        core_back = []
        for start, end in spans_of(features, back_cuts[step], 0):
            held = jnp.dot(hidden, w_down[0, :, start:end], preferred_element_type=jnp.float32)
            held = (held * weight).astype(jnp.bfloat16)
            step_done.append(held)
            for bit in reversed(ep_bits[1:]):
                half = held.shape[0] // 2
                held = add_up(held[:half], swap(held[half:], "ep", bit)).astype(jnp.bfloat16)
            core_back.append(held)
            returned.append((step, start, end, held))
    last = [held for step, _, _, held in returned if step == steps_here - 1]
    finals, own_gives, owns, restss, crossings = [], [], [], [], []
    for step in range(steps_here):
        split = rows if step >= F_OWN0 else 0
        own, rests, gives = [], [], []
        for _, start, end, held in [entry for entry in returned if entry[0] == step]:
            half = held.shape[0] // 2
            came = swap(held[half + split :], "ep", ep_bits[0])
            mine = [held[:rows]]
            if split:
                gives.append(held[half : half + rows])
            else:
                mine.append(came[:rows])
                came = came[rows:]
            crossings.append(came)
            rest = add_up(held[rows:half], came).astype(jnp.bfloat16)
            for n, bit in enumerate(reversed(sub_bits[1:])):
                half = (rest.shape[0] + rows) // 2
                give = rest[half - rows :]
                if step == 0 and n == 0 and F_Z2R == 2:
                    give = after(give, *last)
                came = swap(give, "sub", bit)
                mine.append(came[:rows])
                rest = add_up(rest[: half - rows], came[rows:]).astype(jnp.bfloat16)
            own.append(mine)
            rests.append(rest)
        owns.append(own)
        restss.append(rests)
        if split:
            own_gives.append(jnp.concatenate(gives, axis=1))
    for step in range(steps_here):
        own, rests = owns[step], restss[step]
        if step == 0 or not F_SPLIT1:
            give = jnp.concatenate(rests, axis=1)
            if step == 0 and F_Z2R == 1:
                give = after(give, *last)
            if step == 0 and F_Z2R == 3:
                give = after(give, crossings[back_cuts[0]])
            if step == 0 and F_Z2R == 4:
                give = after(give, crossings[-1])
            if step and F_FIN0:
                give = after(give, finals[step - 1])
            came = swap(give, "sub", sub_bits[0])
        else:
            came = jnp.concatenate([swap(give, "sub", sub_bits[0]) for give in rests], axis=1)
        own = jnp.concatenate([add_up(*mine) for mine in own], axis=1)
        finals.append(add_up(own, came) if step >= F_OWN0 else add_up(own, came).astype(jnp.bfloat16))
    crossed = swap(join(*own_gives), "ep", ep_bits[0])
    for n in range(len(own_gives)):
        step = steps_here - len(own_gives) + n
        finals[step] = add_up(finals[step], crossed[n * rows : (n + 1) * rows]).astype(jnp.bfloat16)
    return jnp.stack(finals)


def solution(mesh):
    rows = P(None, ("groups", "ep", "sub"), None)
    return jax.shard_map(
        body,
        mesh=mesh,
        in_specs=(rows, rows, rows, rows, P("ep", None, "sub"), P("ep", None, "sub"), P("ep", "sub", None)),
        out_specs=rows,
        check_vma=False,
    )
```

time: 88.5 us -> 81 us (0.915)
  waiting for transfers between devices: 35.7 us -> 20.5 us
  other arithmetic: 3.21 us -> 5.51 us
  matrix products: 7.81 us -> 10.1 us
  Pallas kernels: 0 us -> 2.02 us
    ppermute x34 -> x33, waiting for transfers between devices: 35.7 us -> 20.5 us  [swap(): return lax.ppermute(value, axis_name, [(i, i ^ bit) for i in range(count)])]
    concatenate x9 -> x11, other arithmetic: 0.13 us -> 3.54 us  [join(): return jnp.concatenate(parts, axis=0)]
    dot_general x12, matrix products: 7.81 us -> 10.1 us  [the longest x4 4.77 us: body(): up_value += jnp.dot(part, w_up[0, span], preferred_element_type=jnp.float32)]
    pallas_call x0 -> x1, Pallas kernels: none -> 2.02 us  [prepare(): pl.pallas_call(functools.partial(prepare_kernel, ep_count, extra, cuts),...]
    unnamed x36 -> x32, local copies, waits for them, and re-layouts: 3.98 us -> 5.47 us
    convert_element_type x6 -> x4, other arithmetic: 1.33 us -> 0.19 us  [body(): rest = add_up(held[rows:half], came).astype(jnp.bfloat16)]
    ppermute x34 -> x33, starting transfers between devices: 35.3 us -> 35.9 us  [swap(): return lax.ppermute(value, axis_name, [(i, i ^ bit) for i in range(count)])]
  transfers between devices with their start and end apart: 34 -> 33, of which waited for: 20 -> 15; matrix products, arithmetic and copies ran while one was open for 7% -> 23% of each run, Pallas kernels for 0% -> 0%
where the time goes in v4:
time: 81 us; the launch traced here: 80.5 us
  starting transfers between devices  35.9 us (44%)
  waiting for transfers between devices  20.5 us (25%)
  matrix products  10.1 us (12%)
  local copies, waits for them, and re-layouts  5.87 us (7%)
  other arithmetic  5.51 us (7%)
  Pallas kernels  2.02 us (2%)
    ppermute x33, starting transfers between devices, swap(): return lax.ppermute(value, axis_name, [(i, i ^ bit) for i in range(count)])  35.9 us
    ppermute x33, waiting for transfers between devices, swap(): return lax.ppermute(value, axis_name, [(i, i ^ bit) for i in range(count)])  20.5 us
    unnamed x32, local copies, waits for them, and re-layouts  5.47 us
    dot_general x4, matrix products, body(): up_value += jnp.dot(part, w_up[0, span], preferred_element_type=jnp.float32)  4.77 us
    concatenate x11, other arithmetic, join(): return jnp.concatenate(parts, axis=0)  3.54 us
    dot_general x4, matrix products, body(): jnp.dot(hidden, w_down[0, :, start:end], preferred_element_type=jnp.float32)  2.73 us
    dot_general x4, matrix products, body(): jnp.dot(part, w_gate[0, span], preferred_element_type=jnp.float32)  2.56 us
    pallas_call x1, Pallas kernels, prepare(): pl.pallas_call(functools.partial(prepare_kernel, ep_count, extra, cuts),...  2.02 us
  transfers between devices with their start and end apart: 33, of which 15 were waited for; matrix products, arithmetic and copies ran while one was open for 23% of the time, Pallas kernels for 0%

profile of v4, /device:TPU:0, one launch (start us, length us, event | category | flops | bytes accessed | tf_op | source)
XLA Modules:
  0.0 80.5 jit_solution(10158937123594865532)
XLA Ops:
  0.0 2.0 %shard_map.73 = (bf16[16,7296]{1,0:T(8,128)(2,1)}, bf16[8,3712]{1,0:T(8,128)(2,1)}, bf16[8,3584]{1,0:T(8,128)(2,1)}, bf16[8,3712]{1,0:T(8,128)(2,1)}, bf16[8,3584]{1,0:T(8,128)(2,1)}) custom-call(bf16[2,8,7168]{2,1,0:T(8,128)(2,1)} %codes_hbm.1, f32[2,8,56]{2,1,0:T(8,128)} %scales_hbm.1, s32[2,2,8]{2,1,0:T(2,128)} %bitcast.58, s32[2,2,8]{2,1,0:T(2,128)} %bitcast.59), custom_call_target="tpu_custom_call" | custom-call | tf_op jit(solution)/shard_map/pallas_call | solution.py:106
  2.0 4.1 %collective-permute-start.5 = (bf16[8,3584]{1,0:T(8,128)(2,1)}, bf16[8,3584]{1,0:T(8,128)(2,1)S(1)}, u32[]{:S(2)}, u32[]{:S(2)}) collective-permute-start(bf16[8,3584]{1,0:T(8,128)(2,1)} %get-tuple-element.24), channel_id=1, source_target_pairs={{0,2},{1,3},{2,0},{3,1},{4,6},{5,7},{6,4},{7,5},{8,10},{9,11},{10,... | collective-permute-start | bytes 172040 | tf_op jit(solution)/shard_map/ppermute | solution.py:31
  6.2 1.7 %collective-permute-start.2 = (bf16[16,7296]{1,0:T(8,128)(2,1)}, bf16[16,7296]{1,0:T(8,128)(2,1)S(1)}, u32[]{:S(2)}, u32[]{:S(2)}) collective-permute-start(bf16[16,7296]{1,0:T(8,128)(2,1)} %get-tuple-element.23), channel_id=1, source_target_pairs={{0,8},{4,12},{8,0},{12,4},{1,9},{5,13},{9,1},{13,5},{2,10},{6,14},... | collective-permute-start | bytes 700424 | tf_op jit(solution)/shard_map/ppermute | solution.py:31
  8.8 0.8 %constant_dynamic-update-slice_fusion.4 = (bf16[64,3712]{1,0:T(8,128)(2,1)S(1)}, bf16[128,3712]{1,0:T(8,128)(2,1)S(1)}) fusion(bf16[8,3712]{1,0:T(8,128)(2,1)} %get-tuple-element.22), kind=kLoop, calls=%fused_computation.92 | loop fusion | bytes 178176
  9.6 2.7 %collective-permute-start.16 = (bf16[8,3584]{1,0:T(8,128)(2,1)}, bf16[8,3584]{1,0:T(8,128)(2,1)S(1)}, u32[]{:S(2)}, u32[]{:S(2)}) collective-permute-start(bf16[8,3584]{1,0:T(8,128)(2,1)} %get-tuple-element.32), channel_id=1, source_target_pairs={{0,2},{1,3},{2,0},{3,1},{4,6},{5,7},{6,4},{7,5},{8,10},{9,11},{10,... | collective-permute-start | bytes 172040 | tf_op jit(solution)/shard_map/ppermute | solution.py:31
  12.3 0.9 %constant_dynamic-update-slice_fusion.31 = bf16[64,3584]{1,0:T(8,128)(2,1)S(1)} fusion(bf16[8,3584]{1,0:T(8,128)(2,1)} %get-tuple-element.32), kind=kLoop, calls=%fused_computation.119 | loop fusion | bytes 114688
  14.3 0.8 %constant_dynamic-update-slice_fusion.26 = bf16[64,3712]{1,0:T(8,128)(2,1)S(1)} fusion(bf16[8,3712]{1,0:T(8,128)(2,1)} %get-tuple-element.26), kind=kLoop, calls=%fused_computation.114 | loop fusion | bytes 118784
  15.2 2.3 %collective-permute-start.6 = (bf16[16,3584]{1,0:T(8,128)(2,1)S(1)}, bf16[16,3584]{1,0:T(8,128)(2,1)S(1)}, u32[]{:S(2)}, u32[]{:S(2)}) collective-permute-start(bf16[16,3584]{1,0:T(8,128)(2,1)S(1)} %pad_maximum_fusion.9), channel_id=1, source_target_pairs={{0,1},{1,0},{2,3},{3,2},{4,5},{5,4},{6,7},{7,6},{8,9},{9,8},{10,11... | collective-permute-start | bytes 344072 | tf_op jit(solution)/shard_map/ppermute | solution.py:31
  17.5 0.8 %pad_maximum_fusion.7 = bf16[16,3712]{1,0:T(8,128)(2,1)S(1)} fusion(bf16[8,3712]{1,0:T(8,128)(2,1)S(1)} %collective-permute-done, bf16[8,3712]{1,0:T(8,128)(2,1)} %get-tuple-element.22), kind=kLoop, calls=%fused_computation.73 | loop fusion | flops 237568 | bytes 237568 | tf_op jit(solution)/shard_map/concatenate | solution.py:39
  18.4 0.8 %pad_maximum_fusion.10 = bf16[16,3584]{1,0:T(8,128)(2,1)S(1)} fusion(bf16[8,3584]{1,0:T(8,128)(2,1)S(1)} %collective-permute-done.16, bf16[8,3584]{1,0:T(8,128)(2,1)} %get-tuple-element.32), kind=kLoop, calls=%fused_computation.78 | loop fusion | flops 229376 | bytes 229376 | tf_op jit(solution)/shard_map/concatenate | solution.py:39
  19.3 2.0 %collective-permute-start.17 = (bf16[16,3584]{1,0:T(8,128)(2,1)S(1)}, bf16[16,3584]{1,0:T(8,128)(2,1)S(1)}, u32[]{:S(2)}, u32[]{:S(2)}) collective-permute-start(bf16[16,3584]{1,0:T(8,128)(2,1)S(1)} %pad_maximum_fusion.10), channel_id=1, source_target_pairs={{0,1},{1,0},{2,3},{3,2},{4,5},{5,4},{6,7},{7,6},{8,9},{9,8},{10,11... | collective-permute-start | bytes 344072 | tf_op jit(solution)/shard_map/ppermute | solution.py:31
  21.3 0.8 %pad_maximum_fusion.8 = bf16[16,3712]{1,0:T(8,128)(2,1)S(1)} fusion(bf16[8,3712]{1,0:T(8,128)(2,1)S(1)} %collective-permute-done.11, bf16[8,3712]{1,0:T(8,128)(2,1)} %get-tuple-element.26), kind=kLoop, calls=%fused_computation.74 | loop fusion | flops 237568 | bytes 237568 | tf_op jit(solution)/shard_map/concatenate | solution.py:39
  22.6 1.6 %collective-permute-start.7 = (bf16[24,3584]{1,0:T(8,128)(2,1)S(1)}, bf16[24,3584]{1,0:T(8,128)(2,1)S(1)}, u32[]{:S(2)}, u32[]{:S(2)}) collective-permute-start(bf16[24,3584]{1,0:T(8,128)(2,1)S(1)} %pad_maximum_fusion.5), channel_id=1, source_target_pairs={{0,8},{4,12},{8,0},{12,4},{1,9},{5,13},{9,1},{13,5},{2,10},{6,14},... | collective-permute-start | bytes 516104 | tf_op jit(solution)/shard_map/ppermute | solution.py:31
  24.6 1.6 %collective-permute-start.3 = (bf16[24,3712]{1,0:T(8,128)(2,1)S(1)}, bf16[24,3712]{1,0:T(8,128)(2,1)S(1)}, u32[]{:S(2)}, u32[]{:S(2)}) collective-permute-start(bf16[24,3712]{1,0:T(8,128)(2,1)S(1)} %pad_maximum_fusion.3), channel_id=1, source_target_pairs={{0,8},{4,12},{8,0},{12,4},{1,9},{5,13},{9,1},{13,5},{2,10},{6,14},... | collective-permute-start | bytes 534536 | tf_op jit(solution)/shard_map/ppermute | solution.py:31
  26.2 0.9 %collective-permute-done.17 = bf16[16,3584]{1,0:T(8,128)(2,1)S(1)} collective-permute-done((bf16[16,3584]{1,0:T(8,128)(2,1)S(1)}, bf16[16,3584]{1,0:T(8,128)(2,1)S(1)}, u32[]{:S(2)}, u32[]{:S(2)}) %collective-permute-start.17) | collective-permute-done | bytes 114720 | tf_op jit(solution)/shard_map/ppermute | solution.py:31
  27.1 1.4 %collective-permute-done.12 = bf16[16,3712]{1,0:T(8,128)(2,1)S(1)} collective-permute-done((bf16[16,3712]{1,0:T(8,128)(2,1)S(1)}, bf16[16,3712]{1,0:T(8,128)(2,1)S(1)}, u32[]{:S(2)}, u32[]{:S(2)}) %collective-permute-start.12) | collective-permute-done | bytes 118816 | tf_op jit(solution)/shard_map/ppermute | solution.py:31
  29.4 1.8 %collective-permute-done.3 = bf16[24,3712]{1,0:T(8,128)(2,1)S(1)} collective-permute-done((bf16[24,3712]{1,0:T(8,128)(2,1)S(1)}, bf16[24,3712]{1,0:T(8,128)(2,1)S(1)}, u32[]{:S(2)}, u32[]{:S(2)}) %collective-permute-start.3) | collective-permute-done | bytes 178208 | tf_op jit(solution)/shard_map/ppermute | solution.py:31
  31.2 1.5 %collective-permute-start.18 = (bf16[24,3584]{1,0:T(8,128)(2,1)S(1)}, bf16[24,3584]{1,0:T(8,128)(2,1)S(1)}, u32[]{:S(2)}, u32[]{:S(2)}) collective-permute-start(bf16[24,3584]{1,0:T(8,128)(2,1)S(1)} %pad_maximum_fusion.6), channel_id=1, source_target_pairs={{0,8},{4,12},{8,0},{12,4},{1,9},{5,13},{9,1},{13,5},{2,10},{6,14},... | collective-permute-start | bytes 516104 | tf_op jit(solution)/shard_map/ppermute | solution.py:31
  33.4 2.8 %fusion.10 = f32[128,512]{1,0:T(8,128)S(1)} fusion(bf16[128,3584]{1,0:T(8,128)(2,1)S(1)} %constant_dynamic-update-slice_fusion.16, bf16[1,7168,512]{2,1,0:T(8,128)(2,1)} %param.12), kind=kOutput, calls=%fused_computation.14 | convolution fusion | flops 469762048 | bytes 4849664 | tf_op jit(solution)/shard_map/dot_general | solution.py:172
  39.5 1.0 %slice-done.5 = s8[3145728]{0:T(1024)(128)(4,1)S(1)} async-done(((s8[7340032]{0:T(1024)(128)(4,1)}), s8[3145728]{0:T(1024)(128)(4,1)S(1)}, s32[]{:S(2)}) %slice-start.5) | async-done | bytes 3145752
  44.7 1.6 %collective-permute-start.23 = (bf16[24,3584]{1,0:T(8,128)(2,1)S(1)}, bf16[24,3584]{1,0:T(8,128)(2,1)S(1)}, u32[]{:S(2)}, u32[]{:S(2)}) collective-permute-start(bf16[24,3584]{1,0:T(8,128)(2,1)S(1)} %slice.279), channel_id=1, source_target_pairs={{0,8},{4,12},{8,0},{12,4},{1,9},{5,13},{9,1},{13,5},{2,10},{6,14},... | collective-permute-start | bytes 516104 | tf_op jit(solution)/shard_map/ppermute | solution.py:31
  52.1 3.0 %collective-permute-done.10 = bf16[24,3584]{1,0:T(8,128)(2,1)S(1)} collective-permute-done((bf16[24,3584]{1,0:T(8,128)(2,1)S(1)}, bf16[24,3584]{1,0:T(8,128)(2,1)S(1)}, u32[]{:S(2)}, u32[]{:S(2)}) %collective-permute-start.10) | collective-permute-done | bytes 172064 | tf_op jit(solution)/shard_map/ppermute | solution.py:31
  55.6 1.6 %collective-permute-start.29 = (bf16[24,3584]{1,0:T(8,128)(2,1)S(1)}, bf16[24,3584]{1,0:T(8,128)(2,1)S(1)}, u32[]{:S(2)}, u32[]{:S(2)}) collective-permute-start(bf16[24,3584]{1,0:T(8,128)(2,1)S(1)} %slice.298), channel_id=1, source_target_pairs={{0,8},{4,12},{8,0},{12,4},{1,9},{5,13},{9,1},{13,5},{2,10},{6,14},... | collective-permute-start | bytes 516104 | tf_op jit(solution)/shard_map/ppermute | solution.py:31
  57.1 1.7 %collective-permute-start.22 = (bf16[16,3584]{1,0:T(8,128)(2,1)S(1)}, bf16[16,3584]{1,0:T(8,128)(2,1)S(1)}, u32[]{:S(2)}, u32[]{:S(2)}) collective-permute-start(bf16[16,3584]{1,0:T(8,128)(2,1)S(1)} %slice.265), channel_id=1, source_target_pairs={{0,1},{1,0},{2,3},{3,2},{4,5},{5,4},{6,7},{7,6},{8,9},{9,8},{10,11... | collective-permute-start | bytes 344072 | tf_op jit(solution)/shard_map/ppermute | solution.py:31
  59.7 1.6 %collective-permute-start.26 = (bf16[16,7168]{1,0:T(8,128)(2,1)S(1)}, bf16[16,7168]{1,0:T(8,128)(2,1)S(1)}, u32[]{:S(2)}, u32[]{:S(2)}) collective-permute-start(bf16[16,7168]{1,0:T(8,128)(2,1)S(1)} %maximum_maximum_fusion), channel_id=1, source_target_pairs={{0,8},{4,12},{8,0},{12,4},{1,9},{5,13},{9,1},{13,5},{2,10},{6,14},... | collective-permute-start | bytes 688136 | tf_op jit(solution)/shard_map/ppermute | solution.py:31
  61.3 1.6 %collective-permute-done.22 = bf16[16,3584]{1,0:T(8,128)(2,1)S(1)} collective-permute-done((bf16[16,3584]{1,0:T(8,128)(2,1)S(1)}, bf16[16,3584]{1,0:T(8,128)(2,1)S(1)}, u32[]{:S(2)}, u32[]{:S(2)}) %collective-permute-start.22) | collective-permute-done | bytes 114720 | tf_op jit(solution)/shard_map/ppermute | solution.py:31
  62.9 1.2 %collective-permute-done.24 = bf16[16,3584]{1,0:T(8,128)(2,1)S(1)} collective-permute-done((bf16[16,3584]{1,0:T(8,128)(2,1)S(1)}, bf16[16,3584]{1,0:T(8,128)(2,1)S(1)}, u32[]{:S(2)}, u32[]{:S(2)}) %collective-permute-start.24) | collective-permute-done | bytes 114720 | tf_op jit(solution)/shard_map/ppermute | solution.py:31
  64.2 2.7 %collective-permute-start.25 = (bf16[8,7168]{1,0:T(8,128)(2,1)S(1)}, bf16[8,7168]{1,0:T(8,128)(2,1)S(1)}, u32[]{:S(2)}, u32[]{:S(2)}) collective-permute-start(bf16[8,7168]{1,0:T(8,128)(2,1)S(1)} %pad_maximum_fusion.11), channel_id=1, source_target_pairs={{0,2},{1,3},{2,0},{3,1},{4,6},{5,7},{6,4},{7,5},{8,10},{9,11},{10,... | collective-permute-start | bytes 344072 | tf_op jit(solution)/shard_map/ppermute | solution.py:31
  66.9 1.6 %collective-permute-start.30 = (bf16[16,3584]{1,0:T(8,128)(2,1)S(1)}, bf16[16,3584]{1,0:T(8,128)(2,1)S(1)}, u32[]{:S(2)}, u32[]{:S(2)}) collective-permute-start(bf16[16,3584]{1,0:T(8,128)(2,1)S(1)} %slice.299), channel_id=1, source_target_pairs={{0,1},{1,0},{2,3},{3,2},{4,5},{5,4},{6,7},{7,6},{8,9},{9,8},{10,11... | collective-permute-start | bytes 344072 | tf_op jit(solution)/shard_map/ppermute | solution.py:31
  69.2 3.9 %collective-permute-done.30 = bf16[16,3584]{1,0:T(8,128)(2,1)S(1)} collective-permute-done((bf16[16,3584]{1,0:T(8,128)(2,1)S(1)}, bf16[16,3584]{1,0:T(8,128)(2,1)S(1)}, u32[]{:S(2)}, u32[]{:S(2)}) %collective-permute-start.30) | collective-permute-done | bytes 114720 | tf_op jit(solution)/shard_map/ppermute | solution.py:31
  74.6 1.6 %collective-permute-start.31 = (bf16[8,3584]{1,0:T(8,128)(2,1)S(1)}, bf16[8,3584]{1,0:T(8,128)(2,1)S(1)}, u32[]{:S(2)}, u32[]{:S(2)}) collective-permute-start(bf16[8,3584]{1,0:T(8,128)(2,1)S(1)} %get-tuple-element.61), channel_id=1, source_target_pairs={{0,2},{1,3},{2,0},{3,1},{4,6},{5,7},{6,4},{7,5},{8,10},{9,11},{10,... | collective-permute-start | bytes 172040 | tf_op jit(solution)/shard_map/ppermute | solution.py:31
  76.2 2.8 %collective-permute-done.32 = bf16[8,3584]{1,0:T(8,128)(2,1)S(1)} collective-permute-done((bf16[8,3584]{1,0:T(8,128)(2,1)S(1)}, bf16[8,3584]{1,0:T(8,128)(2,1)S(1)}, u32[]{:S(2)}, u32[]{:S(2)}) %collective-permute-start.32) | collective-permute-done | bytes 57376 | tf_op jit(solution)/shard_map/ppermute | solution.py:31
  (138 shorter events, 22.7 us)
Async XLA Ops:
  2.0 7.6 %collective-permute-start.5 = (bf16[8,3584]{1,0:T(8,128)(2,1)}, bf16[8,3584]{1,0:T(8,128)(2,1)S(1)}, u32[]{:S(2)}, u32[]{:S(2)}) collective-permute-start(bf16[8,3584]{1,0:T(8,128)(2,1)} %get-tuple-element.24), channel_id=1, source_target_pairs={{0,2},{1,3},{2,0},{3,1},{4,6},{5,7},{6,4},{7,5},{8,10},{9,11},{10,... | collective-permute-start | bytes 172040 | tf_op jit(solution)/shard_map/ppermute | solution.py:31
  6.1 11.4 %collective-permute-start = (bf16[8,3712]{1,0:T(8,128)(2,1)}, bf16[8,3712]{1,0:T(8,128)(2,1)S(1)}, u32[]{:S(2)}, u32[]{:S(2)}) collective-permute-start(bf16[8,3712]{1,0:T(8,128)(2,1)} %get-tuple-element.22), channel_id=1, source_target_pairs={{0,2},{1,3},{2,0},{3,1},{4,6},{5,7},{6,4},{7,5},{8,10},{9,11},{10,... | collective-permute-start | bytes 178184 | tf_op jit(solution)/shard_map/ppermute | solution.py:31
  6.2 20.8 %collective-permute-start.2 = (bf16[16,7296]{1,0:T(8,128)(2,1)}, bf16[16,7296]{1,0:T(8,128)(2,1)S(1)}, u32[]{:S(2)}, u32[]{:S(2)}) collective-permute-start(bf16[16,7296]{1,0:T(8,128)(2,1)} %get-tuple-element.23), channel_id=1, source_target_pairs={{0,8},{4,12},{8,0},{12,4},{1,9},{5,13},{9,1},{13,5},{2,10},{6,14},... | collective-permute-start | bytes 700424 | tf_op jit(solution)/shard_map/ppermute | solution.py:31
  9.6 8.8 %collective-permute-start.16 = (bf16[8,3584]{1,0:T(8,128)(2,1)}, bf16[8,3584]{1,0:T(8,128)(2,1)S(1)}, u32[]{:S(2)}, u32[]{:S(2)}) collective-permute-start(bf16[8,3584]{1,0:T(8,128)(2,1)} %get-tuple-element.32), channel_id=1, source_target_pairs={{0,2},{1,3},{2,0},{3,1},{4,6},{5,7},{6,4},{7,5},{8,10},{9,11},{10,... | collective-permute-start | bytes 172040 | tf_op jit(solution)/shard_map/ppermute | solution.py:31
  13.1 8.1 %collective-permute-start.11 = (bf16[8,3712]{1,0:T(8,128)(2,1)}, bf16[8,3712]{1,0:T(8,128)(2,1)S(1)}, u32[]{:S(2)}, u32[]{:S(2)}) collective-permute-start(bf16[8,3712]{1,0:T(8,128)(2,1)} %get-tuple-element.26), channel_id=1, source_target_pairs={{0,2},{1,3},{2,0},{3,1},{4,6},{5,7},{6,4},{7,5},{8,10},{9,11},{10,... | collective-permute-start | bytes 178184 | tf_op jit(solution)/shard_map/ppermute | solution.py:31
  15.2 7.4 %collective-permute-start.6 = (bf16[16,3584]{1,0:T(8,128)(2,1)S(1)}, bf16[16,3584]{1,0:T(8,128)(2,1)S(1)}, u32[]{:S(2)}, u32[]{:S(2)}) collective-permute-start(bf16[16,3584]{1,0:T(8,128)(2,1)S(1)} %pad_maximum_fusion.9), channel_id=1, source_target_pairs={{0,1},{1,0},{2,3},{3,2},{4,5},{5,4},{6,7},{7,6},{8,9},{9,8},{10,11... | collective-permute-start | bytes 344072 | tf_op jit(solution)/shard_map/ppermute | solution.py:31
  18.3 6.2 %collective-permute-start.1 = (bf16[16,3712]{1,0:T(8,128)(2,1)S(1)}, bf16[16,3712]{1,0:T(8,128)(2,1)S(1)}, u32[]{:S(2)}, u32[]{:S(2)}) collective-permute-start(bf16[16,3712]{1,0:T(8,128)(2,1)S(1)} %pad_maximum_fusion.7), channel_id=1, source_target_pairs={{0,1},{1,0},{2,3},{3,2},{4,5},{5,4},{6,7},{7,6},{8,9},{9,8},{10,11... | collective-permute-start | bytes 356360 | tf_op jit(solution)/shard_map/ppermute | solution.py:31
  19.3 7.8 %collective-permute-start.17 = (bf16[16,3584]{1,0:T(8,128)(2,1)S(1)}, bf16[16,3584]{1,0:T(8,128)(2,1)S(1)}, u32[]{:S(2)}, u32[]{:S(2)}) collective-permute-start(bf16[16,3584]{1,0:T(8,128)(2,1)S(1)} %pad_maximum_fusion.10), channel_id=1, source_target_pairs={{0,1},{1,0},{2,3},{3,2},{4,5},{5,4},{6,7},{7,6},{8,9},{9,8},{10,11... | collective-permute-start | bytes 344072 | tf_op jit(solution)/shard_map/ppermute | solution.py:31
  22.1 6.3 %collective-permute-start.12 = (bf16[16,3712]{1,0:T(8,128)(2,1)S(1)}, bf16[16,3712]{1,0:T(8,128)(2,1)S(1)}, u32[]{:S(2)}, u32[]{:S(2)}) collective-permute-start(bf16[16,3712]{1,0:T(8,128)(2,1)S(1)} %pad_maximum_fusion.8), channel_id=1, source_target_pairs={{0,1},{1,0},{2,3},{3,2},{4,5},{5,4},{6,7},{7,6},{8,9},{9,8},{10,11... | collective-permute-start | bytes 356360 | tf_op jit(solution)/shard_map/ppermute | solution.py:31
  22.6 6.7 %collective-permute-start.7 = (bf16[24,3584]{1,0:T(8,128)(2,1)S(1)}, bf16[24,3584]{1,0:T(8,128)(2,1)S(1)}, u32[]{:S(2)}, u32[]{:S(2)}) collective-permute-start(bf16[24,3584]{1,0:T(8,128)(2,1)S(1)} %pad_maximum_fusion.5), channel_id=1, source_target_pairs={{0,8},{4,12},{8,0},{12,4},{1,9},{5,13},{9,1},{13,5},{2,10},{6,14},... | collective-permute-start | bytes 516104 | tf_op jit(solution)/shard_map/ppermute | solution.py:31
  24.6 6.6 %collective-permute-start.3 = (bf16[24,3712]{1,0:T(8,128)(2,1)S(1)}, bf16[24,3712]{1,0:T(8,128)(2,1)S(1)}, u32[]{:S(2)}, u32[]{:S(2)}) collective-permute-start(bf16[24,3712]{1,0:T(8,128)(2,1)S(1)} %pad_maximum_fusion.3), channel_id=1, source_target_pairs={{0,8},{4,12},{8,0},{12,4},{1,9},{5,13},{9,1},{13,5},{2,10},{6,14},... | collective-permute-start | bytes 534536 | tf_op jit(solution)/shard_map/ppermute | solution.py:31
  29.3 4.0 %collective-permute-start.8 = (bf16[64,3584]{1,0:T(8,128)(2,1)S(1)}, bf16[64,3584]{1,0:T(8,128)(2,1)S(1)}, u32[]{:S(2)}, u32[]{:S(2)}) collective-permute-start(bf16[64,3584]{1,0:T(8,128)(2,1)S(1)} %get-tuple-element.53), channel_id=1, source_target_pairs={{0,4},{4,0},{8,12},{12,8},{1,5},{5,1},{9,13},{13,9},{2,6},{6,2},{1... | collective-permute-start | bytes 1376264 | tf_op jit(solution)/shard_map/ppermute | solution.py:31
  31.2 11.2 %collective-permute-start.18 = (bf16[24,3584]{1,0:T(8,128)(2,1)S(1)}, bf16[24,3584]{1,0:T(8,128)(2,1)S(1)}, u32[]{:S(2)}, u32[]{:S(2)}) collective-permute-start(bf16[24,3584]{1,0:T(8,128)(2,1)S(1)} %pad_maximum_fusion.6), channel_id=1, source_target_pairs={{0,8},{4,12},{8,0},{12,4},{1,9},{5,13},{9,1},{13,5},{2,10},{6,14},... | collective-permute-start | bytes 516104 | tf_op jit(solution)/shard_map/ppermute | solution.py:31
  32.7 9.8 %collective-permute-start.13 = (bf16[24,3712]{1,0:T(8,128)(2,1)S(1)}, bf16[24,3712]{1,0:T(8,128)(2,1)S(1)}, u32[]{:S(2)}, u32[]{:S(2)}) collective-permute-start(bf16[24,3712]{1,0:T(8,128)(2,1)S(1)} %pad_maximum_fusion.4), channel_id=1, source_target_pairs={{0,8},{4,12},{8,0},{12,4},{1,9},{5,13},{9,1},{13,5},{2,10},{6,14},... | collective-permute-start | bytes 534536 | tf_op jit(solution)/shard_map/ppermute | solution.py:31
  33.3 3.6 %collective-permute-start.4 = (bf16[64,3712]{1,0:T(8,128)(2,1)S(1)}, bf16[64,3712]{1,0:T(8,128)(2,1)S(1)}, u32[]{:S(2)}, u32[]{:S(2)}) collective-permute-start(bf16[64,3712]{1,0:T(8,128)(2,1)S(1)} %get-tuple-element.51), channel_id=1, source_target_pairs={{0,4},{4,0},{8,12},{12,8},{1,5},{5,1},{9,13},{13,9},{2,6},{6,2},{1... | collective-permute-start | bytes 1425416 | tf_op jit(solution)/shard_map/ppermute | solution.py:31
  42.5 2.0 %collective-permute-start.9 = (bf16[64,3584]{1,0:T(8,128)(2,1)S(1)}, bf16[64,3584]{1,0:T(8,128)(2,1)S(1)}, u32[]{:S(2)}, u32[]{:S(2)}) collective-permute-start(bf16[64,3584]{1,0:T(8,128)(2,1)S(1)} %slice.261), channel_id=1, source_target_pairs={{0,4},{4,0},{8,12},{12,8},{1,5},{5,1},{9,13},{13,9},{2,6},{6,2},{1... | collective-permute-start | bytes 1376264 | tf_op jit(solution)/shard_map/ppermute | solution.py:31
  42.6 4.2 %collective-permute-start.19 = (bf16[64,3584]{1,0:T(8,128)(2,1)S(1)}, bf16[64,3584]{1,0:T(8,128)(2,1)S(1)}, u32[]{:S(2)}, u32[]{:S(2)}) collective-permute-start(bf16[64,3584]{1,0:T(8,128)(2,1)S(1)} %constant_dynamic-update-slice_fusion.27), channel_id=1, source_target_pairs={{0,4},{4,0},{8,12},{12,8},{1,5},{5,1},{9,13},{13,9},{2,6},{6,2},{1... | collective-permute-start | bytes 1376264 | tf_op jit(solution)/shard_map/ppermute | solution.py:31
  43.1 5.1 %collective-permute-start.14 = (bf16[64,3712]{1,0:T(8,128)(2,1)S(1)}, bf16[64,3712]{1,0:T(8,128)(2,1)S(1)}, u32[]{:S(2)}, u32[]{:S(2)}) collective-permute-start(bf16[64,3712]{1,0:T(8,128)(2,1)S(1)} %constant_dynamic-update-slice_fusion.22), channel_id=1, source_target_pairs={{0,4},{4,0},{8,12},{12,8},{1,5},{5,1},{9,13},{13,9},{2,6},{6,2},{1... | collective-permute-start | bytes 1425416 | tf_op jit(solution)/shard_map/ppermute | solution.py:31
  44.7 7.3 %collective-permute-start.23 = (bf16[24,3584]{1,0:T(8,128)(2,1)S(1)}, bf16[24,3584]{1,0:T(8,128)(2,1)S(1)}, u32[]{:S(2)}, u32[]{:S(2)}) collective-permute-start(bf16[24,3584]{1,0:T(8,128)(2,1)S(1)} %slice.279), channel_id=1, source_target_pairs={{0,8},{4,12},{8,0},{12,4},{1,9},{5,13},{9,1},{13,5},{2,10},{6,14},... | collective-permute-start | bytes 516104 | tf_op jit(solution)/shard_map/ppermute | solution.py:31
  46.3 8.8 %collective-permute-start.10 = (bf16[24,3584]{1,0:T(8,128)(2,1)S(1)}, bf16[24,3584]{1,0:T(8,128)(2,1)S(1)}, u32[]{:S(2)}, u32[]{:S(2)}) collective-permute-start(bf16[24,3584]{1,0:T(8,128)(2,1)S(1)} %slice.264), channel_id=1, source_target_pairs={{0,8},{4,12},{8,0},{12,4},{1,9},{5,13},{9,1},{13,5},{2,10},{6,14},... | collective-permute-start | bytes 516104 | tf_op jit(solution)/shard_map/ppermute | solution.py:31
  51.2 4.0 %collective-permute-start.21 = (bf16[64,3584]{1,0:T(8,128)(2,1)S(1)}, bf16[64,3584]{1,0:T(8,128)(2,1)S(1)}, u32[]{:S(2)}, u32[]{:S(2)}) collective-permute-start(bf16[64,3584]{1,0:T(8,128)(2,1)S(1)} %slice.275), channel_id=1, source_target_pairs={{0,4},{4,0},{8,12},{12,8},{1,5},{5,1},{9,13},{13,9},{2,6},{6,2},{1... | collective-permute-start | bytes 1376264 | tf_op jit(solution)/shard_map/ppermute | solution.py:31
  51.3 4.1 %collective-permute-start.20 = (bf16[64,3584]{1,0:T(8,128)(2,1)S(1)}, bf16[64,3584]{1,0:T(8,128)(2,1)S(1)}, u32[]{:S(2)}, u32[]{:S(2)}) collective-permute-start(bf16[64,3584]{1,0:T(8,128)(2,1)S(1)} %slice.273), channel_id=1, source_target_pairs={{0,4},{4,0},{8,12},{12,8},{1,5},{5,1},{9,13},{13,9},{2,6},{6,2},{1... | collective-permute-start | bytes 1376264 | tf_op jit(solution)/shard_map/ppermute | solution.py:31
  55.6 11.3 %collective-permute-start.29 = (bf16[24,3584]{1,0:T(8,128)(2,1)S(1)}, bf16[24,3584]{1,0:T(8,128)(2,1)S(1)}, u32[]{:S(2)}, u32[]{:S(2)}) collective-permute-start(bf16[24,3584]{1,0:T(8,128)(2,1)S(1)} %slice.298), channel_id=1, source_target_pairs={{0,8},{4,12},{8,0},{12,4},{1,9},{5,13},{9,1},{13,5},{2,10},{6,14},... | collective-permute-start | bytes 516104 | tf_op jit(solution)/shard_map/ppermute | solution.py:31
  57.1 5.8 %collective-permute-start.22 = (bf16[16,3584]{1,0:T(8,128)(2,1)S(1)}, bf16[16,3584]{1,0:T(8,128)(2,1)S(1)}, u32[]{:S(2)}, u32[]{:S(2)}) collective-permute-start(bf16[16,3584]{1,0:T(8,128)(2,1)S(1)} %slice.265), channel_id=1, source_target_pairs={{0,1},{1,0},{2,3},{3,2},{4,5},{5,4},{6,7},{7,6},{8,9},{9,8},{10,11... | collective-permute-start | bytes 344072 | tf_op jit(solution)/shard_map/ppermute | solution.py:31
  58.8 5.3 %collective-permute-start.24 = (bf16[16,3584]{1,0:T(8,128)(2,1)S(1)}, bf16[16,3584]{1,0:T(8,128)(2,1)S(1)}, u32[]{:S(2)}, u32[]{:S(2)}) collective-permute-start(bf16[16,3584]{1,0:T(8,128)(2,1)S(1)} %slice.280), channel_id=1, source_target_pairs={{0,1},{1,0},{2,3},{3,2},{4,5},{5,4},{6,7},{7,6},{8,9},{9,8},{10,11... | collective-permute-start | bytes 344072 | tf_op jit(solution)/shard_map/ppermute | solution.py:31
  59.1 9.4 %collective-permute-start.27 = (bf16[24,3584]{1,0:T(8,128)(2,1)S(1)}, bf16[24,3584]{1,0:T(8,128)(2,1)S(1)}, u32[]{:S(2)}, u32[]{:S(2)}) collective-permute-start(bf16[24,3584]{1,0:T(8,128)(2,1)S(1)} %slice.293), channel_id=1, source_target_pairs={{0,8},{4,12},{8,0},{12,4},{1,9},{5,13},{9,1},{13,5},{2,10},{6,14},... | collective-permute-start | bytes 516104 | tf_op jit(solution)/shard_map/ppermute | solution.py:31
  59.7 16.5 %collective-permute-start.26 = (bf16[16,7168]{1,0:T(8,128)(2,1)S(1)}, bf16[16,7168]{1,0:T(8,128)(2,1)S(1)}, u32[]{:S(2)}, u32[]{:S(2)}) collective-permute-start(bf16[16,7168]{1,0:T(8,128)(2,1)S(1)} %maximum_maximum_fusion), channel_id=1, source_target_pairs={{0,8},{4,12},{8,0},{12,4},{1,9},{5,13},{9,1},{13,5},{2,10},{6,14},... | collective-permute-start | bytes 688136 | tf_op jit(solution)/shard_map/ppermute | solution.py:31
  64.2 12.1 %collective-permute-start.25 = (bf16[8,7168]{1,0:T(8,128)(2,1)S(1)}, bf16[8,7168]{1,0:T(8,128)(2,1)S(1)}, u32[]{:S(2)}, u32[]{:S(2)}) collective-permute-start(bf16[8,7168]{1,0:T(8,128)(2,1)S(1)} %pad_maximum_fusion.11), channel_id=1, source_target_pairs={{0,2},{1,3},{2,0},{3,1},{4,6},{5,7},{6,4},{7,5},{8,10},{9,11},{10,... | collective-permute-start | bytes 344072 | tf_op jit(solution)/shard_map/ppermute | solution.py:31
  66.9 6.1 %collective-permute-start.30 = (bf16[16,3584]{1,0:T(8,128)(2,1)S(1)}, bf16[16,3584]{1,0:T(8,128)(2,1)S(1)}, u32[]{:S(2)}, u32[]{:S(2)}) collective-permute-start(bf16[16,3584]{1,0:T(8,128)(2,1)S(1)} %slice.299), channel_id=1, source_target_pairs={{0,1},{1,0},{2,3},{3,2},{4,5},{5,4},{6,7},{7,6},{8,9},{9,8},{10,11... | collective-permute-start | bytes 344072 | tf_op jit(solution)/shard_map/ppermute | solution.py:31
  68.6 6.0 %collective-permute-start.28 = (bf16[16,3584]{1,0:T(8,128)(2,1)S(1)}, bf16[16,3584]{1,0:T(8,128)(2,1)S(1)}, u32[]{:S(2)}, u32[]{:S(2)}) collective-permute-start(bf16[16,3584]{1,0:T(8,128)(2,1)S(1)} %slice.294), channel_id=1, source_target_pairs={{0,1},{1,0},{2,3},{3,2},{4,5},{5,4},{6,7},{7,6},{8,9},{9,8},{10,11... | collective-permute-start | bytes 344072 | tf_op jit(solution)/shard_map/ppermute | solution.py:31
  73.1 5.9 %collective-permute-start.32 = (bf16[8,3584]{1,0:T(8,128)(2,1)S(1)}, bf16[8,3584]{1,0:T(8,128)(2,1)S(1)}, u32[]{:S(2)}, u32[]{:S(2)}) collective-permute-start(bf16[8,3584]{1,0:T(8,128)(2,1)S(1)} %get-tuple-element.63), channel_id=1, source_target_pairs={{0,2},{1,3},{2,0},{3,1},{4,6},{5,7},{6,4},{7,5},{8,10},{9,11},{10,... | collective-permute-start | bytes 172040 | tf_op jit(solution)/shard_map/ppermute | solution.py:31
  74.6 5.1 %collective-permute-start.31 = (bf16[8,3584]{1,0:T(8,128)(2,1)S(1)}, bf16[8,3584]{1,0:T(8,128)(2,1)S(1)}, u32[]{:S(2)}, u32[]{:S(2)}) collective-permute-start(bf16[8,3584]{1,0:T(8,128)(2,1)S(1)} %get-tuple-element.61), channel_id=1, source_target_pairs={{0,2},{1,3},{2,0},{3,1},{4,6},{5,7},{6,4},{7,5},{8,10},{9,11},{10,... | collective-permute-start | bytes 172040 | tf_op jit(solution)/shard_map/ppermute | solution.py:31
  (12 other events, 70.1 us)

commit v5 on v4

--- a/solution.py
+++ b/solution.py
@@ -10,7 +10,7 @@
 routed_scale = 2.5
 column_parts = 2
 F_Z2 = 2
-F_XORD = 1
+F_XORD = 2
 F_C1 = 1
 F_Z2R = 2
 F_CHOLD = 1
@@ -201,7 +201,7 @@
             for n, bit in enumerate(reversed(sub_bits[1:])):
                 half = (rest.shape[0] + rows) // 2
                 give = rest[half - rows :]
-                if step == 0 and n == 0 and F_Z2R == 2:
+                if step == 0 and n == 0 and F_Z2R in (2, 5):
                     give = after(give, *last)
                 came = swap(give, "sub", bit)
                 mine.append(came[:rows])
@@ -218,7 +218,7 @@
             give = jnp.concatenate(rests, axis=1)
             if step == 0 and F_Z2R == 1:
                 give = after(give, *last)
-            if step == 0 and F_Z2R == 3:
+            if step == 0 and F_Z2R in (3, 5):
                 give = after(give, crossings[back_cuts[0]])
             if step == 0 and F_Z2R == 4:
                 give = after(give, crossings[-1])

time: 81 us -> 79.4 us (0.980)
  waiting for transfers between devices: 20.5 us -> 18.8 us
    ppermute x33, waiting for transfers between devices: 20.5 us -> 18.8 us  [swap(): return lax.ppermute(value, axis_name, [(i, i ^ bit) for i in range(count)])]
  transfers between devices with their start and end apart: 33 -> 33, of which waited for: 15 -> 14; matrix products, arithmetic and copies ran while one was open for 23% -> 23% of each run, Pallas kernels for 0% -> 0%
where the time goes in v5:
time: 79.4 us; the launch traced here: 78.8 us
  starting transfers between devices  36 us (45%)
  waiting for transfers between devices  18.8 us (24%)
  matrix products  10.1 us (13%)
  local copies, waits for them, and re-layouts  5.88 us (7%)
  other arithmetic  5.51 us (7%)
  Pallas kernels  2.02 us (3%)
    ppermute x33, starting transfers between devices, swap(): return lax.ppermute(value, axis_name, [(i, i ^ bit) for i in range(count)])  36 us
    ppermute x33, waiting for transfers between devices, swap(): return lax.ppermute(value, axis_name, [(i, i ^ bit) for i in range(count)])  18.8 us
    unnamed x32, local copies, waits for them, and re-layouts  5.49 us
    dot_general x4, matrix products, body(): up_value += jnp.dot(part, w_up[0, span], preferred_element_type=jnp.float32)  4.78 us
    concatenate x11, other arithmetic, join(): return jnp.concatenate(parts, axis=0)  3.54 us
    dot_general x4, matrix products, body(): jnp.dot(hidden, w_down[0, :, start:end], preferred_element_type=jnp.float32)  2.72 us
    dot_general x4, matrix products, body(): jnp.dot(part, w_gate[0, span], preferred_element_type=jnp.float32)  2.57 us
    pallas_call x1, Pallas kernels, prepare(): pl.pallas_call(functools.partial(prepare_kernel, ep_count, extra, cuts),...  2.02 us
  transfers between devices with their start and end apart: 33, of which 14 were waited for; matrix products, arithmetic and copies ran while one was open for 23% of the time, Pallas kernels for 0%

profile of v5, /device:TPU:0, one launch (start us, length us, event | category | flops | bytes accessed | tf_op | source)
XLA Modules:
  0.0 78.8 jit_solution(209304943170215185)
XLA Ops:
  0.0 2.0 %shard_map.73 = (bf16[16,7296]{1,0:T(8,128)(2,1)}, bf16[8,3712]{1,0:T(8,128)(2,1)}, bf16[8,3584]{1,0:T(8,128)(2,1)}, bf16[8,3712]{1,0:T(8,128)(2,1)}, bf16[8,3584]{1,0:T(8,128)(2,1)}) custom-call(bf16[2,8,7168]{2,1,0:T(8,128)(2,1)} %codes_hbm.1, f32[2,8,56]{2,1,0:T(8,128)} %scales_hbm.1, s32[2,2,8]{2,1,0:T(2,128)} %bitcast.58, s32[2,2,8]{2,1,0:T(2,128)} %bitcast.59), custom_call_target="tpu_custom_call" | custom-call | tf_op jit(solution)/shard_map/pallas_call | solution.py:106
  2.0 4.1 %collective-permute-start.5 = (bf16[8,3584]{1,0:T(8,128)(2,1)}, bf16[8,3584]{1,0:T(8,128)(2,1)S(1)}, u32[]{:S(2)}, u32[]{:S(2)}) collective-permute-start(bf16[8,3584]{1,0:T(8,128)(2,1)} %get-tuple-element.24), channel_id=1, source_target_pairs={{0,2},{1,3},{2,0},{3,1},{4,6},{5,7},{6,4},{7,5},{8,10},{9,11},{10,... | collective-permute-start | bytes 172040 | tf_op jit(solution)/shard_map/ppermute | solution.py:31
  6.2 1.7 %collective-permute-start.2 = (bf16[16,7296]{1,0:T(8,128)(2,1)}, bf16[16,7296]{1,0:T(8,128)(2,1)S(1)}, u32[]{:S(2)}, u32[]{:S(2)}) collective-permute-start(bf16[16,7296]{1,0:T(8,128)(2,1)} %get-tuple-element.23), channel_id=1, source_target_pairs={{0,8},{4,12},{8,0},{12,4},{1,9},{5,13},{9,1},{13,5},{2,10},{6,14},... | collective-permute-start | bytes 700424 | tf_op jit(solution)/shard_map/ppermute | solution.py:31
  8.8 0.8 %constant_dynamic-update-slice_fusion.4 = (bf16[64,3712]{1,0:T(8,128)(2,1)S(1)}, bf16[128,3712]{1,0:T(8,128)(2,1)S(1)}) fusion(bf16[8,3712]{1,0:T(8,128)(2,1)} %get-tuple-element.22), kind=kLoop, calls=%fused_computation.92 | loop fusion | bytes 178176
  9.6 2.7 %collective-permute-start.16 = (bf16[8,3584]{1,0:T(8,128)(2,1)}, bf16[8,3584]{1,0:T(8,128)(2,1)S(1)}, u32[]{:S(2)}, u32[]{:S(2)}) collective-permute-start(bf16[8,3584]{1,0:T(8,128)(2,1)} %get-tuple-element.32), channel_id=1, source_target_pairs={{0,2},{1,3},{2,0},{3,1},{4,6},{5,7},{6,4},{7,5},{8,10},{9,11},{10,... | collective-permute-start | bytes 172040 | tf_op jit(solution)/shard_map/ppermute | solution.py:31
  12.3 0.9 %constant_dynamic-update-slice_fusion.31 = bf16[64,3584]{1,0:T(8,128)(2,1)S(1)} fusion(bf16[8,3584]{1,0:T(8,128)(2,1)} %get-tuple-element.32), kind=kLoop, calls=%fused_computation.119 | loop fusion | bytes 114688
  13.5 0.8 %pad_maximum_fusion.9 = bf16[16,3584]{1,0:T(8,128)(2,1)S(1)} fusion(bf16[8,3584]{1,0:T(8,128)(2,1)S(1)} %collective-permute-done.5, bf16[8,3584]{1,0:T(8,128)(2,1)} %get-tuple-element.24), kind=kLoop, calls=%fused_computation.77 | loop fusion | flops 229376 | bytes 229376 | tf_op jit(solution)/shard_map/concatenate | solution.py:39
  14.3 0.8 %constant_dynamic-update-slice_fusion.26 = bf16[64,3712]{1,0:T(8,128)(2,1)S(1)} fusion(bf16[8,3712]{1,0:T(8,128)(2,1)} %get-tuple-element.26), kind=kLoop, calls=%fused_computation.114 | loop fusion | bytes 118784
  15.2 2.3 %collective-permute-start.6 = (bf16[16,3584]{1,0:T(8,128)(2,1)S(1)}, bf16[16,3584]{1,0:T(8,128)(2,1)S(1)}, u32[]{:S(2)}, u32[]{:S(2)}) collective-permute-start(bf16[16,3584]{1,0:T(8,128)(2,1)S(1)} %pad_maximum_fusion.9), channel_id=1, source_target_pairs={{0,1},{1,0},{2,3},{3,2},{4,5},{5,4},{6,7},{7,6},{8,9},{9,8},{10,11... | collective-permute-start | bytes 344072 | tf_op jit(solution)/shard_map/ppermute | solution.py:31
  17.5 0.8 %pad_maximum_fusion.7 = bf16[16,3712]{1,0:T(8,128)(2,1)S(1)} fusion(bf16[8,3712]{1,0:T(8,128)(2,1)S(1)} %collective-permute-done, bf16[8,3712]{1,0:T(8,128)(2,1)} %get-tuple-element.22), kind=kLoop, calls=%fused_computation.73 | loop fusion | flops 237568 | bytes 237568 | tf_op jit(solution)/shard_map/concatenate | solution.py:39
  18.4 0.8 %pad_maximum_fusion.10 = bf16[16,3584]{1,0:T(8,128)(2,1)S(1)} fusion(bf16[8,3584]{1,0:T(8,128)(2,1)S(1)} %collective-permute-done.16, bf16[8,3584]{1,0:T(8,128)(2,1)} %get-tuple-element.32), kind=kLoop, calls=%fused_computation.78 | loop fusion | flops 229376 | bytes 229376 | tf_op jit(solution)/shard_map/concatenate | solution.py:39
  19.3 2.0 %collective-permute-start.17 = (bf16[16,3584]{1,0:T(8,128)(2,1)S(1)}, bf16[16,3584]{1,0:T(8,128)(2,1)S(1)}, u32[]{:S(2)}, u32[]{:S(2)}) collective-permute-start(bf16[16,3584]{1,0:T(8,128)(2,1)S(1)} %pad_maximum_fusion.10), channel_id=1, source_target_pairs={{0,1},{1,0},{2,3},{3,2},{4,5},{5,4},{6,7},{7,6},{8,9},{9,8},{10,11... | collective-permute-start | bytes 344072 | tf_op jit(solution)/shard_map/ppermute | solution.py:31
  21.3 0.8 %pad_maximum_fusion.8 = bf16[16,3712]{1,0:T(8,128)(2,1)S(1)} fusion(bf16[8,3712]{1,0:T(8,128)(2,1)S(1)} %collective-permute-done.11, bf16[8,3712]{1,0:T(8,128)(2,1)} %get-tuple-element.26), kind=kLoop, calls=%fused_computation.74 | loop fusion | flops 237568 | bytes 237568 | tf_op jit(solution)/shard_map/concatenate | solution.py:39
  22.6 1.6 %collective-permute-start.7 = (bf16[24,3584]{1,0:T(8,128)(2,1)S(1)}, bf16[24,3584]{1,0:T(8,128)(2,1)S(1)}, u32[]{:S(2)}, u32[]{:S(2)}) collective-permute-start(bf16[24,3584]{1,0:T(8,128)(2,1)S(1)} %pad_maximum_fusion.5), channel_id=1, source_target_pairs={{0,8},{4,12},{8,0},{12,4},{1,9},{5,13},{9,1},{13,5},{2,10},{6,14},... | collective-permute-start | bytes 516104 | tf_op jit(solution)/shard_map/ppermute | solution.py:31
  24.6 1.6 %collective-permute-start.3 = (bf16[24,3712]{1,0:T(8,128)(2,1)S(1)}, bf16[24,3712]{1,0:T(8,128)(2,1)S(1)}, u32[]{:S(2)}, u32[]{:S(2)}) collective-permute-start(bf16[24,3712]{1,0:T(8,128)(2,1)S(1)} %pad_maximum_fusion.3), channel_id=1, source_target_pairs={{0,8},{4,12},{8,0},{12,4},{1,9},{5,13},{9,1},{13,5},{2,10},{6,14},... | collective-permute-start | bytes 534536 | tf_op jit(solution)/shard_map/ppermute | solution.py:31
  26.2 0.9 %collective-permute-done.17 = bf16[16,3584]{1,0:T(8,128)(2,1)S(1)} collective-permute-done((bf16[16,3584]{1,0:T(8,128)(2,1)S(1)}, bf16[16,3584]{1,0:T(8,128)(2,1)S(1)}, u32[]{:S(2)}, u32[]{:S(2)}) %collective-permute-start.17) | collective-permute-done | bytes 114720 | tf_op jit(solution)/shard_map/ppermute | solution.py:31
  27.1 1.4 %collective-permute-done.12 = bf16[16,3712]{1,0:T(8,128)(2,1)S(1)} collective-permute-done((bf16[16,3712]{1,0:T(8,128)(2,1)S(1)}, bf16[16,3712]{1,0:T(8,128)(2,1)S(1)}, u32[]{:S(2)}, u32[]{:S(2)}) %collective-permute-start.12) | collective-permute-done | bytes 118816 | tf_op jit(solution)/shard_map/ppermute | solution.py:31
  29.4 1.6 %collective-permute-start.18 = (bf16[24,3584]{1,0:T(8,128)(2,1)S(1)}, bf16[24,3584]{1,0:T(8,128)(2,1)S(1)}, u32[]{:S(2)}, u32[]{:S(2)}) collective-permute-start(bf16[24,3584]{1,0:T(8,128)(2,1)S(1)} %pad_maximum_fusion.6), channel_id=1, source_target_pairs={{0,8},{4,12},{8,0},{12,4},{1,9},{5,13},{9,1},{13,5},{2,10},{6,14},... | collective-permute-start | bytes 516104 | tf_op jit(solution)/shard_map/ppermute | solution.py:31
  31.7 2.8 %fusion.10 = f32[128,512]{1,0:T(8,128)S(1)} fusion(bf16[128,3584]{1,0:T(8,128)(2,1)S(1)} %constant_dynamic-update-slice_fusion.16, bf16[1,7168,512]{2,1,0:T(8,128)(2,1)} %param.12), kind=kOutput, calls=%fused_computation.14 | convolution fusion | flops 469762048 | bytes 4849664 | tf_op jit(solution)/shard_map/dot_general | solution.py:172
  37.8 1.0 %slice-done.5 = s8[3145728]{0:T(1024)(128)(4,1)S(1)} async-done(((s8[7340032]{0:T(1024)(128)(4,1)}), s8[3145728]{0:T(1024)(128)(4,1)S(1)}, s32[]{:S(2)}) %slice-start.5) | async-done | bytes 3145752
  43.0 1.6 %collective-permute-start.23 = (bf16[24,3584]{1,0:T(8,128)(2,1)S(1)}, bf16[24,3584]{1,0:T(8,128)(2,1)S(1)}, u32[]{:S(2)}, u32[]{:S(2)}) collective-permute-start(bf16[24,3584]{1,0:T(8,128)(2,1)S(1)} %slice.279), channel_id=1, source_target_pairs={{0,8},{4,12},{8,0},{12,4},{1,9},{5,13},{9,1},{13,5},{2,10},{6,14},... | collective-permute-start | bytes 516104 | tf_op jit(solution)/shard_map/ppermute | solution.py:31
  50.4 3.0 %collective-permute-done.10 = bf16[24,3584]{1,0:T(8,128)(2,1)S(1)} collective-permute-done((bf16[24,3584]{1,0:T(8,128)(2,1)S(1)}, bf16[24,3584]{1,0:T(8,128)(2,1)S(1)}, u32[]{:S(2)}, u32[]{:S(2)}) %collective-permute-start.10) | collective-permute-done | bytes 172064 | tf_op jit(solution)/shard_map/ppermute | solution.py:31
  53.9 1.6 %collective-permute-start.29 = (bf16[24,3584]{1,0:T(8,128)(2,1)S(1)}, bf16[24,3584]{1,0:T(8,128)(2,1)S(1)}, u32[]{:S(2)}, u32[]{:S(2)}) collective-permute-start(bf16[24,3584]{1,0:T(8,128)(2,1)S(1)} %slice.298), channel_id=1, source_target_pairs={{0,8},{4,12},{8,0},{12,4},{1,9},{5,13},{9,1},{13,5},{2,10},{6,14},... | collective-permute-start | bytes 516104 | tf_op jit(solution)/shard_map/ppermute | solution.py:31
  55.4 1.7 %collective-permute-start.22 = (bf16[16,3584]{1,0:T(8,128)(2,1)S(1)}, bf16[16,3584]{1,0:T(8,128)(2,1)S(1)}, u32[]{:S(2)}, u32[]{:S(2)}) collective-permute-start(bf16[16,3584]{1,0:T(8,128)(2,1)S(1)} %slice.265), channel_id=1, source_target_pairs={{0,1},{1,0},{2,3},{3,2},{4,5},{5,4},{6,7},{7,6},{8,9},{9,8},{10,11... | collective-permute-start | bytes 344072 | tf_op jit(solution)/shard_map/ppermute | solution.py:31
  58.0 1.6 %collective-permute-start.26 = (bf16[16,7168]{1,0:T(8,128)(2,1)S(1)}, bf16[16,7168]{1,0:T(8,128)(2,1)S(1)}, u32[]{:S(2)}, u32[]{:S(2)}) collective-permute-start(bf16[16,7168]{1,0:T(8,128)(2,1)S(1)} %maximum_maximum_fusion), channel_id=1, source_target_pairs={{0,8},{4,12},{8,0},{12,4},{1,9},{5,13},{9,1},{13,5},{2,10},{6,14},... | collective-permute-start | bytes 688136 | tf_op jit(solution)/shard_map/ppermute | solution.py:31
  59.6 1.6 %collective-permute-done.22 = bf16[16,3584]{1,0:T(8,128)(2,1)S(1)} collective-permute-done((bf16[16,3584]{1,0:T(8,128)(2,1)S(1)}, bf16[16,3584]{1,0:T(8,128)(2,1)S(1)}, u32[]{:S(2)}, u32[]{:S(2)}) %collective-permute-start.22) | collective-permute-done | bytes 114720 | tf_op jit(solution)/shard_map/ppermute | solution.py:31
  61.2 1.2 %collective-permute-done.24 = bf16[16,3584]{1,0:T(8,128)(2,1)S(1)} collective-permute-done((bf16[16,3584]{1,0:T(8,128)(2,1)S(1)}, bf16[16,3584]{1,0:T(8,128)(2,1)S(1)}, u32[]{:S(2)}, u32[]{:S(2)}) %collective-permute-start.24) | collective-permute-done | bytes 114720 | tf_op jit(solution)/shard_map/ppermute | solution.py:31
  62.5 2.7 %collective-permute-start.25 = (bf16[8,7168]{1,0:T(8,128)(2,1)S(1)}, bf16[8,7168]{1,0:T(8,128)(2,1)S(1)}, u32[]{:S(2)}, u32[]{:S(2)}) collective-permute-start(bf16[8,7168]{1,0:T(8,128)(2,1)S(1)} %pad_maximum_fusion.11), channel_id=1, source_target_pairs={{0,2},{1,3},{2,0},{3,1},{4,6},{5,7},{6,4},{7,5},{8,10},{9,11},{10,... | collective-permute-start | bytes 344072 | tf_op jit(solution)/shard_map/ppermute | solution.py:31
  65.2 1.6 %collective-permute-start.30 = (bf16[16,3584]{1,0:T(8,128)(2,1)S(1)}, bf16[16,3584]{1,0:T(8,128)(2,1)S(1)}, u32[]{:S(2)}, u32[]{:S(2)}) collective-permute-start(bf16[16,3584]{1,0:T(8,128)(2,1)S(1)} %slice.299), channel_id=1, source_target_pairs={{0,1},{1,0},{2,3},{3,2},{4,5},{5,4},{6,7},{7,6},{8,9},{9,8},{10,11... | collective-permute-start | bytes 344072 | tf_op jit(solution)/shard_map/ppermute | solution.py:31
  67.5 3.9 %collective-permute-done.30 = bf16[16,3584]{1,0:T(8,128)(2,1)S(1)} collective-permute-done((bf16[16,3584]{1,0:T(8,128)(2,1)S(1)}, bf16[16,3584]{1,0:T(8,128)(2,1)S(1)}, u32[]{:S(2)}, u32[]{:S(2)}) %collective-permute-start.30) | collective-permute-done | bytes 114720 | tf_op jit(solution)/shard_map/ppermute | solution.py:31
  72.9 1.6 %collective-permute-start.31 = (bf16[8,3584]{1,0:T(8,128)(2,1)S(1)}, bf16[8,3584]{1,0:T(8,128)(2,1)S(1)}, u32[]{:S(2)}, u32[]{:S(2)}) collective-permute-start(bf16[8,3584]{1,0:T(8,128)(2,1)S(1)} %get-tuple-element.61), channel_id=1, source_target_pairs={{0,2},{1,3},{2,0},{3,1},{4,6},{5,7},{6,4},{7,5},{8,10},{9,11},{10,... | collective-permute-start | bytes 172040 | tf_op jit(solution)/shard_map/ppermute | solution.py:31
  74.5 2.9 %collective-permute-done.32 = bf16[8,3584]{1,0:T(8,128)(2,1)S(1)} collective-permute-done((bf16[8,3584]{1,0:T(8,128)(2,1)S(1)}, bf16[8,3584]{1,0:T(8,128)(2,1)S(1)}, u32[]{:S(2)}, u32[]{:S(2)}) %collective-permute-start.32) | collective-permute-done | bytes 57376 | tf_op jit(solution)/shard_map/ppermute | solution.py:31
  (138 shorter events, 21.8 us)
Async XLA Ops:
  2.0 7.6 %collective-permute-start.5 = (bf16[8,3584]{1,0:T(8,128)(2,1)}, bf16[8,3584]{1,0:T(8,128)(2,1)S(1)}, u32[]{:S(2)}, u32[]{:S(2)}) collective-permute-start(bf16[8,3584]{1,0:T(8,128)(2,1)} %get-tuple-element.24), channel_id=1, source_target_pairs={{0,2},{1,3},{2,0},{3,1},{4,6},{5,7},{6,4},{7,5},{8,10},{9,11},{10,... | collective-permute-start | bytes 172040 | tf_op jit(solution)/shard_map/ppermute | solution.py:31
  6.1 11.4 %collective-permute-start = (bf16[8,3712]{1,0:T(8,128)(2,1)}, bf16[8,3712]{1,0:T(8,128)(2,1)S(1)}, u32[]{:S(2)}, u32[]{:S(2)}) collective-permute-start(bf16[8,3712]{1,0:T(8,128)(2,1)} %get-tuple-element.22), channel_id=1, source_target_pairs={{0,2},{1,3},{2,0},{3,1},{4,6},{5,7},{6,4},{7,5},{8,10},{9,11},{10,... | collective-permute-start | bytes 178184 | tf_op jit(solution)/shard_map/ppermute | solution.py:31
  6.2 20.8 %collective-permute-start.2 = (bf16[16,7296]{1,0:T(8,128)(2,1)}, bf16[16,7296]{1,0:T(8,128)(2,1)S(1)}, u32[]{:S(2)}, u32[]{:S(2)}) collective-permute-start(bf16[16,7296]{1,0:T(8,128)(2,1)} %get-tuple-element.23), channel_id=1, source_target_pairs={{0,8},{4,12},{8,0},{12,4},{1,9},{5,13},{9,1},{13,5},{2,10},{6,14},... | collective-permute-start | bytes 700424 | tf_op jit(solution)/shard_map/ppermute | solution.py:31
  9.6 8.8 %collective-permute-start.16 = (bf16[8,3584]{1,0:T(8,128)(2,1)}, bf16[8,3584]{1,0:T(8,128)(2,1)S(1)}, u32[]{:S(2)}, u32[]{:S(2)}) collective-permute-start(bf16[8,3584]{1,0:T(8,128)(2,1)} %get-tuple-element.32), channel_id=1, source_target_pairs={{0,2},{1,3},{2,0},{3,1},{4,6},{5,7},{6,4},{7,5},{8,10},{9,11},{10,... | collective-permute-start | bytes 172040 | tf_op jit(solution)/shard_map/ppermute | solution.py:31
  13.1 8.1 %collective-permute-start.11 = (bf16[8,3712]{1,0:T(8,128)(2,1)}, bf16[8,3712]{1,0:T(8,128)(2,1)S(1)}, u32[]{:S(2)}, u32[]{:S(2)}) collective-permute-start(bf16[8,3712]{1,0:T(8,128)(2,1)} %get-tuple-element.26), channel_id=1, source_target_pairs={{0,2},{1,3},{2,0},{3,1},{4,6},{5,7},{6,4},{7,5},{8,10},{9,11},{10,... | collective-permute-start | bytes 178184 | tf_op jit(solution)/shard_map/ppermute | solution.py:31
  15.2 7.4 %collective-permute-start.6 = (bf16[16,3584]{1,0:T(8,128)(2,1)S(1)}, bf16[16,3584]{1,0:T(8,128)(2,1)S(1)}, u32[]{:S(2)}, u32[]{:S(2)}) collective-permute-start(bf16[16,3584]{1,0:T(8,128)(2,1)S(1)} %pad_maximum_fusion.9), channel_id=1, source_target_pairs={{0,1},{1,0},{2,3},{3,2},{4,5},{5,4},{6,7},{7,6},{8,9},{9,8},{10,11... | collective-permute-start | bytes 344072 | tf_op jit(solution)/shard_map/ppermute | solution.py:31
  18.3 6.2 %collective-permute-start.1 = (bf16[16,3712]{1,0:T(8,128)(2,1)S(1)}, bf16[16,3712]{1,0:T(8,128)(2,1)S(1)}, u32[]{:S(2)}, u32[]{:S(2)}) collective-permute-start(bf16[16,3712]{1,0:T(8,128)(2,1)S(1)} %pad_maximum_fusion.7), channel_id=1, source_target_pairs={{0,1},{1,0},{2,3},{3,2},{4,5},{5,4},{6,7},{7,6},{8,9},{9,8},{10,11... | collective-permute-start | bytes 356360 | tf_op jit(solution)/shard_map/ppermute | solution.py:31
  19.3 7.8 %collective-permute-start.17 = (bf16[16,3584]{1,0:T(8,128)(2,1)S(1)}, bf16[16,3584]{1,0:T(8,128)(2,1)S(1)}, u32[]{:S(2)}, u32[]{:S(2)}) collective-permute-start(bf16[16,3584]{1,0:T(8,128)(2,1)S(1)} %pad_maximum_fusion.10), channel_id=1, source_target_pairs={{0,1},{1,0},{2,3},{3,2},{4,5},{5,4},{6,7},{7,6},{8,9},{9,8},{10,11... | collective-permute-start | bytes 344072 | tf_op jit(solution)/shard_map/ppermute | solution.py:31
  22.1 6.3 %collective-permute-start.12 = (bf16[16,3712]{1,0:T(8,128)(2,1)S(1)}, bf16[16,3712]{1,0:T(8,128)(2,1)S(1)}, u32[]{:S(2)}, u32[]{:S(2)}) collective-permute-start(bf16[16,3712]{1,0:T(8,128)(2,1)S(1)} %pad_maximum_fusion.8), channel_id=1, source_target_pairs={{0,1},{1,0},{2,3},{3,2},{4,5},{5,4},{6,7},{7,6},{8,9},{9,8},{10,11... | collective-permute-start | bytes 356360 | tf_op jit(solution)/shard_map/ppermute | solution.py:31
  22.6 6.7 %collective-permute-start.7 = (bf16[24,3584]{1,0:T(8,128)(2,1)S(1)}, bf16[24,3584]{1,0:T(8,128)(2,1)S(1)}, u32[]{:S(2)}, u32[]{:S(2)}) collective-permute-start(bf16[24,3584]{1,0:T(8,128)(2,1)S(1)} %pad_maximum_fusion.5), channel_id=1, source_target_pairs={{0,8},{4,12},{8,0},{12,4},{1,9},{5,13},{9,1},{13,5},{2,10},{6,14},... | collective-permute-start | bytes 516104 | tf_op jit(solution)/shard_map/ppermute | solution.py:31
  24.6 7.0 %collective-permute-start.3 = (bf16[24,3712]{1,0:T(8,128)(2,1)S(1)}, bf16[24,3712]{1,0:T(8,128)(2,1)S(1)}, u32[]{:S(2)}, u32[]{:S(2)}) collective-permute-start(bf16[24,3712]{1,0:T(8,128)(2,1)S(1)} %pad_maximum_fusion.3), channel_id=1, source_target_pairs={{0,8},{4,12},{8,0},{12,4},{1,9},{5,13},{9,1},{13,5},{2,10},{6,14},... | collective-permute-start | bytes 534536 | tf_op jit(solution)/shard_map/ppermute | solution.py:31
  29.3 2.3 %collective-permute-start.8 = (bf16[64,3584]{1,0:T(8,128)(2,1)S(1)}, bf16[64,3584]{1,0:T(8,128)(2,1)S(1)}, u32[]{:S(2)}, u32[]{:S(2)}) collective-permute-start(bf16[64,3584]{1,0:T(8,128)(2,1)S(1)} %get-tuple-element.53), channel_id=1, source_target_pairs={{0,4},{4,0},{8,12},{12,8},{1,5},{5,1},{9,13},{13,9},{2,6},{6,2},{1... | collective-permute-start | bytes 1376264 | tf_op jit(solution)/shard_map/ppermute | solution.py:31
  29.4 11.3 %collective-permute-start.18 = (bf16[24,3584]{1,0:T(8,128)(2,1)S(1)}, bf16[24,3584]{1,0:T(8,128)(2,1)S(1)}, u32[]{:S(2)}, u32[]{:S(2)}) collective-permute-start(bf16[24,3584]{1,0:T(8,128)(2,1)S(1)} %pad_maximum_fusion.6), channel_id=1, source_target_pairs={{0,8},{4,12},{8,0},{12,4},{1,9},{5,13},{9,1},{13,5},{2,10},{6,14},... | collective-permute-start | bytes 516104 | tf_op jit(solution)/shard_map/ppermute | solution.py:31
  31.0 9.8 %collective-permute-start.13 = (bf16[24,3712]{1,0:T(8,128)(2,1)S(1)}, bf16[24,3712]{1,0:T(8,128)(2,1)S(1)}, u32[]{:S(2)}, u32[]{:S(2)}) collective-permute-start(bf16[24,3712]{1,0:T(8,128)(2,1)S(1)} %pad_maximum_fusion.4), channel_id=1, source_target_pairs={{0,8},{4,12},{8,0},{12,4},{1,9},{5,13},{9,1},{13,5},{2,10},{6,14},... | collective-permute-start | bytes 534536 | tf_op jit(solution)/shard_map/ppermute | solution.py:31
  31.6 3.7 %collective-permute-start.4 = (bf16[64,3712]{1,0:T(8,128)(2,1)S(1)}, bf16[64,3712]{1,0:T(8,128)(2,1)S(1)}, u32[]{:S(2)}, u32[]{:S(2)}) collective-permute-start(bf16[64,3712]{1,0:T(8,128)(2,1)S(1)} %get-tuple-element.51), channel_id=1, source_target_pairs={{0,4},{4,0},{8,12},{12,8},{1,5},{5,1},{9,13},{13,9},{2,6},{6,2},{1... | collective-permute-start | bytes 1425416 | tf_op jit(solution)/shard_map/ppermute | solution.py:31
  40.8 2.0 %collective-permute-start.9 = (bf16[64,3584]{1,0:T(8,128)(2,1)S(1)}, bf16[64,3584]{1,0:T(8,128)(2,1)S(1)}, u32[]{:S(2)}, u32[]{:S(2)}) collective-permute-start(bf16[64,3584]{1,0:T(8,128)(2,1)S(1)} %slice.261), channel_id=1, source_target_pairs={{0,4},{4,0},{8,12},{12,8},{1,5},{5,1},{9,13},{13,9},{2,6},{6,2},{1... | collective-permute-start | bytes 1376264 | tf_op jit(solution)/shard_map/ppermute | solution.py:31
  40.9 4.2 %collective-permute-start.19 = (bf16[64,3584]{1,0:T(8,128)(2,1)S(1)}, bf16[64,3584]{1,0:T(8,128)(2,1)S(1)}, u32[]{:S(2)}, u32[]{:S(2)}) collective-permute-start(bf16[64,3584]{1,0:T(8,128)(2,1)S(1)} %constant_dynamic-update-slice_fusion.27), channel_id=1, source_target_pairs={{0,4},{4,0},{8,12},{12,8},{1,5},{5,1},{9,13},{13,9},{2,6},{6,2},{1... | collective-permute-start | bytes 1376264 | tf_op jit(solution)/shard_map/ppermute | solution.py:31
  41.4 5.1 %collective-permute-start.14 = (bf16[64,3712]{1,0:T(8,128)(2,1)S(1)}, bf16[64,3712]{1,0:T(8,128)(2,1)S(1)}, u32[]{:S(2)}, u32[]{:S(2)}) collective-permute-start(bf16[64,3712]{1,0:T(8,128)(2,1)S(1)} %constant_dynamic-update-slice_fusion.22), channel_id=1, source_target_pairs={{0,4},{4,0},{8,12},{12,8},{1,5},{5,1},{9,13},{13,9},{2,6},{6,2},{1... | collective-permute-start | bytes 1425416 | tf_op jit(solution)/shard_map/ppermute | solution.py:31
  43.0 7.3 %collective-permute-start.23 = (bf16[24,3584]{1,0:T(8,128)(2,1)S(1)}, bf16[24,3584]{1,0:T(8,128)(2,1)S(1)}, u32[]{:S(2)}, u32[]{:S(2)}) collective-permute-start(bf16[24,3584]{1,0:T(8,128)(2,1)S(1)} %slice.279), channel_id=1, source_target_pairs={{0,8},{4,12},{8,0},{12,4},{1,9},{5,13},{9,1},{13,5},{2,10},{6,14},... | collective-permute-start | bytes 516104 | tf_op jit(solution)/shard_map/ppermute | solution.py:31
  44.6 8.8 %collective-permute-start.10 = (bf16[24,3584]{1,0:T(8,128)(2,1)S(1)}, bf16[24,3584]{1,0:T(8,128)(2,1)S(1)}, u32[]{:S(2)}, u32[]{:S(2)}) collective-permute-start(bf16[24,3584]{1,0:T(8,128)(2,1)S(1)} %slice.264), channel_id=1, source_target_pairs={{0,8},{4,12},{8,0},{12,4},{1,9},{5,13},{9,1},{13,5},{2,10},{6,14},... | collective-permute-start | bytes 516104 | tf_op jit(solution)/shard_map/ppermute | solution.py:31
  49.5 4.0 %collective-permute-start.21 = (bf16[64,3584]{1,0:T(8,128)(2,1)S(1)}, bf16[64,3584]{1,0:T(8,128)(2,1)S(1)}, u32[]{:S(2)}, u32[]{:S(2)}) collective-permute-start(bf16[64,3584]{1,0:T(8,128)(2,1)S(1)} %slice.275), channel_id=1, source_target_pairs={{0,4},{4,0},{8,12},{12,8},{1,5},{5,1},{9,13},{13,9},{2,6},{6,2},{1... | collective-permute-start | bytes 1376264 | tf_op jit(solution)/shard_map/ppermute | solution.py:31
  49.6 4.0 %collective-permute-start.20 = (bf16[64,3584]{1,0:T(8,128)(2,1)S(1)}, bf16[64,3584]{1,0:T(8,128)(2,1)S(1)}, u32[]{:S(2)}, u32[]{:S(2)}) collective-permute-start(bf16[64,3584]{1,0:T(8,128)(2,1)S(1)} %slice.273), channel_id=1, source_target_pairs={{0,4},{4,0},{8,12},{12,8},{1,5},{5,1},{9,13},{13,9},{2,6},{6,2},{1... | collective-permute-start | bytes 1376264 | tf_op jit(solution)/shard_map/ppermute | solution.py:31
  53.9 11.3 %collective-permute-start.29 = (bf16[24,3584]{1,0:T(8,128)(2,1)S(1)}, bf16[24,3584]{1,0:T(8,128)(2,1)S(1)}, u32[]{:S(2)}, u32[]{:S(2)}) collective-permute-start(bf16[24,3584]{1,0:T(8,128)(2,1)S(1)} %slice.298), channel_id=1, source_target_pairs={{0,8},{4,12},{8,0},{12,4},{1,9},{5,13},{9,1},{13,5},{2,10},{6,14},... | collective-permute-start | bytes 516104 | tf_op jit(solution)/shard_map/ppermute | solution.py:31
  55.4 5.8 %collective-permute-start.22 = (bf16[16,3584]{1,0:T(8,128)(2,1)S(1)}, bf16[16,3584]{1,0:T(8,128)(2,1)S(1)}, u32[]{:S(2)}, u32[]{:S(2)}) collective-permute-start(bf16[16,3584]{1,0:T(8,128)(2,1)S(1)} %slice.265), channel_id=1, source_target_pairs={{0,1},{1,0},{2,3},{3,2},{4,5},{5,4},{6,7},{7,6},{8,9},{9,8},{10,11... | collective-permute-start | bytes 344072 | tf_op jit(solution)/shard_map/ppermute | solution.py:31
  57.1 5.3 %collective-permute-start.24 = (bf16[16,3584]{1,0:T(8,128)(2,1)S(1)}, bf16[16,3584]{1,0:T(8,128)(2,1)S(1)}, u32[]{:S(2)}, u32[]{:S(2)}) collective-permute-start(bf16[16,3584]{1,0:T(8,128)(2,1)S(1)} %slice.280), channel_id=1, source_target_pairs={{0,1},{1,0},{2,3},{3,2},{4,5},{5,4},{6,7},{7,6},{8,9},{9,8},{10,11... | collective-permute-start | bytes 344072 | tf_op jit(solution)/shard_map/ppermute | solution.py:31
  57.5 9.4 %collective-permute-start.27 = (bf16[24,3584]{1,0:T(8,128)(2,1)S(1)}, bf16[24,3584]{1,0:T(8,128)(2,1)S(1)}, u32[]{:S(2)}, u32[]{:S(2)}) collective-permute-start(bf16[24,3584]{1,0:T(8,128)(2,1)S(1)} %slice.293), channel_id=1, source_target_pairs={{0,8},{4,12},{8,0},{12,4},{1,9},{5,13},{9,1},{13,5},{2,10},{6,14},... | collective-permute-start | bytes 516104 | tf_op jit(solution)/shard_map/ppermute | solution.py:31
  58.0 16.5 %collective-permute-start.26 = (bf16[16,7168]{1,0:T(8,128)(2,1)S(1)}, bf16[16,7168]{1,0:T(8,128)(2,1)S(1)}, u32[]{:S(2)}, u32[]{:S(2)}) collective-permute-start(bf16[16,7168]{1,0:T(8,128)(2,1)S(1)} %maximum_maximum_fusion), channel_id=1, source_target_pairs={{0,8},{4,12},{8,0},{12,4},{1,9},{5,13},{9,1},{13,5},{2,10},{6,14},... | collective-permute-start | bytes 688136 | tf_op jit(solution)/shard_map/ppermute | solution.py:31
  62.5 12.1 %collective-permute-start.25 = (bf16[8,7168]{1,0:T(8,128)(2,1)S(1)}, bf16[8,7168]{1,0:T(8,128)(2,1)S(1)}, u32[]{:S(2)}, u32[]{:S(2)}) collective-permute-start(bf16[8,7168]{1,0:T(8,128)(2,1)S(1)} %pad_maximum_fusion.11), channel_id=1, source_target_pairs={{0,2},{1,3},{2,0},{3,1},{4,6},{5,7},{6,4},{7,5},{8,10},{9,11},{10,... | collective-permute-start | bytes 344072 | tf_op jit(solution)/shard_map/ppermute | solution.py:31
  65.2 6.1 %collective-permute-start.30 = (bf16[16,3584]{1,0:T(8,128)(2,1)S(1)}, bf16[16,3584]{1,0:T(8,128)(2,1)S(1)}, u32[]{:S(2)}, u32[]{:S(2)}) collective-permute-start(bf16[16,3584]{1,0:T(8,128)(2,1)S(1)} %slice.299), channel_id=1, source_target_pairs={{0,1},{1,0},{2,3},{3,2},{4,5},{5,4},{6,7},{7,6},{8,9},{9,8},{10,11... | collective-permute-start | bytes 344072 | tf_op jit(solution)/shard_map/ppermute | solution.py:31
  66.9 6.0 %collective-permute-start.28 = (bf16[16,3584]{1,0:T(8,128)(2,1)S(1)}, bf16[16,3584]{1,0:T(8,128)(2,1)S(1)}, u32[]{:S(2)}, u32[]{:S(2)}) collective-permute-start(bf16[16,3584]{1,0:T(8,128)(2,1)S(1)} %slice.294), channel_id=1, source_target_pairs={{0,1},{1,0},{2,3},{3,2},{4,5},{5,4},{6,7},{7,6},{8,9},{9,8},{10,11... | collective-permute-start | bytes 344072 | tf_op jit(solution)/shard_map/ppermute | solution.py:31
  71.4 6.0 %collective-permute-start.32 = (bf16[8,3584]{1,0:T(8,128)(2,1)S(1)}, bf16[8,3584]{1,0:T(8,128)(2,1)S(1)}, u32[]{:S(2)}, u32[]{:S(2)}) collective-permute-start(bf16[8,3584]{1,0:T(8,128)(2,1)S(1)} %get-tuple-element.63), channel_id=1, source_target_pairs={{0,2},{1,3},{2,0},{3,1},{4,6},{5,7},{6,4},{7,5},{8,10},{9,11},{10,... | collective-permute-start | bytes 172040 | tf_op jit(solution)/shard_map/ppermute | solution.py:31
  72.9 5.1 %collective-permute-start.31 = (bf16[8,3584]{1,0:T(8,128)(2,1)S(1)}, bf16[8,3584]{1,0:T(8,128)(2,1)S(1)}, u32[]{:S(2)}, u32[]{:S(2)}) collective-permute-start(bf16[8,3584]{1,0:T(8,128)(2,1)S(1)} %get-tuple-element.61), channel_id=1, source_target_pairs={{0,2},{1,3},{2,0},{3,1},{4,6},{5,7},{6,4},{7,5},{8,10},{9,11},{10,... | collective-permute-start | bytes 172040 | tf_op jit(solution)/shard_map/ppermute | solution.py:31
  (12 other events, 68.5 us)

commit v6 on v5

--- a/solution.py
+++ b/solution.py
@@ -9,7 +9,7 @@
 
 routed_scale = 2.5
 column_parts = 2
-F_Z2 = 2
+F_Z2 = 0
 F_XORD = 2
 F_C1 = 1
 F_Z2R = 2

time: 79.4 us -> 79.8 us (level)
  local copies, waits for them, and re-layouts: 5.88 us -> 8.22 us
  starting transfers between devices: 36 us -> 33.9 us
    ppermute x33, starting transfers between devices: 36 us -> 33.9 us  [swap(): return lax.ppermute(value, axis_name, [(i, i ^ bit) for i in range(count)])]
    concatenate x6, local copies, waits for them, and re-layouts: 0.16 us -> 1.61 us  [join(): return jnp.concatenate(parts, axis=0)]
    unnamed x32, local copies, waits for them, and re-layouts: 5.49 us -> 6.37 us
  transfers between devices with their start and end apart: 33 -> 33, of which waited for: 14 -> 14; matrix products, arithmetic and copies ran while one was open for 23% -> 26% of each run, Pallas kernels for 0% -> 0%
where the time goes in v6:
time: 79.8 us; the launch traced here: 79.4 us
  starting transfers between devices  33.9 us (42%)
  waiting for transfers between devices  18.9 us (24%)
  matrix products  10.3 us (13%)
  local copies, waits for them, and re-layouts  8.22 us (10%)
  other arithmetic  5.51 us (7%)
  Pallas kernels  2.03 us (3%)
    ppermute x33, starting transfers between devices, swap(): return lax.ppermute(value, axis_name, [(i, i ^ bit) for i in range(count)])  33.9 us
    ppermute x33, waiting for transfers between devices, swap(): return lax.ppermute(value, axis_name, [(i, i ^ bit) for i in range(count)])  18.9 us
    unnamed x32, local copies, waits for them, and re-layouts  6.37 us
    dot_general x4, matrix products, body(): up_value += jnp.dot(part, w_up[0, span], preferred_element_type=jnp.float32)  5.04 us
    concatenate x11, other arithmetic, join(): return jnp.concatenate(parts, axis=0)  3.54 us
    dot_general x4, matrix products, body(): jnp.dot(hidden, w_down[0, :, start:end], preferred_element_type=jnp.float32)  2.67 us
    dot_general x4, matrix products, body(): jnp.dot(part, w_gate[0, span], preferred_element_type=jnp.float32)  2.56 us
    pallas_call x1, Pallas kernels, prepare(): pl.pallas_call(functools.partial(prepare_kernel, ep_count, extra, cuts),...  2.03 us
  transfers between devices with their start and end apart: 33, of which 14 were waited for; matrix products, arithmetic and copies ran while one was open for 26% of the time, Pallas kernels for 0%

profile of v6, /device:TPU:0, one launch (start us, length us, event | category | flops | bytes accessed | tf_op | source)
XLA Modules:
  0.0 79.4 jit_solution(8697314456639777737)
XLA Ops:
  0.0 2.0 %shard_map.73 = (bf16[16,7296]{1,0:T(8,128)(2,1)}, bf16[8,3712]{1,0:T(8,128)(2,1)}, bf16[8,3584]{1,0:T(8,128)(2,1)}, bf16[8,3712]{1,0:T(8,128)(2,1)}, bf16[8,3584]{1,0:T(8,128)(2,1)}) custom-call(bf16[2,8,7168]{2,1,0:T(8,128)(2,1)} %codes_hbm.1, f32[2,8,56]{2,1,0:T(8,128)} %scales_hbm.1, s32[2,2,8]{2,1,0:T(2,128)} %bitcast.58, s32[2,2,8]{2,1,0:T(2,128)} %bitcast.59), custom_call_target="tpu_custom_call" | custom-call | tf_op jit(solution)/shard_map/pallas_call | solution.py:106
  2.0 4.1 %collective-permute-start.5 = (bf16[8,3584]{1,0:T(8,128)(2,1)}, bf16[8,3584]{1,0:T(8,128)(2,1)S(1)}, u32[]{:S(2)}, u32[]{:S(2)}) collective-permute-start(bf16[8,3584]{1,0:T(8,128)(2,1)} %get-tuple-element.22), channel_id=1, source_target_pairs={{0,2},{1,3},{2,0},{3,1},{4,6},{5,7},{6,4},{7,5},{8,10},{9,11},{10,... | collective-permute-start | bytes 172040 | tf_op jit(solution)/shard_map/ppermute | solution.py:31
  6.2 2.8 %collective-permute-start = (bf16[8,3712]{1,0:T(8,128)(2,1)}, bf16[8,3712]{1,0:T(8,128)(2,1)S(1)}, u32[]{:S(2)}, u32[]{:S(2)}) collective-permute-start(bf16[8,3712]{1,0:T(8,128)(2,1)} %get-tuple-element.20), channel_id=1, source_target_pairs={{0,2},{1,3},{2,0},{3,1},{4,6},{5,7},{6,4},{7,5},{8,10},{9,11},{10,... | collective-permute-start | bytes 178184 | tf_op jit(solution)/shard_map/ppermute | solution.py:31
  9.1 1.7 %collective-permute-start.2 = (bf16[16,7296]{1,0:T(8,128)(2,1)}, bf16[16,7296]{1,0:T(8,128)(2,1)S(1)}, u32[]{:S(2)}, u32[]{:S(2)}) collective-permute-start(bf16[16,7296]{1,0:T(8,128)(2,1)} %get-tuple-element.21), channel_id=1, source_target_pairs={{0,8},{4,12},{8,0},{12,4},{1,9},{5,13},{9,1},{13,5},{2,10},{6,14},... | collective-permute-start | bytes 700424 | tf_op jit(solution)/shard_map/ppermute | solution.py:31
  10.9 1.5 %constant_dynamic-update-slice_fusion.15 = (bf16[64,3584]{1,0:T(8,128)(2,1)S(1)}, bf16[128,3584]{1,0:T(8,128)(2,1)}, bf16[64,3584]{1,0:T(8,128)(2,1)S(1)}) fusion(bf16[8,3584]{1,0:T(8,128)(2,1)} %get-tuple-element.22, bf16[8,3584]{1,0:T(8,128)(2,1)} %get-tuple-element.28), kind=kLoop, calls=%fused_computation.103 | loop fusion | bytes 286720
  12.4 0.9 %constant_dynamic-update-slice_fusion.4 = (bf16[64,3712]{1,0:T(8,128)(2,1)S(1)}, bf16[128,3712]{1,0:T(8,128)(2,1)S(1)}, bf16[64,3712]{1,0:T(8,128)(2,1)S(1)}) fusion(bf16[8,3712]{1,0:T(8,128)(2,1)} %get-tuple-element.20, bf16[8,3712]{1,0:T(8,128)(2,1)} %get-tuple-element.23), kind=kLoop, calls=%fused_computation.92 | loop fusion | bytes 296960
  13.3 0.8 %pad_maximum_fusion.9 = bf16[16,3584]{1,0:T(8,128)(2,1)S(1)} fusion(bf16[8,3584]{1,0:T(8,128)(2,1)S(1)} %collective-permute-done.5, bf16[8,3584]{1,0:T(8,128)(2,1)} %get-tuple-element.22), kind=kLoop, calls=%fused_computation.77 | loop fusion | flops 229376 | bytes 229376 | tf_op jit(solution)/shard_map/concatenate | solution.py:39
  14.1 1.6 %collective-permute-start.6 = (bf16[16,3584]{1,0:T(8,128)(2,1)S(1)}, bf16[16,3584]{1,0:T(8,128)(2,1)S(1)}, u32[]{:S(2)}, u32[]{:S(2)}) collective-permute-start(bf16[16,3584]{1,0:T(8,128)(2,1)S(1)} %pad_maximum_fusion.9), channel_id=1, source_target_pairs={{0,1},{1,0},{2,3},{3,2},{4,5},{5,4},{6,7},{7,6},{8,9},{9,8},{10,11... | collective-permute-start | bytes 344072 | tf_op jit(solution)/shard_map/ppermute | solution.py:31
  17.6 0.8 %pad_maximum_fusion.7 = bf16[16,3712]{1,0:T(8,128)(2,1)S(1)} fusion(bf16[8,3712]{1,0:T(8,128)(2,1)S(1)} %collective-permute-done, bf16[8,3712]{1,0:T(8,128)(2,1)} %get-tuple-element.20), kind=kLoop, calls=%fused_computation.73 | loop fusion | flops 237568 | bytes 237568 | tf_op jit(solution)/shard_map/concatenate | solution.py:39
  18.4 1.6 %collective-permute-start.1 = (bf16[16,3712]{1,0:T(8,128)(2,1)S(1)}, bf16[16,3712]{1,0:T(8,128)(2,1)S(1)}, u32[]{:S(2)}, u32[]{:S(2)}) collective-permute-start(bf16[16,3712]{1,0:T(8,128)(2,1)S(1)} %pad_maximum_fusion.7), channel_id=1, source_target_pairs={{0,1},{1,0},{2,3},{3,2},{4,5},{5,4},{6,7},{7,6},{8,9},{9,8},{10,11... | collective-permute-start | bytes 356360 | tf_op jit(solution)/shard_map/ppermute | solution.py:31
  20.1 0.8 %pad_maximum_fusion.8 = bf16[16,3712]{1,0:T(8,128)(2,1)S(1)} fusion(bf16[8,3712]{1,0:T(8,128)(2,1)S(1)} %collective-permute-done.11, bf16[8,3712]{1,0:T(8,128)(2,1)} %get-tuple-element.23), kind=kLoop, calls=%fused_computation.74 | loop fusion | flops 237568 | bytes 237568 | tf_op jit(solution)/shard_map/concatenate | solution.py:39
  21.5 1.0 %collective-permute-start.7 = (bf16[24,3584]{1,0:T(8,128)(2,1)S(1)}, bf16[24,3584]{1,0:T(8,128)(2,1)S(1)}, u32[]{:S(2)}, u32[]{:S(2)}) collective-permute-start(bf16[24,3584]{1,0:T(8,128)(2,1)S(1)} %pad_maximum_fusion.5), channel_id=1, source_target_pairs={{0,8},{4,12},{8,0},{12,4},{1,9},{5,13},{9,1},{13,5},{2,10},{6,14},... | collective-permute-start | bytes 516104 | tf_op jit(solution)/shard_map/ppermute | solution.py:31
  23.2 1.9 %collective-permute-done.1 = bf16[16,3712]{1,0:T(8,128)(2,1)S(1)} collective-permute-done((bf16[16,3712]{1,0:T(8,128)(2,1)S(1)}, bf16[16,3712]{1,0:T(8,128)(2,1)S(1)}, u32[]{:S(2)}, u32[]{:S(2)}) %collective-permute-start.1) | collective-permute-done | bytes 118816 | tf_op jit(solution)/shard_map/ppermute | solution.py:31
  25.1 1.5 %collective-permute-start.3 = (bf16[24,3712]{1,0:T(8,128)(2,1)S(1)}, bf16[24,3712]{1,0:T(8,128)(2,1)S(1)}, u32[]{:S(2)}, u32[]{:S(2)}) collective-permute-start(bf16[24,3712]{1,0:T(8,128)(2,1)S(1)} %pad_maximum_fusion.3), channel_id=1, source_target_pairs={{0,8},{4,12},{8,0},{12,4},{1,9},{5,13},{9,1},{13,5},{2,10},{6,14},... | collective-permute-start | bytes 534536 | tf_op jit(solution)/shard_map/ppermute | solution.py:31
  28.8 1.7 %collective-permute-start.18 = (bf16[24,3584]{1,0:T(8,128)(2,1)S(1)}, bf16[24,3584]{1,0:T(8,128)(2,1)S(1)}, u32[]{:S(2)}, u32[]{:S(2)}) collective-permute-start(bf16[24,3584]{1,0:T(8,128)(2,1)S(1)} %pad_maximum_fusion.6), channel_id=1, source_target_pairs={{0,8},{4,12},{8,0},{12,4},{1,9},{5,13},{9,1},{13,5},{2,10},{6,14},... | collective-permute-start | bytes 516104 | tf_op jit(solution)/shard_map/ppermute | solution.py:31
  32.2 3.1 %fusion.10 = f32[128,512]{1,0:T(8,128)S(1)} fusion(bf16[128,3584]{1,0:T(8,128)(2,1)} %constant_dynamic-update-slice_fusion.16, bf16[1,7168,512]{2,1,0:T(8,128)(2,1)} %param.12), kind=kOutput, calls=%fused_computation.14 | convolution fusion | flops 469762048 | bytes 4849664 | tf_op jit(solution)/shard_map/dot_general | solution.py:172
  38.5 1.0 %slice-done.5 = s8[3145728]{0:T(1024)(128)(4,1)S(1)} async-done(((s8[7340032]{0:T(1024)(128)(4,1)}), s8[3145728]{0:T(1024)(128)(4,1)S(1)}, s32[]{:S(2)}) %slice-start.5) | async-done | bytes 3145752
  43.8 1.8 %collective-permute-start.23 = (bf16[24,3584]{1,0:T(8,128)(2,1)S(1)}, bf16[24,3584]{1,0:T(8,128)(2,1)S(1)}, u32[]{:S(2)}, u32[]{:S(2)}) collective-permute-start(bf16[24,3584]{1,0:T(8,128)(2,1)S(1)} %slice.279), channel_id=1, source_target_pairs={{0,8},{4,12},{8,0},{12,4},{1,9},{5,13},{9,1},{13,5},{2,10},{6,14},... | collective-permute-start | bytes 516104 | tf_op jit(solution)/shard_map/ppermute | solution.py:31
  51.1 3.1 %collective-permute-done.10 = bf16[24,3584]{1,0:T(8,128)(2,1)S(1)} collective-permute-done((bf16[24,3584]{1,0:T(8,128)(2,1)S(1)}, bf16[24,3584]{1,0:T(8,128)(2,1)S(1)}, u32[]{:S(2)}, u32[]{:S(2)}) %collective-permute-start.10) | collective-permute-done | bytes 172064 | tf_op jit(solution)/shard_map/ppermute | solution.py:31
  54.6 1.8 %collective-permute-start.29 = (bf16[24,3584]{1,0:T(8,128)(2,1)S(1)}, bf16[24,3584]{1,0:T(8,128)(2,1)S(1)}, u32[]{:S(2)}, u32[]{:S(2)}) collective-permute-start(bf16[24,3584]{1,0:T(8,128)(2,1)S(1)} %slice.298), channel_id=1, source_target_pairs={{0,8},{4,12},{8,0},{12,4},{1,9},{5,13},{9,1},{13,5},{2,10},{6,14},... | collective-permute-start | bytes 516104 | tf_op jit(solution)/shard_map/ppermute | solution.py:31
  56.4 1.0 %collective-permute-start.22 = (bf16[16,3584]{1,0:T(8,128)(2,1)S(1)}, bf16[16,3584]{1,0:T(8,128)(2,1)S(1)}, u32[]{:S(2)}, u32[]{:S(2)}) collective-permute-start(bf16[16,3584]{1,0:T(8,128)(2,1)S(1)} %slice.265), channel_id=1, source_target_pairs={{0,1},{1,0},{2,3},{3,2},{4,5},{5,4},{6,7},{7,6},{8,9},{9,8},{10,11... | collective-permute-start | bytes 344072 | tf_op jit(solution)/shard_map/ppermute | solution.py:31
  57.4 1.0 %collective-permute-start.24 = (bf16[16,3584]{1,0:T(8,128)(2,1)S(1)}, bf16[16,3584]{1,0:T(8,128)(2,1)S(1)}, u32[]{:S(2)}, u32[]{:S(2)}) collective-permute-start(bf16[16,3584]{1,0:T(8,128)(2,1)S(1)} %slice.280), channel_id=1, source_target_pairs={{0,1},{1,0},{2,3},{3,2},{4,5},{5,4},{6,7},{7,6},{8,9},{9,8},{10,11... | collective-permute-start | bytes 344072 | tf_op jit(solution)/shard_map/ppermute | solution.py:31
  58.8 1.8 %collective-permute-start.26 = (bf16[16,7168]{1,0:T(8,128)(2,1)S(1)}, bf16[16,7168]{1,0:T(8,128)(2,1)S(1)}, u32[]{:S(2)}, u32[]{:S(2)}) collective-permute-start(bf16[16,7168]{1,0:T(8,128)(2,1)S(1)} %maximum_maximum_fusion), channel_id=1, source_target_pairs={{0,8},{4,12},{8,0},{12,4},{1,9},{5,13},{9,1},{13,5},{2,10},{6,14},... | collective-permute-start | bytes 688136 | tf_op jit(solution)/shard_map/ppermute | solution.py:31
  60.6 1.4 %collective-permute-done.22 = bf16[16,3584]{1,0:T(8,128)(2,1)S(1)} collective-permute-done((bf16[16,3584]{1,0:T(8,128)(2,1)S(1)}, bf16[16,3584]{1,0:T(8,128)(2,1)S(1)}, u32[]{:S(2)}, u32[]{:S(2)}) %collective-permute-start.22) | collective-permute-done | bytes 114720 | tf_op jit(solution)/shard_map/ppermute | solution.py:31
  62.0 1.2 %collective-permute-done.24 = bf16[16,3584]{1,0:T(8,128)(2,1)S(1)} collective-permute-done((bf16[16,3584]{1,0:T(8,128)(2,1)S(1)}, bf16[16,3584]{1,0:T(8,128)(2,1)S(1)}, u32[]{:S(2)}, u32[]{:S(2)}) %collective-permute-start.24) | collective-permute-done | bytes 114720 | tf_op jit(solution)/shard_map/ppermute | solution.py:31
  63.3 2.0 %collective-permute-start.25 = (bf16[8,7168]{1,0:T(8,128)(2,1)S(1)}, bf16[8,7168]{1,0:T(8,128)(2,1)S(1)}, u32[]{:S(2)}, u32[]{:S(2)}) collective-permute-start(bf16[8,7168]{1,0:T(8,128)(2,1)S(1)} %pad_maximum_fusion.11), channel_id=1, source_target_pairs={{0,2},{1,3},{2,0},{3,1},{4,6},{5,7},{6,4},{7,5},{8,10},{9,11},{10,... | collective-permute-start | bytes 344072 | tf_op jit(solution)/shard_map/ppermute | solution.py:31
  65.4 1.6 %collective-permute-start.30 = (bf16[16,3584]{1,0:T(8,128)(2,1)S(1)}, bf16[16,3584]{1,0:T(8,128)(2,1)S(1)}, u32[]{:S(2)}, u32[]{:S(2)}) collective-permute-start(bf16[16,3584]{1,0:T(8,128)(2,1)S(1)} %slice.299), channel_id=1, source_target_pairs={{0,1},{1,0},{2,3},{3,2},{4,5},{5,4},{6,7},{7,6},{8,9},{9,8},{10,11... | collective-permute-start | bytes 344072 | tf_op jit(solution)/shard_map/ppermute | solution.py:31
  67.6 4.3 %collective-permute-done.30 = bf16[16,3584]{1,0:T(8,128)(2,1)S(1)} collective-permute-done((bf16[16,3584]{1,0:T(8,128)(2,1)S(1)}, bf16[16,3584]{1,0:T(8,128)(2,1)S(1)}, u32[]{:S(2)}, u32[]{:S(2)}) %collective-permute-start.30) | collective-permute-done | bytes 114720 | tf_op jit(solution)/shard_map/ppermute | solution.py:31
  72.5 0.9 %collective-permute-done.28 = bf16[16,3584]{1,0:T(8,128)(2,1)S(1)} collective-permute-done((bf16[16,3584]{1,0:T(8,128)(2,1)S(1)}, bf16[16,3584]{1,0:T(8,128)(2,1)S(1)}, u32[]{:S(2)}, u32[]{:S(2)}) %collective-permute-start.28) | collective-permute-done | bytes 114720 | tf_op jit(solution)/shard_map/ppermute | solution.py:31
  73.4 1.6 %collective-permute-start.31 = (bf16[8,3584]{1,0:T(8,128)(2,1)S(1)}, bf16[8,3584]{1,0:T(8,128)(2,1)S(1)}, u32[]{:S(2)}, u32[]{:S(2)}) collective-permute-start(bf16[8,3584]{1,0:T(8,128)(2,1)S(1)} %get-tuple-element.57), channel_id=1, source_target_pairs={{0,2},{1,3},{2,0},{3,1},{4,6},{5,7},{6,4},{7,5},{8,10},{9,11},{10,... | collective-permute-start | bytes 172040 | tf_op jit(solution)/shard_map/ppermute | solution.py:31
  75.0 2.1 %collective-permute-done.32 = bf16[8,3584]{1,0:T(8,128)(2,1)S(1)} collective-permute-done((bf16[8,3584]{1,0:T(8,128)(2,1)S(1)}, bf16[8,3584]{1,0:T(8,128)(2,1)S(1)}, u32[]{:S(2)}, u32[]{:S(2)}) %collective-permute-start.32) | collective-permute-done | bytes 57376 | tf_op jit(solution)/shard_map/ppermute | solution.py:31
  77.1 1.5 %collective-permute-done.31 = bf16[8,3584]{1,0:T(8,128)(2,1)S(1)} collective-permute-done((bf16[8,3584]{1,0:T(8,128)(2,1)S(1)}, bf16[8,3584]{1,0:T(8,128)(2,1)S(1)}, u32[]{:S(2)}, u32[]{:S(2)}) %collective-permute-start.31) | collective-permute-done | bytes 57376 | tf_op jit(solution)/shard_map/ppermute | solution.py:31
  (138 shorter events, 22.8 us)
Async XLA Ops:
  2.0 11.2 %collective-permute-start.5 = (bf16[8,3584]{1,0:T(8,128)(2,1)}, bf16[8,3584]{1,0:T(8,128)(2,1)S(1)}, u32[]{:S(2)}, u32[]{:S(2)}) collective-permute-start(bf16[8,3584]{1,0:T(8,128)(2,1)} %get-tuple-element.22), channel_id=1, source_target_pairs={{0,2},{1,3},{2,0},{3,1},{4,6},{5,7},{6,4},{7,5},{8,10},{9,11},{10,... | collective-permute-start | bytes 172040 | tf_op jit(solution)/shard_map/ppermute | solution.py:31
  6.1 9.5 %collective-permute-start.16 = (bf16[8,3584]{1,0:T(8,128)(2,1)}, bf16[8,3584]{1,0:T(8,128)(2,1)S(1)}, u32[]{:S(2)}, u32[]{:S(2)}) collective-permute-start(bf16[8,3584]{1,0:T(8,128)(2,1)} %get-tuple-element.28), channel_id=1, source_target_pairs={{0,2},{1,3},{2,0},{3,1},{4,6},{5,7},{6,4},{7,5},{8,10},{9,11},{10,... | collective-permute-start | bytes 172040 | tf_op jit(solution)/shard_map/ppermute | solution.py:31
  6.2 11.4 %collective-permute-start = (bf16[8,3712]{1,0:T(8,128)(2,1)}, bf16[8,3712]{1,0:T(8,128)(2,1)S(1)}, u32[]{:S(2)}, u32[]{:S(2)}) collective-permute-start(bf16[8,3712]{1,0:T(8,128)(2,1)} %get-tuple-element.20), channel_id=1, source_target_pairs={{0,2},{1,3},{2,0},{3,1},{4,6},{5,7},{6,4},{7,5},{8,10},{9,11},{10,... | collective-permute-start | bytes 178184 | tf_op jit(solution)/shard_map/ppermute | solution.py:31
  9.1 11.0 %collective-permute-start.11 = (bf16[8,3712]{1,0:T(8,128)(2,1)}, bf16[8,3712]{1,0:T(8,128)(2,1)S(1)}, u32[]{:S(2)}, u32[]{:S(2)}) collective-permute-start(bf16[8,3712]{1,0:T(8,128)(2,1)} %get-tuple-element.23), channel_id=1, source_target_pairs={{0,2},{1,3},{2,0},{3,1},{4,6},{5,7},{6,4},{7,5},{8,10},{9,11},{10,... | collective-permute-start | bytes 178184 | tf_op jit(solution)/shard_map/ppermute | solution.py:31
  9.1 18.3 %collective-permute-start.2 = (bf16[16,7296]{1,0:T(8,128)(2,1)}, bf16[16,7296]{1,0:T(8,128)(2,1)S(1)}, u32[]{:S(2)}, u32[]{:S(2)}) collective-permute-start(bf16[16,7296]{1,0:T(8,128)(2,1)} %get-tuple-element.21), channel_id=1, source_target_pairs={{0,8},{4,12},{8,0},{12,4},{1,9},{5,13},{9,1},{13,5},{2,10},{6,14},... | collective-permute-start | bytes 700424 | tf_op jit(solution)/shard_map/ppermute | solution.py:31
  14.1 7.4 %collective-permute-start.6 = (bf16[16,3584]{1,0:T(8,128)(2,1)S(1)}, bf16[16,3584]{1,0:T(8,128)(2,1)S(1)}, u32[]{:S(2)}, u32[]{:S(2)}) collective-permute-start(bf16[16,3584]{1,0:T(8,128)(2,1)S(1)} %pad_maximum_fusion.9), channel_id=1, source_target_pairs={{0,1},{1,0},{2,3},{3,2},{4,5},{5,4},{6,7},{7,6},{8,9},{9,8},{10,11... | collective-permute-start | bytes 344072 | tf_op jit(solution)/shard_map/ppermute | solution.py:31
  16.5 6.1 %collective-permute-start.17 = (bf16[16,3584]{1,0:T(8,128)(2,1)S(1)}, bf16[16,3584]{1,0:T(8,128)(2,1)S(1)}, u32[]{:S(2)}, u32[]{:S(2)}) collective-permute-start(bf16[16,3584]{1,0:T(8,128)(2,1)S(1)} %pad_maximum_fusion.10), channel_id=1, source_target_pairs={{0,1},{1,0},{2,3},{3,2},{4,5},{5,4},{6,7},{7,6},{8,9},{9,8},{10,11... | collective-permute-start | bytes 344072 | tf_op jit(solution)/shard_map/ppermute | solution.py:31
  18.4 6.7 %collective-permute-start.1 = (bf16[16,3712]{1,0:T(8,128)(2,1)S(1)}, bf16[16,3712]{1,0:T(8,128)(2,1)S(1)}, u32[]{:S(2)}, u32[]{:S(2)}) collective-permute-start(bf16[16,3712]{1,0:T(8,128)(2,1)S(1)} %pad_maximum_fusion.7), channel_id=1, source_target_pairs={{0,1},{1,0},{2,3},{3,2},{4,5},{5,4},{6,7},{7,6},{8,9},{9,8},{10,11... | collective-permute-start | bytes 356360 | tf_op jit(solution)/shard_map/ppermute | solution.py:31
  20.9 6.5 %collective-permute-start.12 = (bf16[16,3712]{1,0:T(8,128)(2,1)S(1)}, bf16[16,3712]{1,0:T(8,128)(2,1)S(1)}, u32[]{:S(2)}, u32[]{:S(2)}) collective-permute-start(bf16[16,3712]{1,0:T(8,128)(2,1)S(1)} %pad_maximum_fusion.8), channel_id=1, source_target_pairs={{0,1},{1,0},{2,3},{3,2},{4,5},{5,4},{6,7},{7,6},{8,9},{9,8},{10,11... | collective-permute-start | bytes 356360 | tf_op jit(solution)/shard_map/ppermute | solution.py:31
  21.5 6.6 %collective-permute-start.7 = (bf16[24,3584]{1,0:T(8,128)(2,1)S(1)}, bf16[24,3584]{1,0:T(8,128)(2,1)S(1)}, u32[]{:S(2)}, u32[]{:S(2)}) collective-permute-start(bf16[24,3584]{1,0:T(8,128)(2,1)S(1)} %pad_maximum_fusion.5), channel_id=1, source_target_pairs={{0,8},{4,12},{8,0},{12,4},{1,9},{5,13},{9,1},{13,5},{2,10},{6,14},... | collective-permute-start | bytes 516104 | tf_op jit(solution)/shard_map/ppermute | solution.py:31
  25.1 6.1 %collective-permute-start.3 = (bf16[24,3712]{1,0:T(8,128)(2,1)S(1)}, bf16[24,3712]{1,0:T(8,128)(2,1)S(1)}, u32[]{:S(2)}, u32[]{:S(2)}) collective-permute-start(bf16[24,3712]{1,0:T(8,128)(2,1)S(1)} %pad_maximum_fusion.3), channel_id=1, source_target_pairs={{0,8},{4,12},{8,0},{12,4},{1,9},{5,13},{9,1},{13,5},{2,10},{6,14},... | collective-permute-start | bytes 534536 | tf_op jit(solution)/shard_map/ppermute | solution.py:31
  28.8 2.5 %collective-permute-start.8 = (bf16[64,3584]{1,0:T(8,128)(2,1)S(1)}, bf16[64,3584]{1,0:T(8,128)(2,1)S(1)}, u32[]{:S(2)}, u32[]{:S(2)}) collective-permute-start(bf16[64,3584]{1,0:T(8,128)(2,1)S(1)} %get-tuple-element.49), channel_id=1, source_target_pairs={{0,4},{4,0},{8,12},{12,8},{1,5},{5,1},{9,13},{13,9},{2,6},{6,2},{1... | collective-permute-start | bytes 1376264 | tf_op jit(solution)/shard_map/ppermute | solution.py:31
  28.8 12.7 %collective-permute-start.18 = (bf16[24,3584]{1,0:T(8,128)(2,1)S(1)}, bf16[24,3584]{1,0:T(8,128)(2,1)S(1)}, u32[]{:S(2)}, u32[]{:S(2)}) collective-permute-start(bf16[24,3584]{1,0:T(8,128)(2,1)S(1)} %pad_maximum_fusion.6), channel_id=1, source_target_pairs={{0,8},{4,12},{8,0},{12,4},{1,9},{5,13},{9,1},{13,5},{2,10},{6,14},... | collective-permute-start | bytes 516104 | tf_op jit(solution)/shard_map/ppermute | solution.py:31
  30.5 11.0 %collective-permute-start.13 = (bf16[24,3712]{1,0:T(8,128)(2,1)S(1)}, bf16[24,3712]{1,0:T(8,128)(2,1)S(1)}, u32[]{:S(2)}, u32[]{:S(2)}) collective-permute-start(bf16[24,3712]{1,0:T(8,128)(2,1)S(1)} %pad_maximum_fusion.4), channel_id=1, source_target_pairs={{0,8},{4,12},{8,0},{12,4},{1,9},{5,13},{9,1},{13,5},{2,10},{6,14},... | collective-permute-start | bytes 534536 | tf_op jit(solution)/shard_map/ppermute | solution.py:31
  31.3 4.7 %collective-permute-start.4 = (bf16[64,3712]{1,0:T(8,128)(2,1)S(1)}, bf16[64,3712]{1,0:T(8,128)(2,1)S(1)}, u32[]{:S(2)}, u32[]{:S(2)}) collective-permute-start(bf16[64,3712]{1,0:T(8,128)(2,1)S(1)} %get-tuple-element.47), channel_id=1, source_target_pairs={{0,4},{4,0},{8,12},{12,8},{1,5},{5,1},{9,13},{13,9},{2,6},{6,2},{1... | collective-permute-start | bytes 1425416 | tf_op jit(solution)/shard_map/ppermute | solution.py:31
  41.6 2.0 %collective-permute-start.9 = (bf16[64,3584]{1,0:T(8,128)(2,1)S(1)}, bf16[64,3584]{1,0:T(8,128)(2,1)S(1)}, u32[]{:S(2)}, u32[]{:S(2)}) collective-permute-start(bf16[64,3584]{1,0:T(8,128)(2,1)S(1)} %slice.261), channel_id=1, source_target_pairs={{0,4},{4,0},{8,12},{12,8},{1,5},{5,1},{9,13},{13,9},{2,6},{6,2},{1... | collective-permute-start | bytes 1376264 | tf_op jit(solution)/shard_map/ppermute | solution.py:31
  41.7 4.2 %collective-permute-start.19 = (bf16[64,3584]{1,0:T(8,128)(2,1)S(1)}, bf16[64,3584]{1,0:T(8,128)(2,1)S(1)}, u32[]{:S(2)}, u32[]{:S(2)}) collective-permute-start(bf16[64,3584]{1,0:T(8,128)(2,1)S(1)} %constant_dynamic-update-slice_fusion.27), channel_id=1, source_target_pairs={{0,4},{4,0},{8,12},{12,8},{1,5},{5,1},{9,13},{13,9},{2,6},{6,2},{1... | collective-permute-start | bytes 1376264 | tf_op jit(solution)/shard_map/ppermute | solution.py:31
  42.2 5.1 %collective-permute-start.14 = (bf16[64,3712]{1,0:T(8,128)(2,1)S(1)}, bf16[64,3712]{1,0:T(8,128)(2,1)S(1)}, u32[]{:S(2)}, u32[]{:S(2)}) collective-permute-start(bf16[64,3712]{1,0:T(8,128)(2,1)S(1)} %constant_dynamic-update-slice_fusion.22), channel_id=1, source_target_pairs={{0,4},{4,0},{8,12},{12,8},{1,5},{5,1},{9,13},{13,9},{2,6},{6,2},{1... | collective-permute-start | bytes 1425416 | tf_op jit(solution)/shard_map/ppermute | solution.py:31
  43.8 7.3 %collective-permute-start.23 = (bf16[24,3584]{1,0:T(8,128)(2,1)S(1)}, bf16[24,3584]{1,0:T(8,128)(2,1)S(1)}, u32[]{:S(2)}, u32[]{:S(2)}) collective-permute-start(bf16[24,3584]{1,0:T(8,128)(2,1)S(1)} %slice.279), channel_id=1, source_target_pairs={{0,8},{4,12},{8,0},{12,4},{1,9},{5,13},{9,1},{13,5},{2,10},{6,14},... | collective-permute-start | bytes 516104 | tf_op jit(solution)/shard_map/ppermute | solution.py:31
  45.6 8.6 %collective-permute-start.10 = (bf16[24,3584]{1,0:T(8,128)(2,1)S(1)}, bf16[24,3584]{1,0:T(8,128)(2,1)S(1)}, u32[]{:S(2)}, u32[]{:S(2)}) collective-permute-start(bf16[24,3584]{1,0:T(8,128)(2,1)S(1)} %slice.264), channel_id=1, source_target_pairs={{0,8},{4,12},{8,0},{12,4},{1,9},{5,13},{9,1},{13,5},{2,10},{6,14},... | collective-permute-start | bytes 516104 | tf_op jit(solution)/shard_map/ppermute | solution.py:31
  50.2 4.1 %collective-permute-start.21 = (bf16[64,3584]{1,0:T(8,128)(2,1)S(1)}, bf16[64,3584]{1,0:T(8,128)(2,1)S(1)}, u32[]{:S(2)}, u32[]{:S(2)}) collective-permute-start(bf16[64,3584]{1,0:T(8,128)(2,1)S(1)} %slice.275), channel_id=1, source_target_pairs={{0,4},{4,0},{8,12},{12,8},{1,5},{5,1},{9,13},{13,9},{2,6},{6,2},{1... | collective-permute-start | bytes 1376264 | tf_op jit(solution)/shard_map/ppermute | solution.py:31
  50.3 4.1 %collective-permute-start.20 = (bf16[64,3584]{1,0:T(8,128)(2,1)S(1)}, bf16[64,3584]{1,0:T(8,128)(2,1)S(1)}, u32[]{:S(2)}, u32[]{:S(2)}) collective-permute-start(bf16[64,3584]{1,0:T(8,128)(2,1)S(1)} %slice.273), channel_id=1, source_target_pairs={{0,4},{4,0},{8,12},{12,8},{1,5},{5,1},{9,13},{13,9},{2,6},{6,2},{1... | collective-permute-start | bytes 1376264 | tf_op jit(solution)/shard_map/ppermute | solution.py:31
  54.6 10.7 %collective-permute-start.29 = (bf16[24,3584]{1,0:T(8,128)(2,1)S(1)}, bf16[24,3584]{1,0:T(8,128)(2,1)S(1)}, u32[]{:S(2)}, u32[]{:S(2)}) collective-permute-start(bf16[24,3584]{1,0:T(8,128)(2,1)S(1)} %slice.298), channel_id=1, source_target_pairs={{0,8},{4,12},{8,0},{12,4},{1,9},{5,13},{9,1},{13,5},{2,10},{6,14},... | collective-permute-start | bytes 516104 | tf_op jit(solution)/shard_map/ppermute | solution.py:31
  56.4 5.6 %collective-permute-start.22 = (bf16[16,3584]{1,0:T(8,128)(2,1)S(1)}, bf16[16,3584]{1,0:T(8,128)(2,1)S(1)}, u32[]{:S(2)}, u32[]{:S(2)}) collective-permute-start(bf16[16,3584]{1,0:T(8,128)(2,1)S(1)} %slice.265), channel_id=1, source_target_pairs={{0,1},{1,0},{2,3},{3,2},{4,5},{5,4},{6,7},{7,6},{8,9},{9,8},{10,11... | collective-permute-start | bytes 344072 | tf_op jit(solution)/shard_map/ppermute | solution.py:31
  57.4 5.8 %collective-permute-start.24 = (bf16[16,3584]{1,0:T(8,128)(2,1)S(1)}, bf16[16,3584]{1,0:T(8,128)(2,1)S(1)}, u32[]{:S(2)}, u32[]{:S(2)}) collective-permute-start(bf16[16,3584]{1,0:T(8,128)(2,1)S(1)} %slice.280), channel_id=1, source_target_pairs={{0,1},{1,0},{2,3},{3,2},{4,5},{5,4},{6,7},{7,6},{8,9},{9,8},{10,11... | collective-permute-start | bytes 344072 | tf_op jit(solution)/shard_map/ppermute | solution.py:31
  58.5 8.5 %collective-permute-start.27 = (bf16[24,3584]{1,0:T(8,128)(2,1)S(1)}, bf16[24,3584]{1,0:T(8,128)(2,1)S(1)}, u32[]{:S(2)}, u32[]{:S(2)}) collective-permute-start(bf16[24,3584]{1,0:T(8,128)(2,1)S(1)} %slice.293), channel_id=1, source_target_pairs={{0,8},{4,12},{8,0},{12,4},{1,9},{5,13},{9,1},{13,5},{2,10},{6,14},... | collective-permute-start | bytes 516104 | tf_op jit(solution)/shard_map/ppermute | solution.py:31
  58.8 16.3 %collective-permute-start.26 = (bf16[16,7168]{1,0:T(8,128)(2,1)S(1)}, bf16[16,7168]{1,0:T(8,128)(2,1)S(1)}, u32[]{:S(2)}, u32[]{:S(2)}) collective-permute-start(bf16[16,7168]{1,0:T(8,128)(2,1)S(1)} %maximum_maximum_fusion), channel_id=1, source_target_pairs={{0,8},{4,12},{8,0},{12,4},{1,9},{5,13},{9,1},{13,5},{2,10},{6,14},... | collective-permute-start | bytes 688136 | tf_op jit(solution)/shard_map/ppermute | solution.py:31
  63.3 11.8 %collective-permute-start.25 = (bf16[8,7168]{1,0:T(8,128)(2,1)S(1)}, bf16[8,7168]{1,0:T(8,128)(2,1)S(1)}, u32[]{:S(2)}, u32[]{:S(2)}) collective-permute-start(bf16[8,7168]{1,0:T(8,128)(2,1)S(1)} %pad_maximum_fusion.11), channel_id=1, source_target_pairs={{0,2},{1,3},{2,0},{3,1},{4,6},{5,7},{6,4},{7,5},{8,10},{9,11},{10,... | collective-permute-start | bytes 344072 | tf_op jit(solution)/shard_map/ppermute | solution.py:31
  65.4 6.5 %collective-permute-start.30 = (bf16[16,3584]{1,0:T(8,128)(2,1)S(1)}, bf16[16,3584]{1,0:T(8,128)(2,1)S(1)}, u32[]{:S(2)}, u32[]{:S(2)}) collective-permute-start(bf16[16,3584]{1,0:T(8,128)(2,1)S(1)} %slice.299), channel_id=1, source_target_pairs={{0,1},{1,0},{2,3},{3,2},{4,5},{5,4},{6,7},{7,6},{8,9},{9,8},{10,11... | collective-permute-start | bytes 344072 | tf_op jit(solution)/shard_map/ppermute | solution.py:31
  67.0 6.4 %collective-permute-start.28 = (bf16[16,3584]{1,0:T(8,128)(2,1)S(1)}, bf16[16,3584]{1,0:T(8,128)(2,1)S(1)}, u32[]{:S(2)}, u32[]{:S(2)}) collective-permute-start(bf16[16,3584]{1,0:T(8,128)(2,1)S(1)} %slice.294), channel_id=1, source_target_pairs={{0,1},{1,0},{2,3},{3,2},{4,5},{5,4},{6,7},{7,6},{8,9},{9,8},{10,11... | collective-permute-start | bytes 344072 | tf_op jit(solution)/shard_map/ppermute | solution.py:31
  71.9 5.2 %collective-permute-start.32 = (bf16[8,3584]{1,0:T(8,128)(2,1)S(1)}, bf16[8,3584]{1,0:T(8,128)(2,1)S(1)}, u32[]{:S(2)}, u32[]{:S(2)}) collective-permute-start(bf16[8,3584]{1,0:T(8,128)(2,1)S(1)} %get-tuple-element.59), channel_id=1, source_target_pairs={{0,2},{1,3},{2,0},{3,1},{4,6},{5,7},{6,4},{7,5},{8,10},{9,11},{10,... | collective-permute-start | bytes 172040 | tf_op jit(solution)/shard_map/ppermute | solution.py:31
  73.4 5.1 %collective-permute-start.31 = (bf16[8,3584]{1,0:T(8,128)(2,1)S(1)}, bf16[8,3584]{1,0:T(8,128)(2,1)S(1)}, u32[]{:S(2)}, u32[]{:S(2)}) collective-permute-start(bf16[8,3584]{1,0:T(8,128)(2,1)S(1)} %get-tuple-element.57), channel_id=1, source_target_pairs={{0,2},{1,3},{2,0},{3,1},{4,6},{5,7},{6,4},{7,5},{8,10},{9,11},{10,... | collective-permute-start | bytes 172040 | tf_op jit(solution)/shard_map/ppermute | solution.py:31
  (13 other events, 74.6 us)

commit v7 on v5

--- a/solution.py
+++ b/solution.py
@@ -12,7 +12,7 @@
 F_Z2 = 2
 F_XORD = 2
 F_C1 = 1
-F_Z2R = 2
+F_Z2R = 5
 F_CHOLD = 1
 F_OUT1 = 2
 F_FIN0 = 1

time: 79.4 us -> 79.5 us (level)
  waiting for transfers between devices: 18.8 us -> 15.1 us
  starting transfers between devices: 36 us -> 39.1 us
    ppermute x33, waiting for transfers between devices: 18.8 us -> 15.1 us  [swap(): return lax.ppermute(value, axis_name, [(i, i ^ bit) for i in range(count)])]
    ppermute x33, starting transfers between devices: 36 us -> 39.1 us  [swap(): return lax.ppermute(value, axis_name, [(i, i ^ bit) for i in range(count)])]
  transfers between devices with their start and end apart: 33 -> 33, of which waited for: 14 -> 14; matrix products, arithmetic and copies ran while one was open for 23% -> 24% of each run, Pallas kernels for 0% -> 0%
where the time goes in v7:
time: 79.5 us; the launch traced here: 78.3 us
  starting transfers between devices  39.1 us (49%)
  waiting for transfers between devices  15.1 us (19%)
  matrix products  10.1 us (13%)
  local copies, waits for them, and re-layouts  5.88 us (7%)
  other arithmetic  5.51 us (7%)
  Pallas kernels  2.02 us (3%)
    ppermute x33, starting transfers between devices, swap(): return lax.ppermute(value, axis_name, [(i, i ^ bit) for i in range(count)])  39.1 us
    ppermute x33, waiting for transfers between devices, swap(): return lax.ppermute(value, axis_name, [(i, i ^ bit) for i in range(count)])  15.1 us
    unnamed x32, local copies, waits for them, and re-layouts  5.49 us
    dot_general x4, matrix products, body(): up_value += jnp.dot(part, w_up[0, span], preferred_element_type=jnp.float32)  4.78 us
    concatenate x11, other arithmetic, join(): return jnp.concatenate(parts, axis=0)  3.54 us
    dot_general x4, matrix products, body(): jnp.dot(hidden, w_down[0, :, start:end], preferred_element_type=jnp.float32)  2.72 us
    dot_general x4, matrix products, body(): jnp.dot(part, w_gate[0, span], preferred_element_type=jnp.float32)  2.57 us
    pallas_call x1, Pallas kernels, prepare(): pl.pallas_call(functools.partial(prepare_kernel, ep_count, extra, cuts),...  2.02 us
  transfers between devices with their start and end apart: 33, of which 14 were waited for; matrix products, arithmetic and copies ran while one was open for 24% of the time, Pallas kernels for 0%

profile of v7, /device:TPU:0, one launch (start us, length us, event | category | flops | bytes accessed | tf_op | source)
XLA Modules:
  0.0 78.3 jit_solution(8360254774827848359)
XLA Ops:
  0.0 2.0 %shard_map.73 = (bf16[16,7296]{1,0:T(8,128)(2,1)}, bf16[8,3712]{1,0:T(8,128)(2,1)}, bf16[8,3584]{1,0:T(8,128)(2,1)}, bf16[8,3712]{1,0:T(8,128)(2,1)}, bf16[8,3584]{1,0:T(8,128)(2,1)}) custom-call(bf16[2,8,7168]{2,1,0:T(8,128)(2,1)} %codes_hbm.1, f32[2,8,56]{2,1,0:T(8,128)} %scales_hbm.1, s32[2,2,8]{2,1,0:T(2,128)} %bitcast.58, s32[2,2,8]{2,1,0:T(2,128)} %bitcast.59), custom_call_target="tpu_custom_call" | custom-call | tf_op jit(solution)/shard_map/pallas_call | solution.py:106
  2.0 4.1 %collective-permute-start.5 = (bf16[8,3584]{1,0:T(8,128)(2,1)}, bf16[8,3584]{1,0:T(8,128)(2,1)S(1)}, u32[]{:S(2)}, u32[]{:S(2)}) collective-permute-start(bf16[8,3584]{1,0:T(8,128)(2,1)} %get-tuple-element.25), channel_id=1, source_target_pairs={{0,2},{1,3},{2,0},{3,1},{4,6},{5,7},{6,4},{7,5},{8,10},{9,11},{10,... | collective-permute-start | bytes 172040 | tf_op jit(solution)/shard_map/ppermute | solution.py:31
  6.2 1.7 %collective-permute-start.2 = (bf16[16,7296]{1,0:T(8,128)(2,1)}, bf16[16,7296]{1,0:T(8,128)(2,1)S(1)}, u32[]{:S(2)}, u32[]{:S(2)}) collective-permute-start(bf16[16,7296]{1,0:T(8,128)(2,1)} %get-tuple-element.24), channel_id=1, source_target_pairs={{0,8},{4,12},{8,0},{12,4},{1,9},{5,13},{9,1},{13,5},{2,10},{6,14},... | collective-permute-start | bytes 700424 | tf_op jit(solution)/shard_map/ppermute | solution.py:31
  8.8 0.8 %constant_dynamic-update-slice_fusion.4 = (bf16[64,3712]{1,0:T(8,128)(2,1)S(1)}, bf16[128,3712]{1,0:T(8,128)(2,1)S(1)}) fusion(bf16[8,3712]{1,0:T(8,128)(2,1)} %get-tuple-element.23), kind=kLoop, calls=%fused_computation.92 | loop fusion | bytes 178176
  9.6 2.7 %collective-permute-start.16 = (bf16[8,3584]{1,0:T(8,128)(2,1)}, bf16[8,3584]{1,0:T(8,128)(2,1)S(1)}, u32[]{:S(2)}, u32[]{:S(2)}) collective-permute-start(bf16[8,3584]{1,0:T(8,128)(2,1)} %get-tuple-element.33), channel_id=1, source_target_pairs={{0,2},{1,3},{2,0},{3,1},{4,6},{5,7},{6,4},{7,5},{8,10},{9,11},{10,... | collective-permute-start | bytes 172040 | tf_op jit(solution)/shard_map/ppermute | solution.py:31
  12.3 0.9 %constant_dynamic-update-slice_fusion.31 = bf16[64,3584]{1,0:T(8,128)(2,1)S(1)} fusion(bf16[8,3584]{1,0:T(8,128)(2,1)} %get-tuple-element.33), kind=kLoop, calls=%fused_computation.119 | loop fusion | bytes 114688
  15.2 2.3 %collective-permute-start.6 = (bf16[16,3584]{1,0:T(8,128)(2,1)S(1)}, bf16[16,3584]{1,0:T(8,128)(2,1)S(1)}, u32[]{:S(2)}, u32[]{:S(2)}) collective-permute-start(bf16[16,3584]{1,0:T(8,128)(2,1)S(1)} %pad_maximum_fusion.9), channel_id=1, source_target_pairs={{0,1},{1,0},{2,3},{3,2},{4,5},{5,4},{6,7},{7,6},{8,9},{9,8},{10,11... | collective-permute-start | bytes 344072 | tf_op jit(solution)/shard_map/ppermute | solution.py:31
  17.5 0.8 %pad_maximum_fusion.7 = bf16[16,3712]{1,0:T(8,128)(2,1)S(1)} fusion(bf16[8,3712]{1,0:T(8,128)(2,1)S(1)} %collective-permute-done, bf16[8,3712]{1,0:T(8,128)(2,1)} %get-tuple-element.23), kind=kLoop, calls=%fused_computation.73 | loop fusion | flops 237568 | bytes 237568 | tf_op jit(solution)/shard_map/concatenate | solution.py:39
  19.3 2.0 %collective-permute-start.17 = (bf16[16,3584]{1,0:T(8,128)(2,1)S(1)}, bf16[16,3584]{1,0:T(8,128)(2,1)S(1)}, u32[]{:S(2)}, u32[]{:S(2)}) collective-permute-start(bf16[16,3584]{1,0:T(8,128)(2,1)S(1)} %pad_maximum_fusion.10), channel_id=1, source_target_pairs={{0,1},{1,0},{2,3},{3,2},{4,5},{5,4},{6,7},{7,6},{8,9},{9,8},{10,11... | collective-permute-start | bytes 344072 | tf_op jit(solution)/shard_map/ppermute | solution.py:31
  21.3 0.8 %pad_maximum_fusion.8 = bf16[16,3712]{1,0:T(8,128)(2,1)S(1)} fusion(bf16[8,3712]{1,0:T(8,128)(2,1)S(1)} %collective-permute-done.11, bf16[8,3712]{1,0:T(8,128)(2,1)} %get-tuple-element.27), kind=kLoop, calls=%fused_computation.74 | loop fusion | flops 237568 | bytes 237568 | tf_op jit(solution)/shard_map/concatenate | solution.py:39
  22.6 1.6 %collective-permute-start.7 = (bf16[24,3584]{1,0:T(8,128)(2,1)S(1)}, bf16[24,3584]{1,0:T(8,128)(2,1)S(1)}, u32[]{:S(2)}, u32[]{:S(2)}) collective-permute-start(bf16[24,3584]{1,0:T(8,128)(2,1)S(1)} %pad_maximum_fusion.5), channel_id=1, source_target_pairs={{0,8},{4,12},{8,0},{12,4},{1,9},{5,13},{9,1},{13,5},{2,10},{6,14},... | collective-permute-start | bytes 516104 | tf_op jit(solution)/shard_map/ppermute | solution.py:31
  24.6 1.6 %collective-permute-start.3 = (bf16[24,3712]{1,0:T(8,128)(2,1)S(1)}, bf16[24,3712]{1,0:T(8,128)(2,1)S(1)}, u32[]{:S(2)}, u32[]{:S(2)}) collective-permute-start(bf16[24,3712]{1,0:T(8,128)(2,1)S(1)} %pad_maximum_fusion.3), channel_id=1, source_target_pairs={{0,8},{4,12},{8,0},{12,4},{1,9},{5,13},{9,1},{13,5},{2,10},{6,14},... | collective-permute-start | bytes 534536 | tf_op jit(solution)/shard_map/ppermute | solution.py:31
  26.2 0.9 %collective-permute-done.17 = bf16[16,3584]{1,0:T(8,128)(2,1)S(1)} collective-permute-done((bf16[16,3584]{1,0:T(8,128)(2,1)S(1)}, bf16[16,3584]{1,0:T(8,128)(2,1)S(1)}, u32[]{:S(2)}, u32[]{:S(2)}) %collective-permute-start.17) | collective-permute-done | bytes 114720 | tf_op jit(solution)/shard_map/ppermute | solution.py:31
  27.1 1.4 %collective-permute-done.12 = bf16[16,3712]{1,0:T(8,128)(2,1)S(1)} collective-permute-done((bf16[16,3712]{1,0:T(8,128)(2,1)S(1)}, bf16[16,3712]{1,0:T(8,128)(2,1)S(1)}, u32[]{:S(2)}, u32[]{:S(2)}) %collective-permute-start.12) | collective-permute-done | bytes 118816 | tf_op jit(solution)/shard_map/ppermute | solution.py:31
  29.4 1.6 %collective-permute-start.18 = (bf16[24,3584]{1,0:T(8,128)(2,1)S(1)}, bf16[24,3584]{1,0:T(8,128)(2,1)S(1)}, u32[]{:S(2)}, u32[]{:S(2)}) collective-permute-start(bf16[24,3584]{1,0:T(8,128)(2,1)S(1)} %pad_maximum_fusion.6), channel_id=1, source_target_pairs={{0,8},{4,12},{8,0},{12,4},{1,9},{5,13},{9,1},{13,5},{2,10},{6,14},... | collective-permute-start | bytes 516104 | tf_op jit(solution)/shard_map/ppermute | solution.py:31
  31.7 2.8 %fusion.10 = f32[128,512]{1,0:T(8,128)S(1)} fusion(bf16[128,3584]{1,0:T(8,128)(2,1)S(1)} %constant_dynamic-update-slice_fusion.16, bf16[1,7168,512]{2,1,0:T(8,128)(2,1)} %param.12), kind=kOutput, calls=%fused_computation.14 | convolution fusion | flops 469762048 | bytes 4849664 | tf_op jit(solution)/shard_map/dot_general | solution.py:172
  37.8 1.0 %slice-done.5 = s8[3145728]{0:T(1024)(128)(4,1)S(1)} async-done(((s8[7340032]{0:T(1024)(128)(4,1)}), s8[3145728]{0:T(1024)(128)(4,1)S(1)}, s32[]{:S(2)}) %slice-start.5) | async-done | bytes 3145752
  43.0 1.6 %collective-permute-start.23 = (bf16[24,3584]{1,0:T(8,128)(2,1)S(1)}, bf16[24,3584]{1,0:T(8,128)(2,1)S(1)}, u32[]{:S(2)}, u32[]{:S(2)}) collective-permute-start(bf16[24,3584]{1,0:T(8,128)(2,1)S(1)} %slice.279), channel_id=1, source_target_pairs={{0,8},{4,12},{8,0},{12,4},{1,9},{5,13},{9,1},{13,5},{2,10},{6,14},... | collective-permute-start | bytes 516104 | tf_op jit(solution)/shard_map/ppermute | solution.py:31
  50.4 3.0 %collective-permute-done.10 = bf16[24,3584]{1,0:T(8,128)(2,1)S(1)} collective-permute-done((bf16[24,3584]{1,0:T(8,128)(2,1)S(1)}, bf16[24,3584]{1,0:T(8,128)(2,1)S(1)}, u32[]{:S(2)}, u32[]{:S(2)}) %collective-permute-start.10) | collective-permute-done | bytes 172064 | tf_op jit(solution)/shard_map/ppermute | solution.py:31
  53.9 1.6 %collective-permute-start.29 = (bf16[24,3584]{1,0:T(8,128)(2,1)S(1)}, bf16[24,3584]{1,0:T(8,128)(2,1)S(1)}, u32[]{:S(2)}, u32[]{:S(2)}) collective-permute-start(bf16[24,3584]{1,0:T(8,128)(2,1)S(1)} %slice.298), channel_id=1, source_target_pairs={{0,8},{4,12},{8,0},{12,4},{1,9},{5,13},{9,1},{13,5},{2,10},{6,14},... | collective-permute-start | bytes 516104 | tf_op jit(solution)/shard_map/ppermute | solution.py:31
  55.4 1.7 %collective-permute-start.22 = (bf16[16,3584]{1,0:T(8,128)(2,1)S(1)}, bf16[16,3584]{1,0:T(8,128)(2,1)S(1)}, u32[]{:S(2)}, u32[]{:S(2)}) collective-permute-start(bf16[16,3584]{1,0:T(8,128)(2,1)S(1)} %slice.265), channel_id=1, source_target_pairs={{0,1},{1,0},{2,3},{3,2},{4,5},{5,4},{6,7},{7,6},{8,9},{9,8},{10,11... | collective-permute-start | bytes 344072 | tf_op jit(solution)/shard_map/ppermute | solution.py:31
  58.0 1.6 %collective-permute-start.27 = (bf16[16,7168]{1,0:T(8,128)(2,1)S(1)}, bf16[16,7168]{1,0:T(8,128)(2,1)S(1)}, u32[]{:S(2)}, u32[]{:S(2)}) collective-permute-start(bf16[16,7168]{1,0:T(8,128)(2,1)S(1)} %maximum_maximum_fusion), channel_id=1, source_target_pairs={{0,8},{4,12},{8,0},{12,4},{1,9},{5,13},{9,1},{13,5},{2,10},{6,14},... | collective-permute-start | bytes 688136 | tf_op jit(solution)/shard_map/ppermute | solution.py:31
  59.6 1.6 %collective-permute-done.22 = bf16[16,3584]{1,0:T(8,128)(2,1)S(1)} collective-permute-done((bf16[16,3584]{1,0:T(8,128)(2,1)S(1)}, bf16[16,3584]{1,0:T(8,128)(2,1)S(1)}, u32[]{:S(2)}, u32[]{:S(2)}) %collective-permute-start.22) | collective-permute-done | bytes 114720 | tf_op jit(solution)/shard_map/ppermute | solution.py:31
  61.2 1.2 %collective-permute-done.24 = bf16[16,3584]{1,0:T(8,128)(2,1)S(1)} collective-permute-done((bf16[16,3584]{1,0:T(8,128)(2,1)S(1)}, bf16[16,3584]{1,0:T(8,128)(2,1)S(1)}, u32[]{:S(2)}, u32[]{:S(2)}) %collective-permute-start.24) | collective-permute-done | bytes 114720 | tf_op jit(solution)/shard_map/ppermute | solution.py:31
  62.6 1.6 %collective-permute-start.30 = (bf16[16,3584]{1,0:T(8,128)(2,1)S(1)}, bf16[16,3584]{1,0:T(8,128)(2,1)S(1)}, u32[]{:S(2)}, u32[]{:S(2)}) collective-permute-start(bf16[16,3584]{1,0:T(8,128)(2,1)S(1)} %slice.299), channel_id=1, source_target_pairs={{0,1},{1,0},{2,3},{3,2},{4,5},{5,4},{6,7},{7,6},{8,9},{9,8},{10,11... | collective-permute-start | bytes 344072 | tf_op jit(solution)/shard_map/ppermute | solution.py:31
  64.8 2.6 %collective-permute-start.26 = (bf16[8,7168]{1,0:T(8,128)(2,1)S(1)}, bf16[8,7168]{1,0:T(8,128)(2,1)S(1)}, u32[]{:S(2)}, u32[]{:S(2)}) collective-permute-start(bf16[8,7168]{1,0:T(8,128)(2,1)S(1)} %pad_maximum_fusion.11), channel_id=1, source_target_pairs={{0,2},{1,3},{2,0},{3,1},{4,6},{5,7},{6,4},{7,5},{8,10},{9,11},{10,... | collective-permute-start | bytes 344072 | tf_op jit(solution)/shard_map/ppermute | solution.py:31
  67.5 1.8 %collective-permute-start.28 = (bf16[16,3584]{1,0:T(8,128)(2,1)S(1)}, bf16[16,3584]{1,0:T(8,128)(2,1)S(1)}, u32[]{:S(2)}, u32[]{:S(2)}) collective-permute-start(bf16[16,3584]{1,0:T(8,128)(2,1)S(1)} %slice.294), channel_id=1, source_target_pairs={{0,1},{1,0},{2,3},{3,2},{4,5},{5,4},{6,7},{7,6},{8,9},{9,8},{10,11... | collective-permute-start | bytes 344072 | tf_op jit(solution)/shard_map/ppermute | solution.py:31
  69.3 2.2 %collective-permute-start.32 = (bf16[8,3584]{1,0:T(8,128)(2,1)S(1)}, bf16[8,3584]{1,0:T(8,128)(2,1)S(1)}, u32[]{:S(2)}, u32[]{:S(2)}) collective-permute-start(bf16[8,3584]{1,0:T(8,128)(2,1)S(1)} %get-tuple-element.65), channel_id=1, source_target_pairs={{0,2},{1,3},{2,0},{3,1},{4,6},{5,7},{6,4},{7,5},{8,10},{9,11},{10,... | collective-permute-start | bytes 172040 | tf_op jit(solution)/shard_map/ppermute | solution.py:31
  71.4 0.9 %collective-permute-done.28 = bf16[16,3584]{1,0:T(8,128)(2,1)S(1)} collective-permute-done((bf16[16,3584]{1,0:T(8,128)(2,1)S(1)}, bf16[16,3584]{1,0:T(8,128)(2,1)S(1)}, u32[]{:S(2)}, u32[]{:S(2)}) %collective-permute-start.28) | collective-permute-done | bytes 114720 | tf_op jit(solution)/shard_map/ppermute | solution.py:31
  72.4 2.3 %collective-permute-start.31 = (bf16[8,3584]{1,0:T(8,128)(2,1)S(1)}, bf16[8,3584]{1,0:T(8,128)(2,1)S(1)}, u32[]{:S(2)}, u32[]{:S(2)}) collective-permute-start(bf16[8,3584]{1,0:T(8,128)(2,1)S(1)} %get-tuple-element.63), channel_id=1, source_target_pairs={{0,2},{1,3},{2,0},{3,1},{4,6},{5,7},{6,4},{7,5},{8,10},{9,11},{10,... | collective-permute-start | bytes 172040 | tf_op jit(solution)/shard_map/ppermute | solution.py:31
  74.6 1.2 %collective-permute-done.32 = bf16[8,3584]{1,0:T(8,128)(2,1)S(1)} collective-permute-done((bf16[8,3584]{1,0:T(8,128)(2,1)S(1)}, bf16[8,3584]{1,0:T(8,128)(2,1)S(1)}, u32[]{:S(2)}, u32[]{:S(2)}) %collective-permute-start.32) | collective-permute-done | bytes 57376 | tf_op jit(solution)/shard_map/ppermute | solution.py:31
  75.9 1.6 %collective-permute-done.31 = bf16[8,3584]{1,0:T(8,128)(2,1)S(1)} collective-permute-done((bf16[8,3584]{1,0:T(8,128)(2,1)S(1)}, bf16[8,3584]{1,0:T(8,128)(2,1)S(1)}, u32[]{:S(2)}, u32[]{:S(2)}) %collective-permute-start.31) | collective-permute-done | bytes 57376 | tf_op jit(solution)/shard_map/ppermute | solution.py:31
  (138 shorter events, 22.3 us)
Async XLA Ops:
  2.0 7.6 %collective-permute-start.5 = (bf16[8,3584]{1,0:T(8,128)(2,1)}, bf16[8,3584]{1,0:T(8,128)(2,1)S(1)}, u32[]{:S(2)}, u32[]{:S(2)}) collective-permute-start(bf16[8,3584]{1,0:T(8,128)(2,1)} %get-tuple-element.25), channel_id=1, source_target_pairs={{0,2},{1,3},{2,0},{3,1},{4,6},{5,7},{6,4},{7,5},{8,10},{9,11},{10,... | collective-permute-start | bytes 172040 | tf_op jit(solution)/shard_map/ppermute | solution.py:31
  6.1 11.4 %collective-permute-start = (bf16[8,3712]{1,0:T(8,128)(2,1)}, bf16[8,3712]{1,0:T(8,128)(2,1)S(1)}, u32[]{:S(2)}, u32[]{:S(2)}) collective-permute-start(bf16[8,3712]{1,0:T(8,128)(2,1)} %get-tuple-element.23), channel_id=1, source_target_pairs={{0,2},{1,3},{2,0},{3,1},{4,6},{5,7},{6,4},{7,5},{8,10},{9,11},{10,... | collective-permute-start | bytes 178184 | tf_op jit(solution)/shard_map/ppermute | solution.py:31
  6.2 20.8 %collective-permute-start.2 = (bf16[16,7296]{1,0:T(8,128)(2,1)}, bf16[16,7296]{1,0:T(8,128)(2,1)S(1)}, u32[]{:S(2)}, u32[]{:S(2)}) collective-permute-start(bf16[16,7296]{1,0:T(8,128)(2,1)} %get-tuple-element.24), channel_id=1, source_target_pairs={{0,8},{4,12},{8,0},{12,4},{1,9},{5,13},{9,1},{13,5},{2,10},{6,14},... | collective-permute-start | bytes 700424 | tf_op jit(solution)/shard_map/ppermute | solution.py:31
  9.6 8.8 %collective-permute-start.16 = (bf16[8,3584]{1,0:T(8,128)(2,1)}, bf16[8,3584]{1,0:T(8,128)(2,1)S(1)}, u32[]{:S(2)}, u32[]{:S(2)}) collective-permute-start(bf16[8,3584]{1,0:T(8,128)(2,1)} %get-tuple-element.33), channel_id=1, source_target_pairs={{0,2},{1,3},{2,0},{3,1},{4,6},{5,7},{6,4},{7,5},{8,10},{9,11},{10,... | collective-permute-start | bytes 172040 | tf_op jit(solution)/shard_map/ppermute | solution.py:31
  13.1 8.1 %collective-permute-start.11 = (bf16[8,3712]{1,0:T(8,128)(2,1)}, bf16[8,3712]{1,0:T(8,128)(2,1)S(1)}, u32[]{:S(2)}, u32[]{:S(2)}) collective-permute-start(bf16[8,3712]{1,0:T(8,128)(2,1)} %get-tuple-element.27), channel_id=1, source_target_pairs={{0,2},{1,3},{2,0},{3,1},{4,6},{5,7},{6,4},{7,5},{8,10},{9,11},{10,... | collective-permute-start | bytes 178184 | tf_op jit(solution)/shard_map/ppermute | solution.py:31
  15.2 7.4 %collective-permute-start.6 = (bf16[16,3584]{1,0:T(8,128)(2,1)S(1)}, bf16[16,3584]{1,0:T(8,128)(2,1)S(1)}, u32[]{:S(2)}, u32[]{:S(2)}) collective-permute-start(bf16[16,3584]{1,0:T(8,128)(2,1)S(1)} %pad_maximum_fusion.9), channel_id=1, source_target_pairs={{0,1},{1,0},{2,3},{3,2},{4,5},{5,4},{6,7},{7,6},{8,9},{9,8},{10,11... | collective-permute-start | bytes 344072 | tf_op jit(solution)/shard_map/ppermute | solution.py:31
  18.3 6.2 %collective-permute-start.1 = (bf16[16,3712]{1,0:T(8,128)(2,1)S(1)}, bf16[16,3712]{1,0:T(8,128)(2,1)S(1)}, u32[]{:S(2)}, u32[]{:S(2)}) collective-permute-start(bf16[16,3712]{1,0:T(8,128)(2,1)S(1)} %pad_maximum_fusion.7), channel_id=1, source_target_pairs={{0,1},{1,0},{2,3},{3,2},{4,5},{5,4},{6,7},{7,6},{8,9},{9,8},{10,11... | collective-permute-start | bytes 356360 | tf_op jit(solution)/shard_map/ppermute | solution.py:31
  19.3 7.8 %collective-permute-start.17 = (bf16[16,3584]{1,0:T(8,128)(2,1)S(1)}, bf16[16,3584]{1,0:T(8,128)(2,1)S(1)}, u32[]{:S(2)}, u32[]{:S(2)}) collective-permute-start(bf16[16,3584]{1,0:T(8,128)(2,1)S(1)} %pad_maximum_fusion.10), channel_id=1, source_target_pairs={{0,1},{1,0},{2,3},{3,2},{4,5},{5,4},{6,7},{7,6},{8,9},{9,8},{10,11... | collective-permute-start | bytes 344072 | tf_op jit(solution)/shard_map/ppermute | solution.py:31
  22.1 6.3 %collective-permute-start.12 = (bf16[16,3712]{1,0:T(8,128)(2,1)S(1)}, bf16[16,3712]{1,0:T(8,128)(2,1)S(1)}, u32[]{:S(2)}, u32[]{:S(2)}) collective-permute-start(bf16[16,3712]{1,0:T(8,128)(2,1)S(1)} %pad_maximum_fusion.8), channel_id=1, source_target_pairs={{0,1},{1,0},{2,3},{3,2},{4,5},{5,4},{6,7},{7,6},{8,9},{9,8},{10,11... | collective-permute-start | bytes 356360 | tf_op jit(solution)/shard_map/ppermute | solution.py:31
  22.6 6.7 %collective-permute-start.7 = (bf16[24,3584]{1,0:T(8,128)(2,1)S(1)}, bf16[24,3584]{1,0:T(8,128)(2,1)S(1)}, u32[]{:S(2)}, u32[]{:S(2)}) collective-permute-start(bf16[24,3584]{1,0:T(8,128)(2,1)S(1)} %pad_maximum_fusion.5), channel_id=1, source_target_pairs={{0,8},{4,12},{8,0},{12,4},{1,9},{5,13},{9,1},{13,5},{2,10},{6,14},... | collective-permute-start | bytes 516104 | tf_op jit(solution)/shard_map/ppermute | solution.py:31
  24.6 7.0 %collective-permute-start.3 = (bf16[24,3712]{1,0:T(8,128)(2,1)S(1)}, bf16[24,3712]{1,0:T(8,128)(2,1)S(1)}, u32[]{:S(2)}, u32[]{:S(2)}) collective-permute-start(bf16[24,3712]{1,0:T(8,128)(2,1)S(1)} %pad_maximum_fusion.3), channel_id=1, source_target_pairs={{0,8},{4,12},{8,0},{12,4},{1,9},{5,13},{9,1},{13,5},{2,10},{6,14},... | collective-permute-start | bytes 534536 | tf_op jit(solution)/shard_map/ppermute | solution.py:31
  29.3 2.3 %collective-permute-start.8 = (bf16[64,3584]{1,0:T(8,128)(2,1)S(1)}, bf16[64,3584]{1,0:T(8,128)(2,1)S(1)}, u32[]{:S(2)}, u32[]{:S(2)}) collective-permute-start(bf16[64,3584]{1,0:T(8,128)(2,1)S(1)} %get-tuple-element.55), channel_id=1, source_target_pairs={{0,4},{4,0},{8,12},{12,8},{1,5},{5,1},{9,13},{13,9},{2,6},{6,2},{1... | collective-permute-start | bytes 1376264 | tf_op jit(solution)/shard_map/ppermute | solution.py:31
  29.4 11.3 %collective-permute-start.18 = (bf16[24,3584]{1,0:T(8,128)(2,1)S(1)}, bf16[24,3584]{1,0:T(8,128)(2,1)S(1)}, u32[]{:S(2)}, u32[]{:S(2)}) collective-permute-start(bf16[24,3584]{1,0:T(8,128)(2,1)S(1)} %pad_maximum_fusion.6), channel_id=1, source_target_pairs={{0,8},{4,12},{8,0},{12,4},{1,9},{5,13},{9,1},{13,5},{2,10},{6,14},... | collective-permute-start | bytes 516104 | tf_op jit(solution)/shard_map/ppermute | solution.py:31
  31.0 9.8 %collective-permute-start.13 = (bf16[24,3712]{1,0:T(8,128)(2,1)S(1)}, bf16[24,3712]{1,0:T(8,128)(2,1)S(1)}, u32[]{:S(2)}, u32[]{:S(2)}) collective-permute-start(bf16[24,3712]{1,0:T(8,128)(2,1)S(1)} %pad_maximum_fusion.4), channel_id=1, source_target_pairs={{0,8},{4,12},{8,0},{12,4},{1,9},{5,13},{9,1},{13,5},{2,10},{6,14},... | collective-permute-start | bytes 534536 | tf_op jit(solution)/shard_map/ppermute | solution.py:31
  31.6 3.7 %collective-permute-start.4 = (bf16[64,3712]{1,0:T(8,128)(2,1)S(1)}, bf16[64,3712]{1,0:T(8,128)(2,1)S(1)}, u32[]{:S(2)}, u32[]{:S(2)}) collective-permute-start(bf16[64,3712]{1,0:T(8,128)(2,1)S(1)} %get-tuple-element.53), channel_id=1, source_target_pairs={{0,4},{4,0},{8,12},{12,8},{1,5},{5,1},{9,13},{13,9},{2,6},{6,2},{1... | collective-permute-start | bytes 1425416 | tf_op jit(solution)/shard_map/ppermute | solution.py:31
  40.8 2.0 %collective-permute-start.9 = (bf16[64,3584]{1,0:T(8,128)(2,1)S(1)}, bf16[64,3584]{1,0:T(8,128)(2,1)S(1)}, u32[]{:S(2)}, u32[]{:S(2)}) collective-permute-start(bf16[64,3584]{1,0:T(8,128)(2,1)S(1)} %slice.261), channel_id=1, source_target_pairs={{0,4},{4,0},{8,12},{12,8},{1,5},{5,1},{9,13},{13,9},{2,6},{6,2},{1... | collective-permute-start | bytes 1376264 | tf_op jit(solution)/shard_map/ppermute | solution.py:31
  40.9 4.2 %collective-permute-start.19 = (bf16[64,3584]{1,0:T(8,128)(2,1)S(1)}, bf16[64,3584]{1,0:T(8,128)(2,1)S(1)}, u32[]{:S(2)}, u32[]{:S(2)}) collective-permute-start(bf16[64,3584]{1,0:T(8,128)(2,1)S(1)} %constant_dynamic-update-slice_fusion.27), channel_id=1, source_target_pairs={{0,4},{4,0},{8,12},{12,8},{1,5},{5,1},{9,13},{13,9},{2,6},{6,2},{1... | collective-permute-start | bytes 1376264 | tf_op jit(solution)/shard_map/ppermute | solution.py:31
  41.4 5.1 %collective-permute-start.14 = (bf16[64,3712]{1,0:T(8,128)(2,1)S(1)}, bf16[64,3712]{1,0:T(8,128)(2,1)S(1)}, u32[]{:S(2)}, u32[]{:S(2)}) collective-permute-start(bf16[64,3712]{1,0:T(8,128)(2,1)S(1)} %constant_dynamic-update-slice_fusion.22), channel_id=1, source_target_pairs={{0,4},{4,0},{8,12},{12,8},{1,5},{5,1},{9,13},{13,9},{2,6},{6,2},{1... | collective-permute-start | bytes 1425416 | tf_op jit(solution)/shard_map/ppermute | solution.py:31
  43.0 7.3 %collective-permute-start.23 = (bf16[24,3584]{1,0:T(8,128)(2,1)S(1)}, bf16[24,3584]{1,0:T(8,128)(2,1)S(1)}, u32[]{:S(2)}, u32[]{:S(2)}) collective-permute-start(bf16[24,3584]{1,0:T(8,128)(2,1)S(1)} %slice.279), channel_id=1, source_target_pairs={{0,8},{4,12},{8,0},{12,4},{1,9},{5,13},{9,1},{13,5},{2,10},{6,14},... | collective-permute-start | bytes 516104 | tf_op jit(solution)/shard_map/ppermute | solution.py:31
  44.6 8.8 %collective-permute-start.10 = (bf16[24,3584]{1,0:T(8,128)(2,1)S(1)}, bf16[24,3584]{1,0:T(8,128)(2,1)S(1)}, u32[]{:S(2)}, u32[]{:S(2)}) collective-permute-start(bf16[24,3584]{1,0:T(8,128)(2,1)S(1)} %slice.264), channel_id=1, source_target_pairs={{0,8},{4,12},{8,0},{12,4},{1,9},{5,13},{9,1},{13,5},{2,10},{6,14},... | collective-permute-start | bytes 516104 | tf_op jit(solution)/shard_map/ppermute | solution.py:31
  49.5 4.0 %collective-permute-start.21 = (bf16[64,3584]{1,0:T(8,128)(2,1)S(1)}, bf16[64,3584]{1,0:T(8,128)(2,1)S(1)}, u32[]{:S(2)}, u32[]{:S(2)}) collective-permute-start(bf16[64,3584]{1,0:T(8,128)(2,1)S(1)} %slice.275), channel_id=1, source_target_pairs={{0,4},{4,0},{8,12},{12,8},{1,5},{5,1},{9,13},{13,9},{2,6},{6,2},{1... | collective-permute-start | bytes 1376264 | tf_op jit(solution)/shard_map/ppermute | solution.py:31
  49.6 4.0 %collective-permute-start.20 = (bf16[64,3584]{1,0:T(8,128)(2,1)S(1)}, bf16[64,3584]{1,0:T(8,128)(2,1)S(1)}, u32[]{:S(2)}, u32[]{:S(2)}) collective-permute-start(bf16[64,3584]{1,0:T(8,128)(2,1)S(1)} %slice.273), channel_id=1, source_target_pairs={{0,4},{4,0},{8,12},{12,8},{1,5},{5,1},{9,13},{13,9},{2,6},{6,2},{1... | collective-permute-start | bytes 1376264 | tf_op jit(solution)/shard_map/ppermute | solution.py:31
  53.9 8.6 %collective-permute-start.29 = (bf16[24,3584]{1,0:T(8,128)(2,1)S(1)}, bf16[24,3584]{1,0:T(8,128)(2,1)S(1)}, u32[]{:S(2)}, u32[]{:S(2)}) collective-permute-start(bf16[24,3584]{1,0:T(8,128)(2,1)S(1)} %slice.298), channel_id=1, source_target_pairs={{0,8},{4,12},{8,0},{12,4},{1,9},{5,13},{9,1},{13,5},{2,10},{6,14},... | collective-permute-start | bytes 516104 | tf_op jit(solution)/shard_map/ppermute | solution.py:31
  55.4 5.8 %collective-permute-start.22 = (bf16[16,3584]{1,0:T(8,128)(2,1)S(1)}, bf16[16,3584]{1,0:T(8,128)(2,1)S(1)}, u32[]{:S(2)}, u32[]{:S(2)}) collective-permute-start(bf16[16,3584]{1,0:T(8,128)(2,1)S(1)} %slice.265), channel_id=1, source_target_pairs={{0,1},{1,0},{2,3},{3,2},{4,5},{5,4},{6,7},{7,6},{8,9},{9,8},{10,11... | collective-permute-start | bytes 344072 | tf_op jit(solution)/shard_map/ppermute | solution.py:31
  57.1 5.3 %collective-permute-start.24 = (bf16[16,3584]{1,0:T(8,128)(2,1)S(1)}, bf16[16,3584]{1,0:T(8,128)(2,1)S(1)}, u32[]{:S(2)}, u32[]{:S(2)}) collective-permute-start(bf16[16,3584]{1,0:T(8,128)(2,1)S(1)} %slice.280), channel_id=1, source_target_pairs={{0,1},{1,0},{2,3},{3,2},{4,5},{5,4},{6,7},{7,6},{8,9},{9,8},{10,11... | collective-permute-start | bytes 344072 | tf_op jit(solution)/shard_map/ppermute | solution.py:31
  57.5 7.3 %collective-permute-start.25 = (bf16[24,3584]{1,0:T(8,128)(2,1)S(1)}, bf16[24,3584]{1,0:T(8,128)(2,1)S(1)}, u32[]{:S(2)}, u32[]{:S(2)}) collective-permute-start(bf16[24,3584]{1,0:T(8,128)(2,1)S(1)} %slice.286), channel_id=1, source_target_pairs={{0,8},{4,12},{8,0},{12,4},{1,9},{5,13},{9,1},{13,5},{2,10},{6,14},... | collective-permute-start | bytes 516104 | tf_op jit(solution)/shard_map/ppermute | solution.py:31
  58.0 16.6 %collective-permute-start.27 = (bf16[16,7168]{1,0:T(8,128)(2,1)S(1)}, bf16[16,7168]{1,0:T(8,128)(2,1)S(1)}, u32[]{:S(2)}, u32[]{:S(2)}) collective-permute-start(bf16[16,7168]{1,0:T(8,128)(2,1)S(1)} %maximum_maximum_fusion), channel_id=1, source_target_pairs={{0,8},{4,12},{8,0},{12,4},{1,9},{5,13},{9,1},{13,5},{2,10},{6,14},... | collective-permute-start | bytes 688136 | tf_op jit(solution)/shard_map/ppermute | solution.py:31
  62.6 6.7 %collective-permute-start.30 = (bf16[16,3584]{1,0:T(8,128)(2,1)S(1)}, bf16[16,3584]{1,0:T(8,128)(2,1)S(1)}, u32[]{:S(2)}, u32[]{:S(2)}) collective-permute-start(bf16[16,3584]{1,0:T(8,128)(2,1)S(1)} %slice.299), channel_id=1, source_target_pairs={{0,1},{1,0},{2,3},{3,2},{4,5},{5,4},{6,7},{7,6},{8,9},{9,8},{10,11... | collective-permute-start | bytes 344072 | tf_op jit(solution)/shard_map/ppermute | solution.py:31
  64.8 9.9 %collective-permute-start.26 = (bf16[8,7168]{1,0:T(8,128)(2,1)S(1)}, bf16[8,7168]{1,0:T(8,128)(2,1)S(1)}, u32[]{:S(2)}, u32[]{:S(2)}) collective-permute-start(bf16[8,7168]{1,0:T(8,128)(2,1)S(1)} %pad_maximum_fusion.11), channel_id=1, source_target_pairs={{0,2},{1,3},{2,0},{3,1},{4,6},{5,7},{6,4},{7,5},{8,10},{9,11},{10,... | collective-permute-start | bytes 344072 | tf_op jit(solution)/shard_map/ppermute | solution.py:31
  67.5 4.9 %collective-permute-start.28 = (bf16[16,3584]{1,0:T(8,128)(2,1)S(1)}, bf16[16,3584]{1,0:T(8,128)(2,1)S(1)}, u32[]{:S(2)}, u32[]{:S(2)}) collective-permute-start(bf16[16,3584]{1,0:T(8,128)(2,1)S(1)} %slice.294), channel_id=1, source_target_pairs={{0,1},{1,0},{2,3},{3,2},{4,5},{5,4},{6,7},{7,6},{8,9},{9,8},{10,11... | collective-permute-start | bytes 344072 | tf_op jit(solution)/shard_map/ppermute | solution.py:31
  69.3 6.6 %collective-permute-start.32 = (bf16[8,3584]{1,0:T(8,128)(2,1)S(1)}, bf16[8,3584]{1,0:T(8,128)(2,1)S(1)}, u32[]{:S(2)}, u32[]{:S(2)}) collective-permute-start(bf16[8,3584]{1,0:T(8,128)(2,1)S(1)} %get-tuple-element.65), channel_id=1, source_target_pairs={{0,2},{1,3},{2,0},{3,1},{4,6},{5,7},{6,4},{7,5},{8,10},{9,11},{10,... | collective-permute-start | bytes 172040 | tf_op jit(solution)/shard_map/ppermute | solution.py:31
  72.4 5.1 %collective-permute-start.31 = (bf16[8,3584]{1,0:T(8,128)(2,1)S(1)}, bf16[8,3584]{1,0:T(8,128)(2,1)S(1)}, u32[]{:S(2)}, u32[]{:S(2)}) collective-permute-start(bf16[8,3584]{1,0:T(8,128)(2,1)S(1)} %get-tuple-element.63), channel_id=1, source_target_pairs={{0,2},{1,3},{2,0},{3,1},{4,6},{5,7},{6,4},{7,5},{8,10},{9,11},{10,... | collective-permute-start | bytes 172040 | tf_op jit(solution)/shard_map/ppermute | solution.py:31
  (12 other events, 68.5 us)
